TPU v7x, 32 devices: a whole 2x2x4 slice. The times are simulated.
32 devices in a mesh: band: 4 (over y, x), grp: 4 (over z), row: 2 (over core).
Axes of the slice: x: 2, y: 2, z: 4, core: 2. Of those that a mesh axis runs over, the one named last changes fastest.
Arguments:
- kspace_data: float32 [4, 16, 2, 2048], P('grp', 'row'), may hold values from -6 to 6
- coil_maps: bfloat16 [4, 4, 16, 256, 512], P('band', 'grp', 'row'), may hold values from -1.5 to 1.5
- smooth_weight: float32 [4, 4, 256, 256], P('band', 'grp', 'row'), may hold values from 0.3 to 3
- kernel_cols: bfloat16 [2048, 16], replicated, may hold values from -1.5 to 1.5
- kernel_rows: bfloat16 [2048, 16], replicated, may hold values from -1.5 to 1.5
- tile_index: int32 [16], replicated, may hold values from 0 to 255
- caipi_cycle: int32 [4], P('band'), may hold values from 0 to 3
Outputs:
- solution_field: float32 [4, 4, 256, 512], P('band', 'grp', 'row')
- residual: float32 [4, 4, 256, 512], P('band', 'grp', 'row')
All inputs are finite; a program needn't handle non-finite values.
Results may differ from a plain program's by a relative error of at most 0.0003.
Values sent between devices are 32-bit elements; how exact they have to be, the bound alone decides.
No kernel may reach another device: no remote copies, remote signals or barrier semaphores. Data moves between devices by JAX's collectives and lax.ppermute only.
A program may use at most 128 MiB of HBM per device.

v0:
```python
import math

import jax
import jax.numpy as jnp
from jax import lax
from jax.sharding import PartitionSpec as P

NY = 256
NX = 256
TY = 16
TX = 16
SB = 128
NBLK = 16
NTILES = 256


reg_strength = 0.5
damping = 1.0
two_pi = 6.283185307179586
highest = lax.Precision.HIGHEST


def with_halo(block, sides, width):
    for axis, dim in sides:
        count = lax.axis_size(axis)
        forward = [(i, i + 1) for i in range(count - 1)]
        backward = [(target, source) for source, target in forward]
        low = lax.ppermute(
            lax.slice_in_dim(block, block.shape[dim] - width, None, axis=dim), axis, forward
        )
        high = lax.ppermute(lax.slice_in_dim(block, 0, width, axis=dim), axis, backward)
        block = jnp.concatenate([low, block, high], axis=dim)
    return block


def dft_tables(length, sign):
    index = jnp.arange(length, dtype=jnp.int32)
    turns = index[:, None] * index[None, :] % length
    angle = turns.astype(jnp.float32) * (two_pi / length)
    scale = 1.0 / math.sqrt(length)
    return (jnp.cos(angle) * scale, sign * jnp.sin(angle) * scale)


def column_matrix(sign):
    real_part, imag_part = dft_tables(NX, sign)
    upper = jnp.concatenate([real_part, imag_part], axis=1)
    lower = jnp.concatenate([-imag_part, real_part], axis=1)
    return jnp.concatenate([upper, lower], axis=0)


def row_matrix(sign):
    real_part, imag_part = dft_tables(NY, sign)
    return jnp.concatenate([real_part, imag_part], axis=0)


def along_columns(data, matrix):
    flat = data.reshape(-1, data.shape[-1])
    return jnp.dot(flat, matrix, precision=highest).reshape(data.shape)


def along_rows(data, matrix):
    mixed = jnp.einsum("ky,cyx->ckx", matrix, data, precision=highest)
    upper, lower = (mixed[:, :NY], mixed[:, NY:])
    real_part = upper[..., :NX] - lower[..., NX:]
    imag_part = lower[..., :NX] + upper[..., NX:]
    return jnp.concatenate([real_part, imag_part], axis=-1)


def to_tiles(grid):
    count = grid.shape[0]
    shaped = grid.reshape(count, NY // TY, TY, 2, NX // TX, TX)
    return shaped.transpose(1, 4, 0, 3, 2, 5).reshape(NTILES, count * 2, TY, TX)


def from_tiles(tiles, count):
    shaped = tiles.reshape(NY // TY, NX // TX, count, 2, TY, TX)
    return shaped.transpose(2, 0, 4, 3, 1, 5).reshape(count, NY, 2 * NX)


def coil_images(profiles, image):
    profile = profiles.astype(jnp.float32)
    width = image.shape[-1] // 2
    coil_real, coil_imag = (profile[..., :width], profile[..., width:])
    image_real, image_imag = (image[None, :, :width], image[None, :, width:])
    return jnp.concatenate(
        [
            coil_real * image_real - coil_imag * image_imag,
            coil_real * image_imag + coil_imag * image_real,
        ],
        axis=-1,
    )


def combine_coils(profiles, images):
    profile = profiles.astype(jnp.float32)
    width = images.shape[-1] // 2
    coil_real, coil_imag = (profile[..., :width], profile[..., width:])
    image_real, image_imag = (images[..., :width], images[..., width:])
    real_sum = jnp.sum(coil_real * image_real + coil_imag * image_imag, axis=0)
    imag_sum = jnp.sum(coil_real * image_imag - coil_imag * image_real, axis=0)
    return jnp.concatenate([real_sum, imag_sum], axis=-1)


def edge_term(values, weights, axis):
    count = values.shape[axis]
    diff = lax.slice_in_dim(values, 0, count - 1, axis=axis) - lax.slice_in_dim(
        values, 1, count, axis=axis
    )
    coupling = lax.slice_in_dim(weights, 0, count - 1, axis=axis) * lax.slice_in_dim(
        weights, 1, count, axis=axis
    )
    flux = coupling * diff
    after = [(0, 0)] * values.ndim
    before = [(0, 0)] * values.ndim
    after[axis] = (0, 1)
    before[axis] = (1, 0)
    return jnp.pad(flux, after) - jnp.pad(flux, before)


def laplace_padded(padded, weight_pad):
    doubled = jnp.concatenate([weight_pad, weight_pad], axis=-1)
    total = edge_term(padded, doubled, 1) + edge_term(padded, doubled, 2)
    center = padded[:, 1:-1, 1:-1]
    weight_center = weight_pad[:, 1:-1, 1:-1]
    shaped = center.reshape(center.shape[:-1] + (2, NX))
    columns = edge_term(shaped, weight_center[..., None, :], shaped.ndim - 1)
    return total[:, 1:-1, 1:-1] + columns.reshape(center.shape)


def on_device(
    kspace_data, coil_maps, smooth_weight, kernel_cols, kernel_rows, tile_index, caipi_cycle
):
    coil_count = coil_maps.shape[2]
    band_count = lax.axis_size("band")
    profiles = coil_maps[0, 0]
    blocks = jnp.arange(NBLK, dtype=jnp.int32)
    angle = (caipi_cycle[0] * blocks % band_count).astype(jnp.float32) * (two_pi / band_count)
    phase_cos, phase_sin = (jnp.cos(angle), jnp.sin(angle))
    column_forward, column_inverse = (column_matrix(-1.0), column_matrix(1.0))
    row_forward, row_inverse = (row_matrix(-1.0), row_matrix(1.0))
    selector = (tile_index[None, :] == jnp.arange(NTILES, dtype=jnp.int32)[:, None]).astype(
        jnp.float32
    )
    col_weight = kernel_cols.astype(jnp.float32).reshape(NBLK, SB, TX)
    row_weight = kernel_rows.astype(jnp.float32).reshape(NBLK, SB, TY)
    weight_pad = with_halo(smooth_weight, (("grp", 1), ("row", 2)), 1)

    def transformed_rows(piece):
        return along_columns(coil_images(profiles, piece[0, 0]), column_forward)

    def predict(grid_half):
        grid = along_rows(grid_half, row_forward)
        picked = jnp.take(to_tiles(grid), tile_index, axis=0)
        partial_sum = jnp.einsum("bcyx,bsx->bcys", picked, col_weight, precision=highest)
        predicted = jnp.einsum("bcys,bsy->bcs", partial_sum, row_weight, precision=highest)
        predicted = predicted.reshape(NBLK, coil_count, 2, SB)
        real_part, imag_part = (predicted[:, :, 0], predicted[:, :, 1])
        cosine, sine = (phase_cos[:, None, None], phase_sin[:, None, None])
        turned = jnp.stack(
            [cosine * real_part - sine * imag_part, sine * real_part + cosine * imag_part], axis=2
        )
        return lax.psum(turned.transpose(1, 2, 0, 3), "band")

    def forward(direction):
        grid_half = transformed_rows(lax.all_gather(direction, "row", axis=2, tiled=True))
        return predict(grid_half)

    def back_project(kspace):
        real_part, imag_part = (kspace[:, 0], kspace[:, 1])
        cosine, sine = (phase_cos[None, :, None], phase_sin[None, :, None])
        back = jnp.stack(
            [cosine * real_part + sine * imag_part, cosine * imag_part - sine * real_part], axis=1
        )
        values = back.transpose(2, 0, 1, 3).reshape(NBLK, coil_count * 2, SB)
        partial_sum = jnp.einsum("bcs,bsy->bcys", values, row_weight, precision=highest)
        spread = jnp.einsum("bcys,bsx->bcyx", partial_sum, col_weight, precision=highest)
        summed = jnp.dot(selector, spread.reshape(NBLK, -1), precision=highest)
        grid = from_tiles(summed, coil_count)
        return along_rows(grid, row_inverse)

    def adjoint(kspace):
        rows_half = back_project(kspace)
        summed = lax.psum_scatter(
            combine_coils(profiles, along_columns(rows_half, column_inverse)),
            "row",
            scatter_dimension=0,
            tiled=True,
        )
        return summed[None, None]

    rhs = adjoint(kspace_data[0].reshape(coil_count, 2, NBLK, SB))
    residual = rhs
    direction = rhs
    mine = residual
    norm_now = lax.psum(jnp.sum(mine * mine), ("band", "grp", "row"))
    padded = with_halo(direction, (("grp", 1), ("row", 2)), 1)
    smoothed = laplace_padded(padded, weight_pad)
    collapsed = forward(direction)
    image = adjoint(collapsed) + reg_strength * smoothed + damping * direction
    curvature = lax.psum(jnp.sum(direction * image), ("band", "grp", "row"))
    alpha = norm_now / curvature
    solution_field = alpha * direction
    residual = residual - alpha * image
    return (solution_field, residual)


def solution(mesh):
    return jax.shard_map(
        on_device,
        mesh=mesh,
        in_specs=(
            P("grp", "row", None, None),
            P("band", "grp", "row", None, None),
            P("band", "grp", "row", None),
            P(),
            P(),
            P(),
            P("band"),
        ),
        out_specs=(P("band", "grp", "row", None), P("band", "grp", "row", None)),
        check_vma=False,
    )
```

profile of v0, /device:TPU:0, one launch (start us, length us, event | category | flops | bytes accessed | tf_op | source)
XLA Modules:
  0.0 392.6 jit_solution(16444229723303604805)
XLA Ops:
  7.2 5.6 %collective-permute-start = (f32[1,1,128,256]{3,2,1,0:T(8,128)}, f32[1,1,128,256]{3,2,1,0:T(8,128)}, u32[]{:S(2)}, u32[]{:S(2)}) collective-permute-start(f32[1,1,128,256]{3,2,1,0:T(8,128)} %param.9), channel_id=1, source_target_pairs={{0,2},{2,4},{4,6},{1,3},{3,5},{5,7},{8,10},{10,12},{12,14},{9,11},... | collective-permute-start | bytes 393224 | tf_op jit(solution)/shard_map/ppermute | solution.py:28
  20.1 1.6 reshape.188
  21.7 1.9 copy.35
  23.6 15.1 %convolution_bitcast_fusion.1 = f32[8,16,16,2,16,16]{5,4,2,3,0,1:T(8,128)S(1)} fusion(f32[8,2,16,16,16,1]{4,3,2,1,0,5:T(8,128)} %bitcast.121, s32[16,16]{1,0:T(8,128)S(1)} %multiply_add_fusion.4, s32[16]{0:T(128)S(1)} %copy-done.12), kind=kOutput, calls=%fused_computation.2 | convolution fusion | flops 201330688 | bytes 4457536 | tf_op jit(solution)/shard_map/dot_general | solution.py:177
  38.8 11.4 %copy.36 = f32[8,16,16,2,16,16]{5,4,3,2,1,0:T(8,128)} copy(f32[8,16,16,2,16,16]{5,4,2,3,0,1:T(8,128)S(1)} %convolution_bitcast_fusion.1) | data formatting | bytes 8388608 | tf_op jit(solution)/shard_map/transpose | solution.py:77
  50.1 28.2 %reshape.223 = f32[8,256,512]{2,1,0:T(8,128)} reshape(f32[8,16,16,2,16,16]{5,4,3,2,1,0:T(8,128)} %copy.36) | data formatting | bytes 8388608 | tf_op jit(solution)/shard_map/reshape | solution.py:77
  78.3 15.8 %convolution_bitcast_fusion.4 = f32[8,512,512]{1,2,0:T(8,128)S(1)} fusion(f32[8,256,512]{2,1,0:T(8,128)} %reshape.223, f32[256,256]{1,0:T(8,128)S(1)} %get-tuple-element.32, f32[256,256]{1,0:T(8,128)S(1)} %get-tuple-element.33), kind=kOutput, calls=%fused_computation.18 | convolution fusion | flops 6442582016 | bytes 13107200 | tf_op jit(solution)/shard_map/ky,cyx->ckx/dot_general | solution.py:62
  96.3 7.2 %fusion = f32[8,256,512]{2,1,0:T(8,128)S(1)} fusion(f32[8,256,256]{1,2,0:T(8,128)S(1)} %get-tuple-element.15, f32[8,256,256]{1,2,0:T(8,128)S(1)} %get-tuple-element.14, f32[256,256]{1,0:T(8,128)S(1)} %get-tuple-element.32, f32[256,256]{1,0:T(8,128)S(1)} %fusion.63, f32[256,256]{1,0:T(8,128)S(1)} %get-tuple-element.33), kind=kOutput, calls=%fused_computation.3 | convolution fusion | flops 6444285952 | bytes 9175040 | tf_op jit(solution)/shard_map/dot_general | solution.py:58
  108.8 1.5 collective-permute-start.2
  111.5 3.9 %reduce-scatter.3.cloned.1.call-done = f32[128,512]{1,0:T(8,128)} async-done(((f32[256,512]{1,0:T(8,128)}), f32[128,512]{1,0:T(8,128)}) %reduce-scatter.3.cloned.1.call-update) | async-done | bytes 262160 | tf_op jit(solution)/shard_map/reduce_scatter | solution.py:183
  115.5 2.8 all-gather
  118.3 2.8 multiply_subtract_fusion
  121.1 7.0 %fusion.4 = f32[8,256,512]{1,2,0:T(8,128)S(1)} fusion(f32[8,256,256]{2,1,0:T(8,128)S(1)} %get-tuple-element.17, f32[8,256,256]{2,1,0:T(8,128)S(1)} %get-tuple-element.16, f32[256,256]{1,0:T(8,128)S(1)} %get-tuple-element.32, f32[256,256]{1,0:T(8,128)S(1)} %get-tuple-element.35, f32[256,256]{1,0:T(8,128)S(1)} %get-tuple-element.34), kind=kOutput, calls=%fused_computation.7 | convolution fusion | flops 6444285952 | bytes 9175040 | tf_op jit(solution)/shard_map/dot_general | solution.py:58
  128.1 7.6 %convolution_bitcast_fusion.3 = f32[8,512,512]{1,2,0:T(8,128)S(1)} fusion(f32[8,256,512]{1,2,0:T(8,128)S(1)} %fusion.4, f32[256,256]{1,0:T(8,128)S(1)} %get-tuple-element.32, f32[256,256]{1,0:T(8,128)S(1)} %get-tuple-element.34), kind=kOutput, calls=%fused_computation.17 | convolution fusion | flops 6442582016 | bytes 13107200 | tf_op jit(solution)/shard_map/ky,cyx->ckx/dot_general | solution.py:62
  136.4 2.5 pad_maximum_fusion
  138.9 19.4 %reshape.190 = f32[8,16,16,2,16,16]{2,1,5,4,3,0:T(8,128)} reshape(f32[8,256,512]{1,2,0:T(8,128)} %pad_maximum_fusion) | data formatting | bytes 8388608 | tf_op jit(solution)/shard_map/reshape | solution.py:71
  158.4 34.2 %copy.68 = f32[16,16,8,2,16,16]{5,4,3,2,1,0:T(8,128)} copy(f32[16,16,8,2,16,16]{4,0,5,1,3,2:T(8,128)} %bitcast.113) | data formatting | bytes 8388608 | tf_op jit(solution)/shard_map/reshape | solution.py:72
  192.5 3.6 gather_fusion
  196.1 3.2 multiply_reduce_fusion
  200.3 4.3 %collective-permute-start.4 = (f32[1,1,128,512]{3,2,1,0:T(8,128)S(1)}, f32[1,1,128,512]{3,2,1,0:T(8,128)}, u32[]{:S(2)}, u32[]{:S(2)}) collective-permute-start(f32[1,1,128,512]{3,2,1,0:T(8,128)S(1)} %bitcast.115), channel_id=1, source_target_pairs={{0,2},{2,4},{4,6},{1,3},{3,5},{5,7},{8,10},{10,12},{12,14},{9,11},... | collective-permute-start | bytes 786440 | tf_op jit(solution)/shard_map/ppermute | solution.py:28
  206.8 36.7 %all-reduce.9.cloned.1.call-done = f32[8,2,16,128]{3,2,1,0:T(8,128)} async-done(((f32[8,2,16,128]{3,2,1,0:T(8,128)}), f32[8,2,16,128]{3,2,1,0:T(8,128)}) %all-reduce.9.cloned.1.call-update) | async-done | bytes 131088 | tf_op jit(solution)/shard_map/psum | solution.py:162
  244.5 2.5 fusion.12
  247.0 3.1 reshape.195
  250.1 1.9 copy.45
  252.1 15.2 %convolution_bitcast_fusion = f32[8,16,16,2,16,16]{5,4,2,3,0,1:T(8,128)S(1)} fusion(f32[8,2,16,16,16,1]{4,3,2,1,0,5:T(8,128)} %bitcast.120, s32[16,16]{1,0:T(8,128)S(1)} %multiply_add_fusion.4, s32[16]{0:T(128)S(1)} %copy-done.12), kind=kOutput, calls=%fused_computation.1 | convolution fusion | flops 201330688 | bytes 4457536 | tf_op jit(solution)/shard_map/dot_general | solution.py:177
  267.2 11.4 %copy.46 = f32[8,16,16,2,16,16]{5,4,3,2,1,0:T(8,128)} copy(f32[8,16,16,2,16,16]{5,4,2,3,0,1:T(8,128)S(1)} %convolution_bitcast_fusion) | data formatting | bytes 8388608 | tf_op jit(solution)/shard_map/transpose | solution.py:77
  278.6 28.2 %reshape.225 = f32[8,256,512]{2,1,0:T(8,128)} reshape(f32[8,16,16,2,16,16]{5,4,3,2,1,0:T(8,128)} %copy.46) | data formatting | bytes 8388608 | tf_op jit(solution)/shard_map/reshape | solution.py:77
  306.8 15.8 %convolution_bitcast_fusion.2 = f32[8,512,512]{1,2,0:T(8,128)S(1)} fusion(f32[8,256,512]{2,1,0:T(8,128)} %reshape.225, f32[256,256]{1,0:T(8,128)S(1)} %get-tuple-element.32, f32[256,256]{1,0:T(8,128)S(1)} %get-tuple-element.33), kind=kOutput, calls=%fused_computation.16 | convolution fusion | flops 6442582016 | bytes 13107200 | tf_op jit(solution)/shard_map/ky,cyx->ckx/dot_general | solution.py:62
  323.6 7.2 %fusion.8 = f32[8,256,512]{2,1,0:T(8,128)S(1)} fusion(f32[8,256,256]{1,2,0:T(8,128)S(1)} %get-tuple-element.11, f32[8,256,256]{1,2,0:T(8,128)S(1)} %get-tuple-element.10, f32[256,256]{1,0:T(8,128)S(1)} %get-tuple-element.32, f32[256,256]{1,0:T(8,128)S(1)} %copy-done.4, f32[256,256]{1,0:T(8,128)S(1)} %get-tuple-element.33), kind=kOutput, calls=%fused_computation.12 | convolution fusion | flops 6444285952 | bytes 9175040 | tf_op jit(solution)/shard_map/dot_general | solution.py:58
  339.9 1.5 fusion.37
  341.4 1.7 multiply_reduce_fusion.1
  343.1 39.7 %all-reduce.6 = (f32[]{:T(128)}, f32[]{:T(128)}) all-reduce(f32[]{:T(128)} %multiply_reduce_fusion.2, f32[]{:T(128)} %get-tuple-element.8), channel_id=1, replica_groups=mesh['band'=4,'grp'=4,'row'=2] {'band','grp','row'}, use_global_device_ids=true, to_apply=%region_4.5 | all-reduce | flops 2 | bytes 16 | tf_op jit(solution)/shard_map/psum | solution.py:195
  (94 shorter events, 31.3 us)
Async XLA Ops:
  7.2 11.8 %copy-start.11 = (bf16[2048,16]{0,1:T(8,128)(2,1)S(1)}, bf16[2048,16]{0,1:T(8,128)(2,1)}, u32[]{:S(2)}) copy-start(bf16[2048,16]{0,1:T(8,128)(2,1)} %param.10) | copy-start | bytes 196612
  7.2 108.3 %reduce-scatter.3.cloned.1.call-start = ((), (), s32[]{:S(2)}) async-start(), calls=%async_computation.2 | async-start | bytes 786432 | tf_op jit(solution)/shard_map/reduce_scatter | solution.py:183
  7.2 99.7 %collective-permute-start = (f32[1,1,128,256]{3,2,1,0:T(8,128)}, f32[1,1,128,256]{3,2,1,0:T(8,128)}, u32[]{:S(2)}, u32[]{:S(2)}) collective-permute-start(f32[1,1,128,256]{3,2,1,0:T(8,128)} %param.9), channel_id=1, source_target_pairs={{0,2},{2,4},{4,6},{1,3},{3,5},{5,7},{8,10},{10,12},{12,14},{9,11},... | collective-permute-start | bytes 393224 | tf_op jit(solution)/shard_map/ppermute | solution.py:28
  12.8 95.0 %collective-permute-start.1 = (f32[1,1,128,256]{3,2,1,0:T(8,128)}, f32[1,1,128,256]{3,2,1,0:T(8,128)}, u32[]{:S(2)}, u32[]{:S(2)}) collective-permute-start(f32[1,1,128,256]{3,2,1,0:T(8,128)} %param.9), channel_id=1, source_target_pairs={{2,0},{4,2},{6,4},{3,1},{5,3},{7,5},{10,8},{12,10},{14,12},{11,9},... | collective-permute-start | bytes 393224 | tf_op jit(solution)/shard_map/ppermute | solution.py:31
  16.1 80.2 %copy-start.3 = (f32[256,256]{1,0:T(8,128)}, f32[256,256]{1,0:T(8,128)S(1)}, u32[]{:S(2)}) copy-start(f32[256,256]{1,0:T(8,128)S(1)} %fusion.63) | copy-start | bytes 786436
  19.0 177.2 %copy-start.7 = (f32[16,128,16]{1,2,0:T(8,128)}, f32[16,128,16]{1,2,0:T(8,128)S(1)}, u32[]{:S(2)}) copy-start(f32[16,128,16]{1,2,0:T(8,128)S(1)} %copy.33) | copy-start | bytes 393220
  20.1 3.5 copy-start.12
  94.1 1.6 copy-start.6
  96.3 7.2 %copy-start = (f32[8,256,512]{2,1,0:T(8,128)}, f32[8,256,512]{2,1,0:T(8,128)S(1)}, u32[]{:S(2)}) copy-start(f32[8,256,512]{2,1,0:T(8,128)S(1)} %bitcast_convert_fusion) | copy-start | bytes 12582916
  103.5 1.6 copy-start.9
  105.0 138.4 %all-reduce.9.cloned.1.call-start = ((), (), s32[]{:S(2)}) async-start(), calls=%async_computation.3 | async-start | bytes 262144 | tf_op jit(solution)/shard_map/psum | solution.py:162
  108.8 91.5 %collective-permute-start.2 = (f32[1,3,1,256]{3,2,1,0:T(1,128)S(1)}, f32[1,3,1,256]{3,2,1,0:T(1,128)S(1)}, u32[]{:S(2)}, u32[]{:S(2)}) collective-permute-start(f32[1,3,1,256]{3,2,1,0:T(1,128)S(1)} %get-tuple-element.22), channel_id=1, source_target_pairs={{0,1},{2,3},{4,5},{6,7},{8,9},{10,11},{12,13},{14,15},{16,17},{18,... | collective-permute-start | bytes 9224 | tf_op jit(solution)/shard_map/ppermute | solution.py:28
  110.2 90.0 %collective-permute-start.3 = (f32[1,3,1,256]{3,2,1,0:T(1,128)S(1)}, f32[1,3,1,256]{3,2,1,0:T(1,128)S(1)}, u32[]{:S(2)}, u32[]{:S(2)}) collective-permute-start(f32[1,3,1,256]{3,2,1,0:T(1,128)S(1)} %get-tuple-element.23), channel_id=1, source_target_pairs={{1,0},{3,2},{5,4},{7,6},{9,8},{11,10},{13,12},{15,14},{17,16},{19,... | collective-permute-start | bytes 9224 | tf_op jit(solution)/shard_map/ppermute | solution.py:31
  196.1 4.2 %copy-start.2 = (f32[128,512]{1,0:T(8,128)S(1)}, f32[128,512]{1,0:T(8,128)}, u32[]{:S(2)}) copy-start(f32[128,512]{1,0:T(8,128)} %reduce-scatter.3.cloned.1.call-done) | copy-start | bytes 786436
  199.3 45.2 %copy-start.8 = (f32[16,128,16]{1,2,0:T(8,128)S(1)}, f32[16,128,16]{1,2,0:T(8,128)}, u32[]{:S(2)}) copy-start(f32[16,128,16]{1,2,0:T(8,128)} %copy-done.7) | copy-start | bytes 393220
  200.2 141.2 %reduce-scatter.5.cloned.1.call-start = ((), (), s32[]{:S(2)}) async-start(), calls=%async_computation.4 | async-start | bytes 786432 | tf_op jit(solution)/shard_map/reduce_scatter | solution.py:183
  200.3 133.0 %collective-permute-start.4 = (f32[1,1,128,512]{3,2,1,0:T(8,128)S(1)}, f32[1,1,128,512]{3,2,1,0:T(8,128)}, u32[]{:S(2)}, u32[]{:S(2)}) collective-permute-start(f32[1,1,128,512]{3,2,1,0:T(8,128)S(1)} %bitcast.115), channel_id=1, source_target_pairs={{0,2},{2,4},{4,6},{1,3},{3,5},{5,7},{8,10},{10,12},{12,14},{9,11},... | collective-permute-start | bytes 786440 | tf_op jit(solution)/shard_map/ppermute | solution.py:28
  204.7 128.7 %collective-permute-start.5 = (f32[1,1,128,512]{3,2,1,0:T(8,128)S(1)}, f32[1,1,128,512]{3,2,1,0:T(8,128)}, u32[]{:S(2)}, u32[]{:S(2)}) collective-permute-start(f32[1,1,128,512]{3,2,1,0:T(8,128)S(1)} %bitcast.116), channel_id=1, source_target_pairs={{2,0},{4,2},{6,4},{3,1},{5,3},{7,5},{10,8},{12,10},{14,12},{11,9},... | collective-permute-start | bytes 786440 | tf_op jit(solution)/shard_map/ppermute | solution.py:31
  322.6 1.0 copy-start.4
  323.6 7.2 %copy-start.1 = (f32[8,256,512]{2,1,0:T(8,128)S(1)}, f32[8,256,512]{2,1,0:T(8,128)}, u32[]{:S(2)}) copy-start(f32[8,256,512]{2,1,0:T(8,128)} %copy-done) | copy-start | bytes 12582916
  330.8 1.5 copy-start.5
  330.8 1.5 copy-start.10
  334.1 3.2 collective-permute-start.6
  335.5 3.1 collective-permute-start.7
Sparse Core Ops, SparseCore 0:
  105.2 10.2 reduce-scatter.2
  200.3 43.1 all-reduce.8
  332.4 7.9 reduce-scatter.4
where the time goes:
time: 400 us; the launch traced here: 393 us
  local copies, waits for them, and re-layouts  151 us (38%)
  matrix products  97.8 us (24%)
  blocking collectives  42.5 us (11%)
  waiting for transfers between devices  41.9 us (10%)
  other arithmetic  24.5 us (6%)
  starting transfers between devices  18 us (4%)
  between operations  16.7 us (4%)
    reshape x2, local copies, waits for them, and re-layouts, from_tiles(): return shaped.transpose(2, 0, 4, 3, 1, 5).reshape(count, NY, 2 * NX)  56.4 us
    psum x1, blocking collectives, on_device(): norm_now = lax.psum(jnp.sum(mine * mine), ('band', 'grp', 'row'))  39.7 us
    dot_general x3, matrix products, along_rows(): mixed = jnp.einsum('ky,cyx->ckx', matrix, data, precision=highest)  39.3 us
    psum x1, waiting for transfers between devices, predict(): return lax.psum(turned.transpose(1, 2, 0, 3), 'band')  36.7 us
    reshape x1, local copies, waits for them, and re-layouts, to_tiles(): return shaped.transpose(1, 4, 0, 3, 2, 5).reshape(NTILES, count * 2, TY, TX)  34.2 us
    dot_general x2, matrix products, back_project(): summed = jnp.dot(selector, spread.reshape(NBLK, -1), precision=highest)  30.3 us
    transpose x2, local copies, waits for them, and re-layouts, from_tiles(): return shaped.transpose(2, 0, 4, 3, 1, 5).reshape(count, NY, 2 * NX)  22.7 us
    dot_general x3, matrix products, along_columns(): return jnp.dot(flat, matrix, precision=highest).reshape(data.shape)  21.4 us
  transfers between devices with their start and end apart: 11, of which 3 were waited for; matrix products, arithmetic and copies ran while one was open for 69% of the time, Pallas kernels for 0%

commit v1 on v0

v1 whole, which is shorter than its diff:
```python
import functools
import math

import jax
import jax.numpy as jnp
import ml_dtypes
import numpy as np
from jax import lax
from jax.experimental import pallas as pl
from jax.experimental.pallas import tpu as pltpu
from jax.sharding import PartitionSpec as P

reg_strength = 0.5
damping = 1.0
f32 = jnp.float32
bf16 = jnp.bfloat16
VMEM = pl.BlockSpec(memory_space=pltpu.VMEM)
SMEM = pl.BlockSpec(memory_space=pltpu.SMEM)
HBM = pl.BlockSpec(memory_space=pltpu.HBM)
TN = (((0,), (0,)), ((), ()))
NT = (((1,), (1,)), ((), ()))
large_vmem = 20 * 1024 * 1024
small_vmem = 8 * 1024 * 1024


def dft_table(length):
    index = np.arange(length)
    angle = (index[:, None] * index[None, :] % length) * (2.0 * np.pi / length)
    parts = []
    for part in (np.cos(angle) / math.sqrt(length), -np.sin(angle) / math.sqrt(length)):
        high = part.astype(ml_dtypes.bfloat16)
        low = (part - high.astype(np.float64)).astype(ml_dtypes.bfloat16)
        parts += [high, low]
    return np.concatenate(parts, axis=0)


def split(values):
    high = values.astype(bf16)
    return high, (values - high.astype(f32)).astype(bf16)


def matmul(left, right):
    return jnp.dot(left, right, preferred_element_type=f32)


def quarter_turn(cycle, block):
    turn = lax.rem(cycle * block, 4)
    one, zero = jnp.float32(1.0), jnp.float32(0.0)
    cosine = jnp.where(turn == 0, one, zero) - jnp.where(turn == 2, one, zero)
    sine = jnp.where(turn == 1, one, zero) - jnp.where(turn == 3, one, zero)
    return cosine, sine


def spread(values, row_weight, whigh, wlow, xhigh, xlow, k, coils, ty):
    weighted = values[:, None, :] * row_weight[None, :, :]
    parts = split(weighted.reshape(coils * ty, values.shape[1]))
    sb = values.shape[1] // 2
    vhigh, vlow = (
        jnp.concatenate([part, jnp.concatenate([part[:, sb:], -part[:, :sb]], axis=1)], axis=0) for part in parts
    )
    rows = matmul(
        jnp.concatenate([vhigh, vlow, vhigh], axis=1),
        jnp.concatenate([whigh, whigh, wlow], axis=0),
    )
    high, low = split(rows)
    half = xhigh.shape[1] // 2
    for part in range(2):
        there = pl.ds(part * half + k * ty, ty)
        for c in range(coils):
            here = slice((part * coils + c) * ty, (part * coils + c + 1) * ty)
            xhigh[c, there, :] = high[here]
            xlow[c, there, :] = low[here]


def back_rows(table, xhigh, xlow, coil, coils, out_rows):
    nx = xhigh.shape[2]
    real_sum = imag_sum = None
    for c in range(coils):
        high, low = xhigh[c], xlow[c]
        image = matmul(table, jnp.concatenate([high, high, low], axis=0))
        real, imag = image[:out_rows], image[out_rows:]
        coil_real = coil[c, :, :nx].astype(f32)
        coil_imag = coil[c, :, nx:].astype(f32)
        real_term = coil_real * real + coil_imag * imag
        imag_term = coil_real * imag - coil_imag * real
        real_sum = real_term if c == 0 else real_sum + real_term
        imag_sum = imag_term if c == 0 else imag_sum + imag_term
    return real_sum, imag_sum


def rhs_kernel(
    coils, blocks, place_ref, tile_ref, cycle_ref, table_ref, cols_ref, rows_ref, data_ref, weight_ref, coil_any,
    part_ref, whigh, wlow, adj, row_weight_ref, coil, xhigh, xlow, sem,
):
    ny = table_ref.shape[1]
    ty, tx = rows_ref.shape[0], cols_ref.shape[0]
    sb = rows_ref.shape[1] // blocks
    width = blocks * ty
    fetch = pltpu.make_async_copy(coil_any, coil, sem)
    fetch.start()

    lane = lax.broadcasted_iota(jnp.int32, (ny, width), 1)
    wanted = lax.rem(lane, ty)
    for k in range(blocks):
        first = (tile_ref[k] // (ny // tx)) * ty
        wanted = wanted + jnp.where(lane // ty == k, first, 0)
    pick = (lax.broadcasted_iota(jnp.int32, (ny, width), 0) == wanted).astype(f32).astype(bf16)
    picked = matmul(table_ref[...], pick).astype(bf16)
    real_high, real_low, imag_high, imag_low = (picked[i * ny : (i + 1) * ny] for i in range(4))
    high = jnp.concatenate(
        [jnp.concatenate([real_high, imag_high], axis=1), jnp.concatenate([-imag_high, real_high], axis=1)], axis=0
    )
    low = jnp.concatenate(
        [jnp.concatenate([real_low, imag_low], axis=1), jnp.concatenate([-imag_low, real_low], axis=1)], axis=0
    )
    adj[:, : 2 * width] = high
    adj[:, 2 * width : 4 * width] = low
    adj[:, 4 * width :] = high

    for k in range(blocks):
        left = pl.multiple_of(lax.rem(tile_ref[k], ny // tx) * tx, tx)
        chosen = [table_ref[pl.ds(i * ny + left, tx), :] for i in range(4)]
        stacked = jnp.concatenate(
            [jnp.concatenate([chosen[0], chosen[2]], axis=1), jnp.concatenate([chosen[1], chosen[3]], axis=1)], axis=0
        )
        here = slice(k * sb, (k + 1) * sb)
        cols = cols_ref[:, here]
        mixed = lax.dot_general(
            jnp.concatenate([cols, cols], axis=0), stacked, TN, preferred_element_type=f32
        )
        for ref, part in zip((whigh, wlow), split(mixed)):
            ref[k, :sb, :] = part[:, :ny]
            ref[k, sb:, :] = part[:, ny:]
        turned = rows_ref[:, here].astype(f32)
        row_weight = jnp.concatenate([turned, turned], axis=1)
        row_weight_ref[k] = row_weight
        cosine, sine = quarter_turn(cycle_ref[0], k)
        real, imag = data_ref[:, 0, here], data_ref[:, 1, here]
        values = jnp.concatenate([cosine * real + sine * imag, cosine * imag - sine * real], axis=1)
        spread(values, row_weight, whigh[k], wlow[k], xhigh, xlow, k, coils, ty)

    fetch.wait()
    real_sum, imag_sum = back_rows(adj[...], xhigh, xlow, coil, coils, ny)
    part_ref[:ny, :] = jnp.concatenate([real_sum, imag_sum], axis=1)
    count = weight_ref.shape[0]
    edge = jnp.concatenate([weight_ref[0:1, :], weight_ref[count - 1 : count, :]], axis=0)
    edge = jnp.concatenate([edge, jnp.zeros((6, edge.shape[1]), f32)], axis=0)
    part_ref[ny:, :] = jnp.concatenate([edge, jnp.zeros_like(edge)], axis=1)


def sum_kernel(ny, count, place_ref, weight_ref, *refs):
    parts, (image_ref, packed_ref) = refs[:-2], refs[-2:]
    total = parts[0][:ny, :]
    for part in parts[1:]:
        total = total + part[:ny, :]
    image_ref[...] = total
    start = pl.multiple_of(place_ref[0] * count, count)
    width = total.shape[1]
    packed_ref[:, :width] = image_ref[pl.ds(start, count), :]
    packed_ref[:, width:] = weight_ref[...]


def predict_kernel(
    coils, blocks, tile_ref, cycle_ref, table_ref, row_weight_ref, image_ref, coil, whigh, wlow,
    out_ref, fwd, thigh, tlow,
):
    ny = table_ref.shape[1]
    nx = image_ref.shape[1] // 2
    ty = row_weight_ref.shape[1]
    sb = row_weight_ref.shape[2] // 2
    width = blocks * ty
    for k in range(blocks):
        top = pl.multiple_of((tile_ref[k] // (nx // ty)) * ty, ty)
        real_high, real_low, imag_high, imag_low = (table_ref[pl.ds(i * ny + top, ty), :] for i in range(4))
        upper, lower = slice(k * ty, (k + 1) * ty), slice(width + k * ty, width + (k + 1) * ty)
        for place, real, imag in ((0, real_high, imag_high), (2, real_low, imag_low), (4, real_high, imag_high)):
            fwd[upper, place * ny : (place + 1) * ny] = real
            fwd[upper, (place + 1) * ny : (place + 2) * ny] = -imag
            fwd[lower, place * ny : (place + 1) * ny] = imag
            fwd[lower, (place + 1) * ny : (place + 2) * ny] = real
    image_real, image_imag = image_ref[:, :nx], image_ref[:, nx:]
    for c in range(coils):
        coil_real = coil[c, :, :nx].astype(f32)
        coil_imag = coil[c, :, nx:].astype(f32)
        product = jnp.concatenate(
            [coil_real * image_real - coil_imag * image_imag, coil_real * image_imag + coil_imag * image_real], axis=0
        )
        high, low = split(product)
        grid = matmul(fwd[...], jnp.concatenate([high, high, low], axis=0))
        for ref, part in zip((thigh, tlow), split(grid)):
            ref[:, 0, c * ty : (c + 1) * ty, :] = part[:width].reshape(blocks, ty, nx)
            ref[:, 1, c * ty : (c + 1) * ty, :] = part[width:].reshape(blocks, ty, nx)
    for k in range(blocks):
        left_high, left_low = (ref[k].reshape(2 * coils * ty, nx) for ref in (thigh, tlow))
        right_high = whigh[k]
        mixed = lax.dot_general(
            jnp.concatenate([left_high, left_low, left_high], axis=1),
            jnp.concatenate([right_high, right_high, wlow[k]], axis=1),
            NT,
            preferred_element_type=f32,
        )
        of_real, of_imag = mixed[: coils * ty], mixed[coils * ty :]
        product = jnp.concatenate(
            [of_real[:, :sb] - of_imag[:, sb:], of_real[:, sb:] + of_imag[:, :sb]], axis=1
        )
        summed = jnp.sum(product.reshape(coils, ty, 2 * sb) * row_weight_ref[k][None, :, :], axis=1)
        real, imag = summed[:, :sb], summed[:, sb:]
        cosine, sine = quarter_turn(cycle_ref[0], k)
        out_ref[k] = jnp.concatenate([cosine * real - sine * imag, sine * real + cosine * imag], axis=1)


def image_kernel(
    coils, blocks, place_ref, cycle_ref, row_weight_ref, collapsed_ref, adj, coil, whigh, wlow, *refs,
):
    *out_refs, whole, xhigh, xlow = refs
    ty = row_weight_ref.shape[1]
    sb = row_weight_ref.shape[2] // 2
    for k in range(blocks):
        cosine, sine = quarter_turn(cycle_ref[0], k)
        real, imag = collapsed_ref[k, :, :sb], collapsed_ref[k, :, sb:]
        values = jnp.concatenate([cosine * real + sine * imag, cosine * imag - sine * real], axis=1)
        spread(values, row_weight_ref[k], whigh[k], wlow[k], xhigh, xlow, k, coils, ty)
    real_sum, imag_sum = back_rows(adj[...], xhigh, xlow, coil, coils, whole.shape[0])
    whole[...] = jnp.concatenate([real_sum, imag_sum], axis=1)
    for shift, out_ref in enumerate(out_refs):
        count = out_ref.shape[0]
        start = lax.rem(place_ref[0] + shift, whole.shape[0] // count) * count
        out_ref[...] = whole[pl.ds(pl.multiple_of(start, count), count), :]


def smooth_kernel(place_ref, image_ref, own_ref, low_ref, high_ref, before_ref, after_ref, out_ref, sums_ref):
    count = own_ref.shape[0]
    width = image_ref.shape[1]
    nx = width // 2
    place, places = place_ref[0], place_ref[1]
    total_rows = image_ref.shape[0]
    start = place * count
    weight = own_ref[:, width:]
    none = jnp.zeros((1, nx), f32)
    weight_up = jnp.where(place > 0, before_ref[total_rows + 1 : total_rows + 2, :nx], none)
    weight_down = jnp.where(place < places - 1, after_ref[total_rows : total_rows + 1, :nx], none)
    image_up = image_ref[pl.ds(jnp.maximum(start - 1, 0), 1), :]
    image_down = image_ref[pl.ds(jnp.minimum(start + count, total_rows - 1), 1), :]
    row = lax.broadcasted_iota(jnp.int32, (count, nx), 0)
    column = lax.broadcasted_iota(jnp.int32, (count, nx), 1)

    def above(values, edge):
        return jnp.where(row == 0, edge, pltpu.roll(values, 1, 0))

    def below(values, edge):
        return jnp.where(row == count - 1, edge, pltpu.roll(values, count - 1, 0))

    weight_left = jnp.where(column == 0, 0.0, pltpu.roll(weight, 1, 1))
    weight_right = jnp.where(column == nx - 1, 0.0, pltpu.roll(weight, nx - 1, 1))
    weight_above, weight_below = above(weight, weight_up), below(weight, weight_down)
    weight_low, weight_high = low_ref[:, width:], high_ref[:, width:]
    squares = curvature = 0.0
    for part in range(2):
        lanes = slice(part * nx, (part + 1) * nx)
        here = own_ref[:, lanes]
        flux = weight_low * (here - low_ref[:, lanes]) + weight_high * (here - high_ref[:, lanes])
        flux += weight_above * (here - above(here, image_up[:, lanes]))
        flux += weight_below * (here - below(here, image_down[:, lanes]))
        flux += weight_left * (here - pltpu.roll(here, 1, 1))
        flux += weight_right * (here - pltpu.roll(here, nx - 1, 1))
        result = reg_strength * (weight * flux) + damping * here
        out_ref[:, lanes] = result
        squares += jnp.sum(here * here)
        curvature += jnp.sum(here * result)
    lane = lax.broadcasted_iota(jnp.int32, sums_ref.shape, 1)
    sums_ref[...] = jnp.where(lane == 0, squares, jnp.where(lane == 1, curvature, 0.0))


def collapse_kernel(sums_ref, *refs):
    parts, (out_ref, out_sums_ref) = refs[:-2], refs[-2:]
    total = parts[0][...]
    for part in parts[1:]:
        total = total + part[...]
    out_ref[...] = total
    lane = lax.broadcasted_iota(jnp.int32, sums_ref.shape, 1)
    out_sums_ref[...] = sums_ref[...] + jnp.where(lane == 1, jnp.sum(total * total), 0.0)


def call(kernel, outs, specs, out_specs, scratch=(), flops=0, nbytes=0, limit=small_vmem):
    return pl.pallas_call(
        kernel,
        out_shape=outs,
        in_specs=specs,
        out_specs=out_specs,
        scratch_shapes=scratch,
        compiler_params=pltpu.CompilerParams(vmem_limit_bytes=limit),
        cost_estimate=pl.CostEstimate(flops=flops, bytes_accessed=nbytes, transcendentals=0),
    )


def shape(dims, dtype=f32):
    return jax.ShapeDtypeStruct(dims, dtype)


def sum_over(values, axes):
    for axis in axes:
        count = lax.axis_size(axis)
        step = 1
        if count & (count - 1):
            values = lax.psum(values, axis)
            continue
        while step < count:
            values = values + lax.ppermute(values, axis, [(i, i ^ step) for i in range(count)])
            step *= 2
    return values


def from_others(values, axis):
    count = lax.axis_size(axis)
    return [
        lax.ppermute(values, axis, [(i, (i + shift) % count) for i in range(count)]) for shift in range(1, count)
    ]


def on_device(kspace_data, coil_maps, smooth_weight, kernel_cols, kernel_rows, tile_index, caipi_cycle):
    profiles, data, weight = coil_maps[0, 0], kspace_data[0], smooth_weight[0, 0]
    coils, ny, width = profiles.shape
    nx = width // 2
    blocks = tile_index.shape[0]
    samples, ty = kernel_rows.shape
    sb = samples // blocks
    count = weight.shape[0]
    bands, rows, groups = lax.axis_size("band"), lax.axis_size("row"), lax.axis_size("grp")
    row_place = lax.axis_index("row")
    table = jnp.asarray(dft_table(ny))
    wide = blocks * ty
    w_shape = (blocks, 2 * sb, nx)
    row_flops = 2 * 3 * coils * (2 * wide) * (2 * ny) * nx
    col_flops = 2 * 3 * coils * ty * blocks * (2 * sb) * width
    place = jnp.stack([row_place, jnp.int32(rows)])
    dma = pltpu.SemaphoreType.DMA
    x_scratch = [pltpu.VMEM((coils, 2 * wide, nx), bf16)] * 2

    data, weight, profiles, cols, rows_of, tile_index = (
        pltpu.with_memory_space_constraint(x, pltpu.HBM)
        for x in (data, weight, profiles, kernel_cols.T, kernel_rows.T, tile_index)
    )
    partial, *kept = call(
        functools.partial(rhs_kernel, coils, blocks),
        [
            shape((ny + 8, width)),
            pltpu.VMEM(w_shape, bf16),
            pltpu.VMEM(w_shape, bf16),
            pltpu.VMEM((2 * ny, 6 * wide), bf16),
            pltpu.VMEM((blocks, ty, 2 * sb), f32),
            pltpu.VMEM(profiles.shape, bf16),
        ],
        [SMEM, SMEM, SMEM, VMEM, VMEM, VMEM, VMEM, VMEM, HBM],
        [VMEM] * 6,
        [*x_scratch, dma],
        row_flops + 2 * col_flops,
        limit=large_vmem,
    )(place, tile_index, caipi_cycle, table, cols, rows_of, data, weight, profiles)

    whigh, wlow, adj, row_weight, coil = (pltpu.with_memory_space_constraint(x, pltpu.VMEM) for x in kept)

    received = from_others(partial, "row")
    image, packed = call(
        functools.partial(sum_kernel, ny, count),
        [shape((ny, width)), shape((count, width + nx))],
        [SMEM] + [VMEM] * (2 + len(received)),
        [VMEM, VMEM],
    )(place, weight, partial, *received)

    low = lax.ppermute(packed, "grp", [(i, i + 1) for i in range(groups - 1)])
    high = lax.ppermute(packed, "grp", [(i + 1, i) for i in range(groups - 1)])

    predicted = call(
        functools.partial(predict_kernel, coils, blocks),
        shape((blocks, coils, 2 * sb)),
        [SMEM, SMEM] + [VMEM] * 6,
        VMEM,
        [
            pltpu.VMEM((2 * wide, 6 * ny), bf16),
            *[pltpu.VMEM((blocks, 2, coils * ty, nx), bf16)] * 2,
        ],
        row_flops + col_flops,
        limit=large_vmem,
    )(tile_index, caipi_cycle, table, row_weight, image, coil, whigh, wlow)

    others = from_others(predicted, "band")
    smoothed, sums = call(
        smooth_kernel,
        [shape((count, width)), shape((8, 128))],
        [SMEM] + [VMEM] * 6,
        [VMEM, VMEM],
    )(place, image, packed, low, high, received[0], received[-1])
    sums = sum_over(sums, ("band",))
    collapsed, sums = call(
        collapse_kernel,
        [shape(predicted.shape), shape((8, 128))],
        [VMEM] * (2 + len(others)),
        [VMEM, VMEM],
    )(sums, predicted, *others)

    halves = call(
        functools.partial(image_kernel, coils, blocks),
        [shape((count, width))] * 2 if rows == 2 else [shape((ny, width))],
        [SMEM, SMEM] + [VMEM] * 6,
        [VMEM] * (2 if rows == 2 else 1),
        [pltpu.VMEM((ny, width), f32), *x_scratch],
        row_flops + col_flops,
        limit=large_vmem,
    )(place, caipi_cycle, row_weight, collapsed, adj, coil, whigh, wlow)
    sums = sum_over(sums, ("row", "grp"))

    if rows == 2:
        normal = halves[0] + lax.ppermute(halves[1], "row", [(0, 1), (1, 0)])
    else:
        normal = lax.psum_scatter(halves[0], "row", scatter_dimension=0, tiled=True)
    alpha = sums[0, 0] / sums[0, 1]
    direction = packed[:, :width]
    solution_field = alpha * direction
    residual = direction - alpha * (normal + smoothed)
    return solution_field[None, None], residual[None, None]


def solution(mesh):
    return jax.shard_map(
        on_device,
        mesh=mesh,
        in_specs=(
            P("grp", "row", None, None),
            P("band", "grp", "row", None, None),
            P("band", "grp", "row", None),
            P(),
            P(),
            P(),
            P("band"),
        ),
        out_specs=(P("band", "grp", "row", None), P("band", "grp", "row", None)),
        check_vma=False,
    )
```

time: 400 us -> 60.8 us (0.15); the launches traced: 393 us -> 60.5 us
  local copies, waits for them, and re-layouts: 151 us -> 1.63 us
  matrix products: 97.8 us -> 0 us
  blocking collectives: 42.5 us -> 0 us
  waiting for transfers between devices: 41.9 us -> 10.7 us
  Pallas kernels: 0 us -> 24.7 us
  other arithmetic: 24.5 us -> 0.97 us
  between operations: 16.7 us -> 2.72 us
    reshape x9 -> x0, local copies, waits for them, and re-layouts: 115 us -> none  [the longest x2 56.4 us: from_tiles(): return shaped.transpose(2, 0, 4, 3, 1, 5).reshape(count, NY, 2 * NX)]
    dot_general x11 -> x0, matrix products: 97.8 us -> none  [the longest x3 39.3 us: along_rows(): mixed = jnp.einsum('ky,cyx->ckx', matrix, data, precision=highest)]
    psum x1 -> x0, blocking collectives: 39.7 us -> none  [on_device(): norm_now = lax.psum(jnp.sum(mine * mine), ('band', 'grp', 'row'))]
    psum x1 -> x0, waiting for transfers between devices: 36.7 us -> none  [predict(): return lax.psum(turned.transpose(1, 2, 0, 3), 'band')]
    pallas_call x0 -> x6, Pallas kernels: none -> 24.7 us  [the longest x1 9.81 us: on_device(): call(functools.partial(rhs_kernel, coils, blocks), [shape((ny + 8, width)...]
    transpose x2 -> x0, local copies, waits for them, and re-layouts: 22.7 us -> none  [from_tiles(): return shaped.transpose(2, 0, 4, 3, 1, 5).reshape(count, NY, 2 * NX)]
    ppermute x8 -> x12, waiting for transfers between devices: 1.21 us -> 10.7 us  [the longest x5 8.45 us: sum_over(): lax.ppermute(values, axis, [(i, i ^ step) for i in range(count)])]
    concatenate x6 -> x0, other arithmetic: 6.25 us -> none  [the longest x1 2.53 us: along_rows(): return jnp.concatenate([real_part, imag_part], axis=-1)]
  transfers between devices with their start and end apart: 11 -> 12, of which waited for: 3 -> 7; matrix products, arithmetic and copies ran while one was open for 69% -> 1% of each run, Pallas kernels for 0% -> 12%
where the time goes in v1:
time: 60.8 us; the launch traced here: 60.5 us
  Pallas kernels  24.7 us (41%)
  starting transfers between devices  19.8 us (33%)
  waiting for transfers between devices  10.7 us (18%)
  between operations  2.72 us (4%)
  local copies, waits for them, and re-layouts  1.63 us (3%)
  other arithmetic  0.97 us (2%)
    pallas_call x1, Pallas kernels, on_device(): call(functools.partial(rhs_kernel, coils, blocks), [shape((ny + 8, width)...  9.81 us
    ppermute x5, starting transfers between devices, sum_over(): lax.ppermute(values, axis, [(i, i ^ step) for i in range(count)])  8.52 us
    ppermute x5, waiting for transfers between devices, sum_over(): lax.ppermute(values, axis, [(i, i ^ step) for i in range(count)])  8.45 us
    pallas_call x1, Pallas kernels, on_device(): call(functools.partial(image_kernel, coils, blocks), [shape((count, width...  6.41 us
    pallas_call x1, Pallas kernels, on_device(): call(functools.partial(predict_kernel, coils, blocks), shape((blocks, coi...  6.29 us
    ppermute x4, starting transfers between devices, from_others(): lax.ppermute(values, axis, [(i, (i + shift) % count) for i in range(count)])  5.03 us
    ppermute x1, starting transfers between devices, on_device(): low = lax.ppermute(packed, 'grp', [(i, i + 1) for i in range(groups - 1)])  4.87 us
    ppermute x4, waiting for transfers between devices, from_others(): lax.ppermute(values, axis, [(i, (i + shift) % count) for i in range(count)])  1.57 us
  transfers between devices with their start and end apart: 12, of which 7 were waited for; matrix products, arithmetic and copies ran while one was open for 1% of the time, Pallas kernels for 12%

profile of v1, /device:TPU:0, one launch (start us, length us, event | category | flops | bytes accessed | tf_op | source)
XLA Modules:
  0.0 60.5 jit_solution(6218946910336120788)
XLA Ops:
  1.3 0.1 pad_add_fusion.place_ref
  1.4 1.0 %copy-done = bf16[1024,256]{1,0:T(8,128)(2,1)S(1)} copy-done((bf16[1024,256]{1,0:T(8,128)(2,1)S(1)}, bf16[1024,256]{1,0:T(8,128)(2,1)}, u32[]{:S(2)}) %copy-start) | copy-done | bytes 524312
  2.4 9.8 %shard_map.95 = (f32[264,512]{1,0:T(8,128)S(1)}, bf16[16,256,256]{2,1,0:T(8,128)(2,1)S(1)}, bf16[16,256,256]{2,1,0:T(8,128)(2,1)S(1)}, bf16[512,1536]{1,0:T(8,12...) custom-call(s32[2]{0:T(128)S(1)} %pad_add_fusion.place_ref, s32[16]{0:T(128)} %tile_ref.3, ...), custom_call_target="tpu_custom_call" | custom-call | flops 6442450944 | tf_op jit(solution)/shard_map/pallas_call | solution.py:343
  12.2 0.5 collective-permute-start
  12.7 1.6 %collective-permute-done.refs_1_.before_ref.after_ref = f32[264,512]{1,0:T(8,128)S(1)} collective-permute-done((f32[264,512]{1,0:T(8,128)S(1)}, f32[264,512]{1,0:T(8,128)S(1)}, u32[]{:S(2)}, u32[]{:S(2)}) %collective-permute-start) | collective-permute-done | bytes 540704 | tf_op jit(solution)/shard_map/ppermute | solution.py:316
  14.3 1.0 %shard_map.96 = (f32[256,512]{1,0:T(8,128)S(1)}, f32[128,768]{1,0:T(8,128)S(1)}) custom-call(s32[2]{0:T(128)S(1)} %pad_add_fusion.place_ref, f32[128,256]{1,0:T(8,128)} %bitcast.12, f32[264,512]{1,0:T(8,128)S(1)} %get-tuple-element.16.refs_0_, f32[264,512]{1,0:T(8,128)S(1)} %collective-permute-done.refs_1_.before_ref.after_ref), custom_call_target="tpu_custom_call" | custom-call | tf_op jit(solution)/shard_map/pallas_call | solution.py:363
  15.3 4.9 %collective-permute-start.1 = (f32[128,768]{1,0:T(8,128)S(1)}, f32[128,768]{1,0:T(8,128)S(1)}, u32[]{:S(2)}, u32[]{:S(2)}) collective-permute-start(f32[128,768]{1,0:T(8,128)S(1)} %get-tuple-element.18.own_ref), channel_id=1, source_target_pairs={{0,2},{2,4},{4,6},{1,3},{3,5},{5,7},{8,10},{10,12},{12,14},{9,11},... | collective-permute-start | bytes 1179656 | tf_op jit(solution)/shard_map/ppermute | solution.py:370
  20.2 1.3 %collective-permute-start.2 = (f32[128,768]{1,0:T(8,128)S(1)}, f32[128,768]{1,0:T(8,128)S(1)}, u32[]{:S(2)}, u32[]{:S(2)}) collective-permute-start(f32[128,768]{1,0:T(8,128)S(1)} %get-tuple-element.18.own_ref), channel_id=1, source_target_pairs={{2,0},{4,2},{6,4},{3,1},{5,3},{7,5},{10,8},{12,10},{14,12},{11,9},... | collective-permute-start | bytes 1179656 | tf_op jit(solution)/shard_map/ppermute | solution.py:371
  21.5 6.3 %shard_map.98.refs_0_ = f32[16,8,256]{2,1,0:T(8,128)S(1)} custom-call(s32[16]{0:T(128)} %tile_ref.3, s32[1]{0:T(128)S(6)} %copy.10.cycle_ref, bf16[1024,256]{1,0:T(8,128)(2,1)S(1)} %copy-done, f32[16,16,256]{2,1,0:T(8,128)S(1)} %get-tuple-element.20.row_weight_ref, f32[256,512]{1,0:T(8,128)S(1)} %get-tuple-element.17.image_ref, ...), custom_call_target="tpu_custom_call" | custom-call | flops 4831838208 | tf_op jit(solution)/shard_map/pallas_call | solution.py:373
  27.8 1.5 %collective-permute-start.5 = (f32[16,8,256]{2,1,0:T(8,128)S(1)}, f32[16,8,256]{2,1,0:T(8,128)S(1)}, u32[]{:S(2)}, u32[]{:S(2)}) collective-permute-start(f32[16,8,256]{2,1,0:T(8,128)S(1)} %shard_map.98.refs_0_), channel_id=1, source_target_pairs={{0,8},{8,16},{16,24},{24,0},{1,9},{9,17},{17,25},{25,1},{2,10},{10... | collective-permute-start | bytes 393224 | tf_op jit(solution)/shard_map/ppermute | solution.py:316
  29.3 1.5 %collective-permute-start.6 = (f32[16,8,256]{2,1,0:T(8,128)S(1)}, f32[16,8,256]{2,1,0:T(8,128)S(1)}, u32[]{:S(2)}, u32[]{:S(2)}) collective-permute-start(f32[16,8,256]{2,1,0:T(8,128)S(1)} %shard_map.98.refs_0_), channel_id=1, source_target_pairs={{0,16},{8,24},{16,0},{24,8},{1,17},{9,25},{17,1},{25,9},{2,18},{10... | collective-permute-start | bytes 393224 | tf_op jit(solution)/shard_map/ppermute | solution.py:316
  30.8 1.4 %collective-permute-start.7 = (f32[16,8,256]{2,1,0:T(8,128)S(1)}, f32[16,8,256]{2,1,0:T(8,128)S(1)}, u32[]{:S(2)}, u32[]{:S(2)}) collective-permute-start(f32[16,8,256]{2,1,0:T(8,128)S(1)} %shard_map.98.refs_0_), channel_id=1, source_target_pairs={{0,24},{8,0},{16,8},{24,16},{1,25},{9,1},{17,9},{25,17},{2,26},{10... | collective-permute-start | bytes 393224 | tf_op jit(solution)/shard_map/ppermute | solution.py:316
  32.3 0.0 collective-permute-done.1.low_ref
  32.3 0.7 %collective-permute-done.2.high_ref = f32[128,768]{1,0:T(8,128)S(1)} collective-permute-done((f32[128,768]{1,0:T(8,128)S(1)}, f32[128,768]{1,0:T(8,128)S(1)}, u32[]{:S(2)}, u32[]{:S(2)}) %collective-permute-start.2) | collective-permute-done | bytes 393248 | tf_op jit(solution)/shard_map/ppermute | solution.py:371
  33.0 1.1 %shard_map.97 = (f32[128,512]{1,0:T(8,128)S(1)}, f32[8,128]{1,0:T(8,128)S(1)}) custom-call(s32[2]{0:T(128)S(1)} %pad_add_fusion.place_ref, f32[256,512]{1,0:T(8,128)S(1)} %get-tuple-element.17.image_ref, f32[128,768]{1,0:T(8,128)S(1)} %get-tuple-element.18.own_ref, f32[128,768]{1,0:T(8,128)S(1)} %collective-permute-done.1.low_ref, ...), custom_call_target="tpu_custom_call" | custom-call | tf_op jit(solution)/shard_map/pallas_call | solution.py:387
  34.0 1.5 %collective-permute-start.3 = (f32[8,128]{1,0:T(8,128)S(1)}, f32[8,128]{1,0:T(8,128)S(1)}, u32[]{:S(2)}, u32[]{:S(2)}) collective-permute-start(f32[8,128]{1,0:T(8,128)S(1)} %get-tuple-element.19), channel_id=1, source_target_pairs={{0,8},{8,0},{16,24},{24,16},{1,9},{9,1},{17,25},{25,17},{2,10},{10... | collective-permute-start | bytes 12296 | tf_op jit(solution)/shard_map/ppermute | solution.py:308
  35.6 2.1 %collective-permute-done.3 = f32[8,128]{1,0:T(8,128)S(1)} collective-permute-done((f32[8,128]{1,0:T(8,128)S(1)}, f32[8,128]{1,0:T(8,128)S(1)}, u32[]{:S(2)}, u32[]{:S(2)}) %collective-permute-start.3) | collective-permute-done | bytes 4128 | tf_op jit(solution)/shard_map/ppermute | solution.py:308
  37.7 1.5 %collective-permute-start.4 = (f32[8,128]{1,0:T(8,128)S(1)}, f32[8,128]{1,0:T(8,128)S(1)}, u32[]{:S(2)}, u32[]{:S(2)}) collective-permute-start(f32[8,128]{1,0:T(8,128)S(1)} %add.21), channel_id=1, source_target_pairs={{0,16},{8,24},{16,0},{24,8},{1,17},{9,25},{17,1},{25,9},{2,18},{10... | collective-permute-start | bytes 12296 | tf_op jit(solution)/shard_map/ppermute | solution.py:308
  39.2 2.1 %collective-permute-done.4 = f32[8,128]{1,0:T(8,128)S(1)} collective-permute-done((f32[8,128]{1,0:T(8,128)S(1)}, f32[8,128]{1,0:T(8,128)S(1)}, u32[]{:S(2)}, u32[]{:S(2)}) %collective-permute-start.4) | collective-permute-done | bytes 4128 | tf_op jit(solution)/shard_map/ppermute | solution.py:308
  41.3 0.0 collective-permute-done.5.refs_1_
  41.3 0.0 collective-permute-done.7.refs_3_
  41.3 0.2 shard_map.99
  41.5 6.4 %shard_map.100 = (f32[128,512]{1,0:T(8,128)S(1)}, f32[128,512]{1,0:T(8,128)S(1)}) custom-call(s32[2]{0:T(128)S(1)} %pad_add_fusion.place_ref, s32[1]{0:T(128)S(6)} %copy.10.cycle_ref, f32[16,16,256]{2,1,0:T(8,128)S(1)} %get-tuple-element.20.row_weight_ref, f32[16,8,256]{2,1,0:T(8,128)S(1)} %get-tuple-element.25.collapsed_ref, ...), custom_call_target="tpu_custom_call" | custom-call | flops 4831838208 | tf_op jit(solution)/shard_map/pallas_call | solution.py:401
  47.9 0.1 collective-permute-start.11
  48.0 0.5 collective-permute-start.8
  48.5 1.0 %collective-permute-done.8 = f32[8,128]{1,0:T(8,128)S(1)} collective-permute-done((f32[8,128]{1,0:T(8,128)S(1)}, f32[8,128]{1,0:T(8,128)S(1)}, u32[]{:S(2)}, u32[]{:S(2)}) %collective-permute-start.8) | collective-permute-done | bytes 4128 | tf_op jit(solution)/shard_map/ppermute | solution.py:308
  49.5 2.0 %collective-permute-start.9 = (f32[8,128]{1,0:T(8,128)S(1)}, f32[8,128]{1,0:T(8,128)S(1)}, u32[]{:S(2)}, u32[]{:S(2)}) collective-permute-start(f32[8,128]{1,0:T(8,128)S(1)} %add.23), channel_id=1, source_target_pairs={{0,2},{2,0},{4,6},{6,4},{1,3},{3,1},{5,7},{7,5},{8,10},{10,8},{12,... | collective-permute-start | bytes 12296 | tf_op jit(solution)/shard_map/ppermute | solution.py:308
  51.5 1.6 %collective-permute-done.9 = f32[8,128]{1,0:T(8,128)S(1)} collective-permute-done((f32[8,128]{1,0:T(8,128)S(1)}, f32[8,128]{1,0:T(8,128)S(1)}, u32[]{:S(2)}, u32[]{:S(2)}) %collective-permute-start.9) | collective-permute-done | bytes 4128 | tf_op jit(solution)/shard_map/ppermute | solution.py:308
  53.2 3.0 %collective-permute-start.10 = (f32[8,128]{1,0:T(8,128)S(1)}, f32[8,128]{1,0:T(8,128)S(1)}, u32[]{:S(2)}, u32[]{:S(2)}) collective-permute-start(f32[8,128]{1,0:T(8,128)S(1)} %add.24), channel_id=1, source_target_pairs={{0,4},{2,6},{4,0},{6,2},{1,5},{3,7},{5,1},{7,3},{8,12},{10,14},{12... | collective-permute-start | bytes 12296 | tf_op jit(solution)/shard_map/ppermute | solution.py:308
  56.1 1.6 %collective-permute-done.10 = f32[8,128]{1,0:T(8,128)S(1)} collective-permute-done((f32[8,128]{1,0:T(8,128)S(1)}, f32[8,128]{1,0:T(8,128)S(1)}, u32[]{:S(2)}, u32[]{:S(2)}) %collective-permute-start.10) | collective-permute-done | bytes 4128 | tf_op jit(solution)/shard_map/ppermute | solution.py:308
  57.7 0.6 fusion
  59.6 0.9 %subtract_bitcast_fusion = (f32[1,1,128,512]{3,2,1,0:T(8,128)}, f32[1,1,128,512]{3,2,1,0:T(8,128)}) fusion(f32[128,512]{1,0:T(8,128)S(1)} %get-tuple-element.29, f32[128,512]{1,0:T(8,128)S(1)} %get-tuple-element.27, f32[128,512]{1,0:T(8,128)S(1)} %collective-permute-done.11, f32[128,768]{1,0:T(8,128)S(1)} %get-tuple-element.18.own_ref, f32[]{:T(128)} %bitcast.6), kind=kLoop, calls=%fused_computation | loop fusion | flops 327680 | bytes 1572868 | tf_op jit(solution)/shard_map/broadcast_in_dim | solution.py:420
  (8 shorter events, 0.0 us)
Async XLA Ops:
  1.4 1.0 %copy-start = (bf16[1024,256]{1,0:T(8,128)(2,1)S(1)}, bf16[1024,256]{1,0:T(8,128)(2,1)}, u32[]{:S(2)}) copy-start(bf16[1024,256]{1,0:T(8,128)(2,1)} %constant.8.clone.table_ref) | copy-start | bytes 1572868
  12.2 2.1 %collective-permute-start = (f32[264,512]{1,0:T(8,128)S(1)}, f32[264,512]{1,0:T(8,128)S(1)}, u32[]{:S(2)}, u32[]{:S(2)}) collective-permute-start(f32[264,512]{1,0:T(8,128)S(1)} %get-tuple-element.16.refs_0_), channel_id=1, source_target_pairs={{0,1},{1,0},{2,3},{3,2},{4,5},{5,4},{6,7},{7,6},{8,9},{9,8},{10,11... | collective-permute-start | bytes 1622024 | tf_op jit(solution)/shard_map/ppermute | solution.py:316
  15.3 17.0 %collective-permute-start.1 = (f32[128,768]{1,0:T(8,128)S(1)}, f32[128,768]{1,0:T(8,128)S(1)}, u32[]{:S(2)}, u32[]{:S(2)}) collective-permute-start(f32[128,768]{1,0:T(8,128)S(1)} %get-tuple-element.18.own_ref), channel_id=1, source_target_pairs={{0,2},{2,4},{4,6},{1,3},{3,5},{5,7},{8,10},{10,12},{12,14},{9,11},... | collective-permute-start | bytes 1179656 | tf_op jit(solution)/shard_map/ppermute | solution.py:370
  20.2 12.8 %collective-permute-start.2 = (f32[128,768]{1,0:T(8,128)S(1)}, f32[128,768]{1,0:T(8,128)S(1)}, u32[]{:S(2)}, u32[]{:S(2)}) collective-permute-start(f32[128,768]{1,0:T(8,128)S(1)} %get-tuple-element.18.own_ref), channel_id=1, source_target_pairs={{2,0},{4,2},{6,4},{3,1},{5,3},{7,5},{10,8},{12,10},{14,12},{11,9},... | collective-permute-start | bytes 1179656 | tf_op jit(solution)/shard_map/ppermute | solution.py:371
  27.8 13.5 %collective-permute-start.5 = (f32[16,8,256]{2,1,0:T(8,128)S(1)}, f32[16,8,256]{2,1,0:T(8,128)S(1)}, u32[]{:S(2)}, u32[]{:S(2)}) collective-permute-start(f32[16,8,256]{2,1,0:T(8,128)S(1)} %shard_map.98.refs_0_), channel_id=1, source_target_pairs={{0,8},{8,16},{16,24},{24,0},{1,9},{9,17},{17,25},{25,1},{2,10},{10... | collective-permute-start | bytes 393224 | tf_op jit(solution)/shard_map/ppermute | solution.py:316
  29.3 12.0 %collective-permute-start.6 = (f32[16,8,256]{2,1,0:T(8,128)S(1)}, f32[16,8,256]{2,1,0:T(8,128)S(1)}, u32[]{:S(2)}, u32[]{:S(2)}) collective-permute-start(f32[16,8,256]{2,1,0:T(8,128)S(1)} %shard_map.98.refs_0_), channel_id=1, source_target_pairs={{0,16},{8,24},{16,0},{24,8},{1,17},{9,25},{17,1},{25,9},{2,18},{10... | collective-permute-start | bytes 393224 | tf_op jit(solution)/shard_map/ppermute | solution.py:316
  30.8 10.5 %collective-permute-start.7 = (f32[16,8,256]{2,1,0:T(8,128)S(1)}, f32[16,8,256]{2,1,0:T(8,128)S(1)}, u32[]{:S(2)}, u32[]{:S(2)}) collective-permute-start(f32[16,8,256]{2,1,0:T(8,128)S(1)} %shard_map.98.refs_0_), channel_id=1, source_target_pairs={{0,24},{8,0},{16,8},{24,16},{1,25},{9,1},{17,9},{25,17},{2,26},{10... | collective-permute-start | bytes 393224 | tf_op jit(solution)/shard_map/ppermute | solution.py:316
  34.0 3.7 %collective-permute-start.3 = (f32[8,128]{1,0:T(8,128)S(1)}, f32[8,128]{1,0:T(8,128)S(1)}, u32[]{:S(2)}, u32[]{:S(2)}) collective-permute-start(f32[8,128]{1,0:T(8,128)S(1)} %get-tuple-element.19), channel_id=1, source_target_pairs={{0,8},{8,0},{16,24},{24,16},{1,9},{9,1},{17,25},{25,17},{2,10},{10... | collective-permute-start | bytes 12296 | tf_op jit(solution)/shard_map/ppermute | solution.py:308
  37.7 3.6 %collective-permute-start.4 = (f32[8,128]{1,0:T(8,128)S(1)}, f32[8,128]{1,0:T(8,128)S(1)}, u32[]{:S(2)}, u32[]{:S(2)}) collective-permute-start(f32[8,128]{1,0:T(8,128)S(1)} %add.21), channel_id=1, source_target_pairs={{0,16},{8,24},{16,0},{24,8},{1,17},{9,25},{17,1},{25,9},{2,18},{10... | collective-permute-start | bytes 12296 | tf_op jit(solution)/shard_map/ppermute | solution.py:308
  47.9 11.7 %collective-permute-start.11 = (f32[128,512]{1,0:T(8,128)S(1)}, f32[128,512]{1,0:T(8,128)S(1)}, u32[]{:S(2)}, u32[]{:S(2)}) collective-permute-start(f32[128,512]{1,0:T(8,128)S(1)} %get-tuple-element.28), channel_id=1, source_target_pairs={{0,1},{1,0},{2,3},{3,2},{4,5},{5,4},{6,7},{7,6},{8,9},{9,8},{10,11... | collective-permute-start | bytes 786440 | tf_op jit(solution)/shard_map/ppermute | solution.py:413
  48.0 1.5 %collective-permute-start.8 = (f32[8,128]{1,0:T(8,128)S(1)}, f32[8,128]{1,0:T(8,128)S(1)}, u32[]{:S(2)}, u32[]{:S(2)}) collective-permute-start(f32[8,128]{1,0:T(8,128)S(1)} %get-tuple-element.24), channel_id=1, source_target_pairs={{0,1},{1,0},{2,3},{3,2},{4,5},{5,4},{6,7},{7,6},{8,9},{9,8},{10,11... | collective-permute-start | bytes 12296 | tf_op jit(solution)/shard_map/ppermute | solution.py:308
  49.5 3.6 %collective-permute-start.9 = (f32[8,128]{1,0:T(8,128)S(1)}, f32[8,128]{1,0:T(8,128)S(1)}, u32[]{:S(2)}, u32[]{:S(2)}) collective-permute-start(f32[8,128]{1,0:T(8,128)S(1)} %add.23), channel_id=1, source_target_pairs={{0,2},{2,0},{4,6},{6,4},{1,3},{3,1},{5,7},{7,5},{8,10},{10,8},{12,... | collective-permute-start | bytes 12296 | tf_op jit(solution)/shard_map/ppermute | solution.py:308
  53.2 4.6 %collective-permute-start.10 = (f32[8,128]{1,0:T(8,128)S(1)}, f32[8,128]{1,0:T(8,128)S(1)}, u32[]{:S(2)}, u32[]{:S(2)}) collective-permute-start(f32[8,128]{1,0:T(8,128)S(1)} %add.24), channel_id=1, source_target_pairs={{0,4},{2,6},{4,0},{6,2},{1,5},{3,7},{5,1},{7,3},{8,12},{10,14},{12... | collective-permute-start | bytes 12296 | tf_op jit(solution)/shard_map/ppermute | solution.py:308

commit v2 on v1

v2 whole, which is shorter than its diff:
```python
import functools
import math

import jax
import jax.numpy as jnp
import ml_dtypes
import numpy as np
from jax import lax
from jax.experimental import pallas as pl
from jax.experimental.pallas import tpu as pltpu
from jax.sharding import PartitionSpec as P

reg_strength = 0.5
damping = 1.0
f32 = jnp.float32
bf16 = jnp.bfloat16
VMEM = pl.BlockSpec(memory_space=pltpu.VMEM)
SMEM = pl.BlockSpec(memory_space=pltpu.SMEM)
HBM = pl.BlockSpec(memory_space=pltpu.HBM)
TN = (((0,), (0,)), ((), ()))
NT = (((1,), (1,)), ((), ()))
large_vmem = 20 * 1024 * 1024
small_vmem = 8 * 1024 * 1024


def dft_table(length):
    index = np.arange(length)
    angle = (index[:, None] * index[None, :] % length) * (2.0 * np.pi / length)
    parts = []
    for part in (np.cos(angle) / math.sqrt(length), -np.sin(angle) / math.sqrt(length)):
        high = part.astype(ml_dtypes.bfloat16)
        low = (part - high.astype(np.float64)).astype(ml_dtypes.bfloat16)
        parts += [high, low]
    return np.concatenate(parts, axis=0)


def split(values):
    high = values.astype(bf16)
    return high, (values - high.astype(f32)).astype(bf16)


def matmul(left, right):
    return jnp.dot(left, right, preferred_element_type=f32)


def quarter_turn(cycle, block):
    turn = lax.rem(cycle * block, 4)
    one, zero = jnp.float32(1.0), jnp.float32(0.0)
    cosine = jnp.where(turn == 0, one, zero) - jnp.where(turn == 2, one, zero)
    sine = jnp.where(turn == 1, one, zero) - jnp.where(turn == 3, one, zero)
    return cosine, sine


def spread(values, row_weight, whigh, wlow, xhigh, xlow, k, coils, ty):
    weighted = values[:, None, :] * row_weight[None, :, :]
    parts = split(weighted.reshape(coils * ty, values.shape[1]))
    sb = values.shape[1] // 2
    vhigh, vlow = (
        jnp.concatenate([part, jnp.concatenate([part[:, sb:], -part[:, :sb]], axis=1)], axis=0) for part in parts
    )
    rows = matmul(
        jnp.concatenate([vhigh, vlow, vhigh], axis=1),
        jnp.concatenate([whigh, whigh, wlow], axis=0),
    )
    high, low = split(rows)
    there, nx = slice(k * ty, (k + 1) * ty), rows.shape[1]
    for part in range(2):
        for c in range(coils):
            here = slice((part * coils + c) * ty, (part * coils + c + 1) * ty)
            xhigh[c, there, part * nx : (part + 1) * nx] = high[here]
            xlow[c, there, part * nx : (part + 1) * nx] = low[here]


def mirror(rows):
    left = lax.broadcasted_iota(jnp.int32, (rows, rows), 0)
    right = lax.broadcasted_iota(jnp.int32, (rows, rows), 1)
    return (lax.rem(left + right, rows) == 0).astype(f32).astype(bf16)


def mirrored(values):
    high, rest = split(values)
    low = (values - high.astype(f32) - rest.astype(f32)).astype(bf16)
    order = mirror(values.shape[0])
    return matmul(order, high) + (matmul(order, rest) + matmul(order, low))


def first_row(rows, columns):
    return lax.broadcasted_iota(jnp.int32, (rows, columns), 0) == 0


def back_rows(adj, xhigh, xlow, coil, first, last):
    ny, nx = adj.shape[0], xhigh.shape[2] // 2
    half = ny // 2
    edge = first_row(half, nx)
    sums = [None] * 4
    for c in range(first, last):
        high, low = xhigh[c], xlow[c]
        folded = matmul(adj[...], jnp.concatenate([high, high, low], axis=0))
        even_real, even_imag = folded[:half, :nx], folded[:half, nx:]
        odd_real, odd_imag = folded[half:, :nx], folded[half:, nx:]
        lower = even_real - jnp.where(edge, 0.0, odd_imag), even_imag + jnp.where(edge, 0.0, odd_real)
        upper = jnp.where(edge, odd_real, even_real + odd_imag), jnp.where(edge, odd_imag, even_imag - odd_real)
        for i, (real, imag) in enumerate((lower, upper)):
            here = slice(i * half, (i + 1) * half)
            coil_real = coil[c, here, :nx].astype(f32)
            coil_imag = coil[c, here, nx:].astype(f32)
            terms = coil_real * real + coil_imag * imag, coil_real * imag - coil_imag * real
            for j, term in enumerate(terms):
                sums[2 * i + j] = term if c == first else sums[2 * i + j] + term
    return jnp.concatenate(sums[:2], axis=1), jnp.concatenate(sums[2:], axis=1)


def rhs_kernel(
    coils, blocks, place_ref, tile_ref, cycle_ref, table_ref, cols_ref, rows_ref, data_ref, weight_ref, coil_any,
    part_ref, whigh, wlow, fwd, adj, row_weight_ref, coil, kept_ref, xhigh, xlow, upper, sems,
):
    ny = table_ref.shape[1]
    half = ny // 2
    ty, tx = rows_ref.shape[0], cols_ref.shape[0]
    sb = rows_ref.shape[1] // blocks
    fetches = [
        pltpu.make_async_copy(coil_any.at[:, half:, :], upper, sems.at[0]),
        pltpu.make_async_copy(coil_any.at[:, :half, :], coil.at[:, :half, :], sems.at[1]),
    ]
    for fetch in fetches:
        fetch.start()

    first = lax.broadcasted_iota(jnp.int32, (ty, half), 1) == 0
    for k in range(blocks):
        top = pl.multiple_of((tile_ref[k] // (ny // tx)) * ty, ty)
        here = slice(k * ty, (k + 1) * ty)
        for i in range(2):
            real = table_ref[pl.ds(i * ny + top, ty), :].astype(f32)
            imag = table_ref[pl.ds((2 + i) * ny + top, ty), :].astype(f32)
            odd = jnp.where(first, real[:, half:], -imag[:, :half])
            row = jnp.concatenate([real[:, :half], odd], axis=1).astype(bf16)
            for place in (0, 2) if i == 0 else (1,):
                fwd[here, place * ny : (place + 1) * ny] = row
    wide = blocks * ty
    for i in range(2):
        turned = fwd[:, i * ny : (i + 1) * ny].astype(f32).T.astype(bf16)
        for place in (0, 2) if i == 0 else (1,):
            adj[:, place * wide : (place + 1) * wide] = turned

    for k in range(blocks):
        left = pl.multiple_of(lax.rem(tile_ref[k], ny // tx) * tx, tx)
        chosen = [table_ref[pl.ds(i * ny + left, tx), :] for i in (0, 1, 2, 3)]
        stacked = jnp.concatenate(
            [jnp.concatenate([chosen[0], chosen[2]], axis=1), jnp.concatenate([chosen[1], chosen[3]], axis=1)], axis=0
        )
        here = slice(k * sb, (k + 1) * sb)
        cols = cols_ref[:, here]
        mixed = lax.dot_general(
            jnp.concatenate([cols, cols], axis=0), stacked, TN, preferred_element_type=f32
        )
        for ref, part in zip((whigh, wlow), split(mixed)):
            ref[k, :sb, :] = part[:, :ny]
            ref[k, sb:, :] = part[:, ny:]
        turned = rows_ref[:, here].astype(f32)
        row_weight = jnp.concatenate([turned, turned], axis=1)
        row_weight_ref[k] = row_weight
        cosine, sine = quarter_turn(cycle_ref[0], k)
        real, imag = data_ref[:, 0, here], data_ref[:, 1, here]
        values = jnp.concatenate([cosine * real + sine * imag, cosine * imag - sine * real], axis=1)
        spread(values, row_weight, whigh[k], wlow[k], xhigh, xlow, k, coils, ty)

    for fetch in fetches:
        fetch.wait()
    order = mirror(half)
    for c in range(coils):
        coil[c, half:, :] = matmul(order, upper[c]).astype(bf16)
    lower_rows, upper_rows = back_rows(adj, xhigh, xlow, coil, 0, coils)
    part_ref[:half, :] = lower_rows
    part_ref[half:ny, :] = upper_rows
    kept_ref[...] = weight_ref[...]
    count = weight_ref.shape[0]
    edge = jnp.concatenate([weight_ref[0:1, :], weight_ref[count - 1 : count, :]], axis=0)
    edge = jnp.concatenate([edge, jnp.zeros((6, edge.shape[1]), f32)], axis=0)
    part_ref[ny:, :] = jnp.concatenate([edge, jnp.zeros_like(edge)], axis=1)


def sum_kernel(ny, place_ref, *refs):
    parts, (folded_ref, image_ref, mine_ref) = refs[:-3], refs[-3:]
    total = parts[0][:ny, :]
    for part in parts[1:]:
        total = total + part[:ny, :]
    folded_ref[...] = total
    image_ref[: ny // 2, :] = total[: ny // 2]
    image_ref[ny // 2 :, :] = mirrored(total[ny // 2 :])
    count = mine_ref.shape[0]
    mine_ref[...] = image_ref[pl.ds(pl.multiple_of(place_ref[0] * count, count), count), :]


def predict_kernel(
    coils, blocks, cycle_ref, row_weight_ref, image_ref, fwd, coil, whigh, wlow, out_ref, thigh, tlow
):
    ny, nx = image_ref.shape[0], image_ref.shape[1] // 2
    half = ny // 2
    ty = row_weight_ref.shape[1]
    sb = row_weight_ref.shape[2] // 2
    edge = first_row(half, nx)
    for c in range(coils):
        products = []
        for i in range(2):
            here = slice(i * half, (i + 1) * half)
            coil_real = coil[c, here, :nx].astype(f32)
            coil_imag = coil[c, here, nx:].astype(f32)
            image_real, image_imag = image_ref[here, :nx], image_ref[here, nx:]
            products.append(coil_real * image_real - coil_imag * image_imag)
            products.append(coil_real * image_imag + coil_imag * image_real)
        lower_real, lower_imag, upper_real, upper_imag = products
        even = [
            lower_real + jnp.where(edge, 0.0, upper_real),
            lower_imag + jnp.where(edge, 0.0, upper_imag),
        ]
        odd = [
            jnp.where(edge, upper_real, lower_imag - upper_imag),
            jnp.where(edge, upper_imag, upper_real - lower_real),
        ]
        folded = jnp.concatenate([jnp.concatenate(even, axis=1), jnp.concatenate(odd, axis=1)], axis=0)
        high, low = split(folded)
        grid = matmul(fwd[...], jnp.concatenate([high, high, low], axis=0))
        for ref, part in zip((thigh, tlow), split(grid)):
            ref[:, 0, c * ty : (c + 1) * ty, :] = part[:, :nx].reshape(blocks, ty, nx)
            ref[:, 1, c * ty : (c + 1) * ty, :] = part[:, nx:].reshape(blocks, ty, nx)
    for k in range(blocks):
        left_high, left_low = (ref[k].reshape(2 * coils * ty, nx) for ref in (thigh, tlow))
        right_high = whigh[k]
        mixed = lax.dot_general(
            jnp.concatenate([left_high, left_low, left_high], axis=1),
            jnp.concatenate([right_high, right_high, wlow[k]], axis=1),
            NT,
            preferred_element_type=f32,
        )
        of_real, of_imag = mixed[: coils * ty], mixed[coils * ty :]
        product = jnp.concatenate(
            [of_real[:, :sb] - of_imag[:, sb:], of_real[:, sb:] + of_imag[:, :sb]], axis=1
        )
        summed = jnp.sum(product.reshape(coils, ty, 2 * sb) * row_weight_ref[k][None, :, :], axis=1)
        real, imag = summed[:, :sb], summed[:, sb:]
        cosine, sine = quarter_turn(cycle_ref[0], k)
        out_ref[k] = jnp.concatenate([cosine * real - sine * imag, sine * real + cosine * imag], axis=1)


def spread_kernel(coils, blocks, cycle_ref, row_weight_ref, whigh, wlow, *refs):
    parts, (xhigh, xlow, sums_ref) = refs[:-3], refs[-3:]
    ty = row_weight_ref.shape[1]
    sb = row_weight_ref.shape[2] // 2
    squares = 0.0
    for k in range(blocks):
        total = parts[0][k]
        for part in parts[1:]:
            total = total + part[k]
        squares += total * total
        cosine, sine = quarter_turn(cycle_ref[0], k)
        real, imag = total[:, :sb], total[:, sb:]
        values = jnp.concatenate([cosine * real + sine * imag, cosine * imag - sine * real], axis=1)
        spread(values, row_weight_ref[k], whigh[k], wlow[k], xhigh, xlow, k, coils, ty)
    lane = lax.broadcasted_iota(jnp.int32, sums_ref.shape, 1)
    sums_ref[...] = jnp.where(lane == 1, jnp.sum(squares), 0.0)


def rows_kernel(first, last, adj, coil, xhigh, xlow, *refs):
    out_ref = refs[-1]
    half = out_ref.shape[0] // 2
    for i, rows in enumerate(back_rows(adj, xhigh, xlow, coil, first, last)):
        here = slice(i * half, (i + 1) * half)
        out_ref[here, :] = rows + refs[0][here, :] if first else rows


def cut_kernel(place_ref, after_ref, folded_ref, *refs):
    *out_refs, whole = refs
    total = whole.shape[0]
    half = total // 2
    whole[:half, :] = folded_ref[:half, :]
    whole[half:, :] = mirrored(folded_ref[half:, :])
    for shift, out_ref in enumerate(out_refs):
        count = out_ref.shape[0]
        start = lax.rem(place_ref[0] + shift, total // count) * count
        out_ref[...] = whole[pl.ds(pl.multiple_of(start, count), count), :]


def neighbours(place_ref, image_ref, weight, before_ref, after_ref):
    count, nx = weight.shape
    total = image_ref.shape[0]
    place = place_ref[0]
    start = place * count
    weight_up = jnp.where(place > 0, before_ref[total + 1 : total + 2, :nx], 0.0)
    weight_down = jnp.where(place < total // count - 1, after_ref[total : total + 1, :nx], 0.0)
    image_up = image_ref[pl.ds(jnp.maximum(start - 1, 0), 1), :]
    image_down = image_ref[pl.ds(jnp.minimum(start + count, total - 1), 1), :]
    row = lax.broadcasted_iota(jnp.int32, (count, nx), 0)
    column = lax.broadcasted_iota(jnp.int32, (count, nx), 1)

    def above(values, edge):
        return jnp.where(row == 0, edge, pltpu.roll(values, 1, 0))

    def below(values, edge):
        return jnp.where(row == count - 1, edge, pltpu.roll(values, count - 1, 0))

    return weight_up, weight_down, image_up, image_down, column, above, below


def smooth_kernel(
    place_ref, image_ref, own_ref, even_ref, odd_ref, weight_ref, weight_even_ref, weight_odd_ref,
    before_ref, after_ref, out_ref, sums_ref,
):
    nx = image_ref.shape[1] // 2
    weight, weight_even, weight_odd = weight_ref[...], weight_even_ref[...], weight_odd_ref[...]
    weight_up, weight_down, image_up, image_down, column, above, below = neighbours(
        place_ref, image_ref, weight, before_ref, after_ref
    )
    weight_left = jnp.where(column == 0, 0.0, pltpu.roll(weight, 1, 1))
    weight_right = jnp.where(column == nx - 1, 0.0, pltpu.roll(weight, nx - 1, 1))
    weight_above, weight_below = above(weight, weight_up), below(weight, weight_down)
    squares = curvature = 0.0
    for part in range(2):
        lanes = slice(part * nx, (part + 1) * nx)
        here = own_ref[:, lanes]
        flux = weight_even * (here - even_ref[:, lanes]) + weight_odd * (here - odd_ref[:, lanes])
        flux += weight_above * (here - above(here, image_up[:, lanes]))
        flux += weight_below * (here - below(here, image_down[:, lanes]))
        flux += weight_left * (here - pltpu.roll(here, 1, 1))
        flux += weight_right * (here - pltpu.roll(here, nx - 1, 1))
        result = reg_strength * (weight * flux) + damping * here
        out_ref[:, lanes] = result
        squares += here * here
        curvature += here * result
    norm, energy = jnp.sum(squares), jnp.sum(curvature)
    lane = lax.broadcasted_iota(jnp.int32, sums_ref.shape, 1)
    sums_ref[...] = jnp.where(lane == 0, norm, jnp.where(lane == 1, energy, 0.0))


def update_kernel(images, own_ref, smooth_ref, *refs):
    image_refs, sums_refs, (field_ref, residual_ref) = refs[:images], refs[images:-2], refs[-2:]
    sums = sums_refs[0][0:1, :]
    for ref in sums_refs[1:]:
        sums = sums + ref[0:1, :]
    alpha = sums[:, 0:1] / sums[:, 1:2]
    here = own_ref[...]
    image = smooth_ref[...]
    for ref in image_refs:
        image = image + ref[...]
    field_ref[...] = alpha * here
    residual_ref[...] = here - alpha * image


def call(kernel, outs, specs, out_specs, scratch=(), flops=0, nbytes=0, limit=small_vmem):
    return pl.pallas_call(
        kernel,
        out_shape=outs,
        in_specs=specs,
        out_specs=out_specs,
        scratch_shapes=scratch,
        compiler_params=pltpu.CompilerParams(vmem_limit_bytes=limit),
        cost_estimate=pl.CostEstimate(flops=flops, bytes_accessed=nbytes, transcendentals=0),
    )


def shape(dims, dtype=f32):
    return jax.ShapeDtypeStruct(dims, dtype)


def exchange(values, axis, step):
    return lax.ppermute(values, axis, [(i, i ^ step) for i in range(lax.axis_size(axis))])


def powers(axis):
    return [1 << i for i in range(lax.axis_size(axis).bit_length() - 1)]


def from_others(values, axis):
    count = lax.axis_size(axis)
    return [
        lax.ppermute(values, axis, [(i, (i + shift) % count) for i in range(count)]) for shift in range(1, count)
    ]


def on_device(kspace_data, coil_maps, smooth_weight, kernel_cols, kernel_rows, tile_index, caipi_cycle):
    profiles, data, weight = coil_maps[0, 0], kspace_data[0], smooth_weight[0, 0]
    coils, ny, width = profiles.shape
    nx = width // 2
    blocks = tile_index.shape[0]
    samples, ty = kernel_rows.shape
    sb = samples // blocks
    count = weight.shape[0]
    rows, groups = lax.axis_size("row"), lax.axis_size("grp")
    row_place = lax.axis_index("row")
    table = jnp.asarray(dft_table(ny))
    wide = blocks * ty
    w_shape = (blocks, 2 * sb, nx)
    row_flops = 2 * 3 * coils * wide * ny * width
    col_flops = 2 * 3 * coils * ty * blocks * (2 * sb) * width
    place = jnp.stack([row_place, jnp.int32(rows)])
    dma = pltpu.SemaphoreType.DMA
    x_shape = pltpu.VMEM((coils, wide, width), bf16)

    data, weight, profiles, cols, rows_of, tile_index, table = (
        pltpu.with_memory_space_constraint(x, pltpu.HBM)
        for x in (data, weight, profiles, kernel_cols.T, kernel_rows.T, tile_index, table)
    )
    partial, *kept = call(
        functools.partial(rhs_kernel, coils, blocks),
        [
            shape((ny + 8, width)),
            pltpu.VMEM(w_shape, bf16),
            pltpu.VMEM(w_shape, bf16),
            pltpu.VMEM((wide, 3 * ny), bf16),
            pltpu.VMEM((ny, 3 * wide), bf16),
            pltpu.VMEM((blocks, ty, 2 * sb), f32),
            pltpu.VMEM(profiles.shape, bf16),
            pltpu.VMEM(weight.shape, f32),
        ],
        [SMEM, SMEM, SMEM, VMEM, VMEM, VMEM, VMEM, VMEM, HBM],
        [VMEM] * 8,
        [x_shape, x_shape, pltpu.VMEM((coils, ny // 2, width), bf16), dma((2,))],
        row_flops + 2 * col_flops,
        limit=large_vmem,
    )(place, tile_index, caipi_cycle, table, cols, rows_of, data, weight, profiles)
    whigh, wlow, fwd, adj, row_weight, coil, weight = (
        pltpu.with_memory_space_constraint(x, pltpu.VMEM) for x in kept
    )

    received = from_others(partial, "row")
    even_pairs = [(i, i ^ 1) for i in range(groups) if i ^ 1 < groups]
    odd_pairs = []
    for i in range(1, groups - 1, 2):
        odd_pairs += [(i, i + 1), (i + 1, i)]
    weights = [lax.ppermute(weight, "grp", pairs) for pairs in (even_pairs, odd_pairs)]
    folded, image, mine = call(
        functools.partial(sum_kernel, ny),
        [shape((ny, width)), shape((ny, width)), shape((count, width))],
        [SMEM] + [VMEM] * (1 + len(received)),
        [VMEM] * 3,
    )(place, partial, *received)
    others = [lax.ppermute(mine, "grp", pairs) for pairs in (even_pairs, odd_pairs)]

    predicted = call(
        functools.partial(predict_kernel, coils, blocks),
        shape((blocks, coils, 2 * sb)),
        [SMEM] + [VMEM] * 6,
        VMEM,
        [pltpu.VMEM((blocks, 2, coils * ty, nx), bf16)] * 2,
        row_flops + col_flops,
        limit=large_vmem,
    )(caipi_cycle, row_weight, folded, fwd, coil, whigh, wlow)

    predicted = [predicted, *from_others(predicted, "band")]
    smoothed, sums = call(
        smooth_kernel,
        [shape((count, width)), shape((8, 128))],
        [SMEM] + [VMEM] * 9,
        [VMEM, VMEM],
    )(place, image, mine, *others, weight, *weights, received[0], received[-1])
    for step in powers("band"):
        sums = sums + exchange(sums, "band", step)

    *kept, squares = call(
        functools.partial(spread_kernel, coils, blocks),
        [x_shape, x_shape, shape((8, 128))],
        [SMEM] + [VMEM] * (3 + len(predicted)),
        [VMEM] * 3,
        (),
        col_flops,
        limit=large_vmem,
    )(caipi_cycle, row_weight, whigh, wlow, *predicted)
    xhigh, xlow = (pltpu.with_memory_space_constraint(x, pltpu.VMEM) for x in kept)
    sums = sums + squares

    steps = powers("grp")
    for step in steps[:-1]:
        sums = sums + exchange(sums, "grp", step)
    middle = coils // 2

    def add_rows(first, last, *before):
        return call(
            functools.partial(rows_kernel, first, last),
            shape((ny, width)),
            [VMEM] * (4 + len(before)),
            VMEM,
            (),
            row_flops // 2,
            limit=large_vmem,
        )(adj, coil, xhigh, xlow, *before)

    unfinished = add_rows(middle, coils, add_rows(0, middle), sums)
    sums = sums + exchange(sums, "grp", steps[-1])
    halves = call(
        cut_kernel,
        [shape((count, width))] * 2 if rows == 2 else [shape((ny, width))],
        [SMEM] + [VMEM] * 2,
        [VMEM] * (2 if rows == 2 else 1),
        [pltpu.VMEM((ny, width), f32)],
    )(place, sums, unfinished)
    if rows == 2:
        images = [halves[0], exchange(halves[1], "row", 1)]
    else:
        images = [lax.psum_scatter(halves[0], "row", scatter_dimension=0, tiled=True)]
    all_sums = [sums, *from_others(sums, "row")]
    solution_field, residual = call(
        functools.partial(update_kernel, len(images)),
        [shape((count, width))] * 2,
        [VMEM] * (2 + len(images) + len(all_sums)),
        [VMEM, VMEM],
    )(mine, smoothed, *images, *all_sums)
    return solution_field[None, None], residual[None, None]


def solution(mesh):
    return jax.shard_map(
        on_device,
        mesh=mesh,
        in_specs=(
            P("grp", "row", None, None),
            P("band", "grp", "row", None, None),
            P("band", "grp", "row", None),
            P(),
            P(),
            P(),
            P("band"),
        ),
        out_specs=(P("band", "grp", "row", None), P("band", "grp", "row", None)),
        check_vma=False,
    )
```

time: 60.8 us -> 49.2 us (0.81)
  waiting for transfers between devices: 10.7 us -> 6.92 us
  Pallas kernels: 24.7 us -> 21.5 us
  local copies, waits for them, and re-layouts: 1.63 us -> 0 us
  between operations: 2.72 us -> 1.39 us
  other arithmetic: 0.97 us -> 0.09 us
    ppermute x8 -> x9, waiting for transfers between devices: 9.12 us -> 5.88 us  [the longest x5 5.87 us: exchange(): lax.ppermute(values, axis, [(i, i ^ step) for i in range(lax.axis_size(ax...]
    pallas_call x1, Pallas kernels: 6.29 us -> 4.38 us  [on_device(): call(functools.partial(predict_kernel, coils, blocks), shape((blocks, coi...]
    ppermute x8 -> x9, starting transfers between devices: 14.8 us -> 13.6 us  [the longest x5 5.21 us: exchange(): lax.ppermute(values, axis, [(i, i ^ step) for i in range(lax.axis_size(ax...]
    unnamed x2 -> x0, local copies, waits for them, and re-layouts: 1.04 us -> none
    broadcast_in_dim x1 -> x0, other arithmetic: 0.88 us -> none  [on_device(): return (solution_field[None, None], residual[None, None])]
    pallas_call x1, Pallas kernels: 9.81 us -> 9.01 us  [on_device(): call(functools.partial(rhs_kernel, coils, blocks), [shape((ny + 8, width)...]
    ppermute x4 -> x5, waiting for transfers between devices: 1.57 us -> 1.04 us  [from_others(): lax.ppermute(values, axis, [(i, (i + shift) % count) for i in range(count)])]
    pallas_call x3 -> x6, Pallas kernels: 7.58 us -> 7.06 us  [the longest x2 2.48 us: add_rows(): call(functools.partial(rows_kernel, first, last), shape((ny, width)), [VM...]
  transfers between devices with their start and end apart: 12 -> 14, of which waited for: 7 -> 5; matrix products, arithmetic and copies ran while one was open for 1% -> 0% of each run, Pallas kernels for 12% -> 22%
where the time goes in v2:
time: 49.2 us; the launch traced here: 49.1 us
  Pallas kernels  21.5 us (44%)
  starting transfers between devices  19.2 us (39%)
  waiting for transfers between devices  6.92 us (14%)
  between operations  1.39 us (3%)
    pallas_call x1, Pallas kernels, on_device(): call(functools.partial(rhs_kernel, coils, blocks), [shape((ny + 8, width)...  9.01 us
    ppermute x5, waiting for transfers between devices, exchange(): lax.ppermute(values, axis, [(i, i ^ step) for i in range(lax.axis_size(ax...  5.87 us
    ppermute x5, starting transfers between devices, from_others(): lax.ppermute(values, axis, [(i, (i + shift) % count) for i in range(count)])  5.51 us
    ppermute x5, starting transfers between devices, exchange(): lax.ppermute(values, axis, [(i, i ^ step) for i in range(lax.axis_size(ax...  5.21 us
    ppermute x2, starting transfers between devices, on_device(): lax.ppermute(mine, 'grp', pairs)  5.13 us
    pallas_call x1, Pallas kernels, on_device(): call(functools.partial(predict_kernel, coils, blocks), shape((blocks, coi...  4.38 us
    ppermute x2, starting transfers between devices, on_device(): lax.ppermute(weight, 'grp', pairs)  3.3 us
    pallas_call x2, Pallas kernels, add_rows(): call(functools.partial(rows_kernel, first, last), shape((ny, width)), [VM...  2.48 us
  transfers between devices with their start and end apart: 14, of which 5 were waited for; matrix products, arithmetic and copies ran while one was open for 0% of the time, Pallas kernels for 22%

profile of v2, /device:TPU:0, one launch (start us, length us, event | category | flops | bytes accessed | tf_op | source)
XLA Modules:
  0.0 49.1 jit_solution(610956688469991028)
XLA Ops:
  1.3 0.1 pad_add_fusion.place_ref
  1.4 9.0 %shard_map.95 = (f32[264,512]{1,0:T(8,128)S(1)}, bf16[16,256,256]{2,1,0:T(8,128)(2,1)S(1)}, bf16[16,256,256]{2,1,0:T(8,128)(2,1)S(1)}, bf16[256,768]{1,0:T(8,128...) custom-call(s32[2]{0:T(128)S(1)} %pad_add_fusion.place_ref, ...), custom_call_target="tpu_custom_call" | custom-call | flops 4831838208 | tf_op jit(solution)/shard_map/pallas_call | solution.py:402
  10.4 0.5 %collective-permute-start = (f32[264,512]{1,0:T(8,128)S(1)}, f32[264,512]{1,0:T(8,128)S(1)}, u32[]{:S(2)}, u32[]{:S(2)}) collective-permute-start(f32[264,512]{1,0:T(8,128)S(1)} %get-tuple-element.22.refs_0_), channel_id=1, source_target_pairs={{0,1},{1,0},{2,3},{3,2},{4,5},{5,4},{6,7},{7,6},{8,9},{9,8},{10,11... | collective-permute-start | bytes 1622024 | tf_op jit(solution)/shard_map/ppermute | solution.py:375
  10.9 2.6 %collective-permute-start.3 = (f32[128,256]{1,0:T(8,128)S(1)}, f32[128,256]{1,0:T(8,128)S(1)}, u32[]{:S(2)}, u32[]{:S(2)}) collective-permute-start(f32[128,256]{1,0:T(8,128)S(1)} %get-tuple-element.25.weight_ref), channel_id=1, source_target_pairs={{0,2},{2,0},{4,6},{6,4},{1,3},{3,1},{5,7},{7,5},{8,10},{10,8},{12,... | collective-permute-start | bytes 393224 | tf_op jit(solution)/shard_map/ppermute | solution.py:429
  13.5 0.7 %collective-permute-start.4 = (f32[128,256]{1,0:T(8,128)S(1)}, f32[128,256]{1,0:T(8,128)S(1)}, u32[]{:S(2)}, u32[]{:S(2)}) collective-permute-start(f32[128,256]{1,0:T(8,128)S(1)} %get-tuple-element.25.weight_ref), channel_id=1, source_target_pairs={{2,4},{4,2},{3,5},{5,3},{10,12},{12,10},{11,13},{13,11},{18,20},{2... | collective-permute-start | bytes 393224 | tf_op jit(solution)/shard_map/ppermute | solution.py:429
  14.2 0.0 collective-permute-done.refs_1_.before_ref.after_ref
  14.2 0.9 %shard_map.96 = (f32[256,512]{1,0:T(8,128)S(1)}, f32[256,512]{1,0:T(8,128)S(1)}, f32[128,512]{1,0:T(8,128)S(1)}) custom-call(s32[2]{0:T(128)S(1)} %pad_add_fusion.place_ref, f32[264,512]{1,0:T(8,128)S(1)} %get-tuple-element.22.refs_0_, f32[264,512]{1,0:T(8,128)S(1)} %collective-permute-done.refs_1_.before_ref.after_ref), custom_call_target="tpu_custom_call" | custom-call | tf_op jit(solution)/shard_map/pallas_call | solution.py:430
  15.1 4.5 %collective-permute-start.1 = (f32[128,512]{1,0:T(8,128)S(1)}, f32[128,512]{1,0:T(8,128)S(1)}, u32[]{:S(2)}, u32[]{:S(2)}) collective-permute-start(f32[128,512]{1,0:T(8,128)S(1)} %get-tuple-element.23.own_ref), channel_id=1, source_target_pairs={{0,2},{2,0},{4,6},{6,4},{1,3},{3,1},{5,7},{7,5},{8,10},{10,8},{12,... | collective-permute-start | bytes 786440 | tf_op jit(solution)/shard_map/ppermute | solution.py:436
  19.6 0.7 %collective-permute-start.2 = (f32[128,512]{1,0:T(8,128)S(1)}, f32[128,512]{1,0:T(8,128)S(1)}, u32[]{:S(2)}, u32[]{:S(2)}) collective-permute-start(f32[128,512]{1,0:T(8,128)S(1)} %get-tuple-element.23.own_ref), channel_id=1, source_target_pairs={{2,4},{4,2},{3,5},{5,3},{10,12},{12,10},{11,13},{13,11},{18,20},{2... | collective-permute-start | bytes 786440 | tf_op jit(solution)/shard_map/ppermute | solution.py:436
  20.2 4.4 %shard_map.98.refs_0_ = f32[16,8,256]{2,1,0:T(8,128)S(1)} custom-call(s32[1]{0:T(128)S(6)} %copy.10.cycle_ref, f32[16,16,256]{2,1,0:T(8,128)S(1)} %get-tuple-element.28.row_weight_ref, f32[256,512]{1,0:T(8,128)S(1)} %get-tuple-element.31.image_ref, bf16[256,768]{1,0:T(8,128)(2,1)S(1)} %get-tuple-element.32.fwd, ...), custom_call_target="tpu_custom_call" | custom-call | flops 3221225472 | tf_op jit(solution)/shard_map/pallas_call | solution.py:438
  24.6 1.5 %collective-permute-start.7 = (f32[16,8,256]{2,1,0:T(8,128)S(1)}, f32[16,8,256]{2,1,0:T(8,128)S(1)}, u32[]{:S(2)}, u32[]{:S(2)}) collective-permute-start(f32[16,8,256]{2,1,0:T(8,128)S(1)} %shard_map.98.refs_0_), channel_id=1, source_target_pairs={{0,8},{8,16},{16,24},{24,0},{1,9},{9,17},{17,25},{25,1},{2,10},{10... | collective-permute-start | bytes 393224 | tf_op jit(solution)/shard_map/ppermute | solution.py:375
  26.2 0.0 collective-permute-done.3.weight_even_ref
  26.2 1.5 %collective-permute-start.8 = (f32[16,8,256]{2,1,0:T(8,128)S(1)}, f32[16,8,256]{2,1,0:T(8,128)S(1)}, u32[]{:S(2)}, u32[]{:S(2)}) collective-permute-start(f32[16,8,256]{2,1,0:T(8,128)S(1)} %shard_map.98.refs_0_), channel_id=1, source_target_pairs={{0,16},{8,24},{16,0},{24,8},{1,17},{9,25},{17,1},{25,9},{2,18},{10... | collective-permute-start | bytes 393224 | tf_op jit(solution)/shard_map/ppermute | solution.py:375
  27.7 1.4 %collective-permute-start.9 = (f32[16,8,256]{2,1,0:T(8,128)S(1)}, f32[16,8,256]{2,1,0:T(8,128)S(1)}, u32[]{:S(2)}, u32[]{:S(2)}) collective-permute-start(f32[16,8,256]{2,1,0:T(8,128)S(1)} %shard_map.98.refs_0_), channel_id=1, source_target_pairs={{0,24},{8,0},{16,8},{24,16},{1,25},{9,1},{17,9},{25,17},{2,26},{10... | collective-permute-start | bytes 393224 | tf_op jit(solution)/shard_map/ppermute | solution.py:375
  29.1 0.0 collective-permute-done.1.even_ref
  29.1 1.0 %shard_map.97 = (f32[128,512]{1,0:T(8,128)S(1)}, f32[8,128]{1,0:T(8,128)S(1)}) custom-call(s32[2]{0:T(128)S(1)} %pad_add_fusion.place_ref, f32[256,512]{1,0:T(8,128)S(1)} %get-tuple-element.24.image_ref, f32[128,512]{1,0:T(8,128)S(1)} %get-tuple-element.23.own_ref, f32[128,512]{1,0:T(8,128)S(1)} %collective-permute-done.1.even_ref, ...), custom_call_target="tpu_custom_call" | custom-call | tf_op jit(solution)/shard_map/pallas_call | solution.py:449
  30.2 0.7 %collective-permute-start.5 = (f32[8,128]{1,0:T(8,128)S(1)}, f32[8,128]{1,0:T(8,128)S(1)}, u32[]{:S(2)}, u32[]{:S(2)}) collective-permute-start(f32[8,128]{1,0:T(8,128)S(1)} %get-tuple-element.27), channel_id=1, source_target_pairs={{0,8},{8,0},{16,24},{24,16},{1,9},{9,1},{17,25},{25,17},{2,10},{10... | collective-permute-start | bytes 12296 | tf_op jit(solution)/shard_map/ppermute | solution.py:365
  30.9 3.0 %collective-permute-done.5 = f32[8,128]{1,0:T(8,128)S(1)} collective-permute-done((f32[8,128]{1,0:T(8,128)S(1)}, f32[8,128]{1,0:T(8,128)S(1)}, u32[]{:S(2)}, u32[]{:S(2)}) %collective-permute-start.5) | collective-permute-done | bytes 4128 | tf_op jit(solution)/shard_map/ppermute | solution.py:365
  33.9 0.5 %collective-permute-start.6 = (f32[8,128]{1,0:T(8,128)S(1)}, f32[8,128]{1,0:T(8,128)S(1)}, u32[]{:S(2)}, u32[]{:S(2)}) collective-permute-start(f32[8,128]{1,0:T(8,128)S(1)} %add.15), channel_id=1, source_target_pairs={{0,16},{8,24},{16,0},{24,8},{1,17},{9,25},{17,1},{25,9},{2,18},{10... | collective-permute-start | bytes 12296 | tf_op jit(solution)/shard_map/ppermute | solution.py:365
  34.4 1.9 %shard_map.99 = (bf16[8,256,512]{2,1,0:T(8,128)(2,1)S(1)}, bf16[8,256,512]{2,1,0:T(8,128)(2,1)S(1)}, f32[8,128]{1,0:T(8,128)S(1)}) custom-call(s32[1]{0:T(128)S(6)} %copy.10.cycle_ref, f32[16,16,256]{2,1,0:T(8,128)S(1)} %get-tuple-element.28.row_weight_ref, bf16[16,256,256]{2,1,0:T(8,128)(2,1)S(1)} %get-tuple-element.29.whigh, ...), custom_call_target="tpu_custom_call" | custom-call | flops 1610612736 | tf_op jit(solution)/shard_map/pallas_call | solution.py:458
  36.3 1.2 %collective-permute-done.6 = f32[8,128]{1,0:T(8,128)S(1)} collective-permute-done((f32[8,128]{1,0:T(8,128)S(1)}, f32[8,128]{1,0:T(8,128)S(1)}, u32[]{:S(2)}, u32[]{:S(2)}) %collective-permute-start.6) | collective-permute-done | bytes 4128 | tf_op jit(solution)/shard_map/ppermute | solution.py:365
  37.5 1.3 %collective-permute-start.10 = (f32[8,128]{1,0:T(8,128)S(1)}, f32[8,128]{1,0:T(8,128)S(1)}, u32[]{:S(2)}, u32[]{:S(2)}) collective-permute-start(f32[8,128]{1,0:T(8,128)S(1)} %add_add_fusion), channel_id=1, source_target_pairs={{0,2},{2,0},{4,6},{6,4},{1,3},{3,1},{5,7},{7,5},{8,10},{10,8},{12,... | collective-permute-start | bytes 12296 | tf_op jit(solution)/shard_map/ppermute | solution.py:365
  38.8 1.2 %shard_map.100.refs_0_ = f32[256,512]{1,0:T(8,128)S(1)} custom-call(bf16[256,768]{1,0:T(8,128)(2,1)S(1)} %get-tuple-element.35.adj, bf16[8,256,512]{2,1,0:T(8,128)(2,1)S(1)} %get-tuple-element.33.coil, bf16[8,256,512]{2,1,0:T(8,128)(2,1)S(1)} %get-tuple-element.36.xhigh, bf16[8,256,512]{2,1,0:T(8,128)(2,1)S(1)} %get-tuple-element.37.xlow), custom_call_target="tpu_custom_call" | custom-call | flops 805306368 | tf_op jit(solution)/shard_map/pallas_call | solution.py:476
  40.0 1.1 %collective-permute-done.10 = f32[8,128]{1,0:T(8,128)S(1)} collective-permute-done((f32[8,128]{1,0:T(8,128)S(1)}, f32[8,128]{1,0:T(8,128)S(1)}, u32[]{:S(2)}, u32[]{:S(2)}) %collective-permute-start.10) | collective-permute-done | bytes 4128 | tf_op jit(solution)/shard_map/ppermute | solution.py:365
  41.1 2.7 %collective-permute-start.11 = (f32[8,128]{1,0:T(8,128)S(1)}, f32[8,128]{1,0:T(8,128)S(1)}, u32[]{:S(2)}, u32[]{:S(2)}) collective-permute-start(f32[8,128]{1,0:T(8,128)S(1)} %add.18.refs_1_), channel_id=1, source_target_pairs={{0,4},{2,6},{4,0},{6,2},{1,5},{3,7},{5,1},{7,3},{8,12},{10,14},{12... | collective-permute-start | bytes 12296 | tf_op jit(solution)/shard_map/ppermute | solution.py:365
  43.8 1.3 %shard_map.101.folded_ref = f32[256,512]{1,0:T(8,128)S(1)} custom-call(bf16[256,768]{1,0:T(8,128)(2,1)S(1)} %get-tuple-element.35.adj, bf16[8,256,512]{2,1,0:T(8,128)(2,1)S(1)} %get-tuple-element.33.coil, bf16[8,256,512]{2,1,0:T(8,128)(2,1)S(1)} %get-tuple-element.36.xhigh, bf16[8,256,512]{2,1,0:T(8,128)(2,1)S(1)} %get-tuple-element.37.xlow, ...), custom_call_target="tpu_custom_call" | custom-call | flops 805306368 | tf_op jit(solution)/shard_map/pallas_call | solution.py:476
  45.1 0.5 %collective-permute-done.11 = f32[8,128]{1,0:T(8,128)S(1)} collective-permute-done((f32[8,128]{1,0:T(8,128)S(1)}, f32[8,128]{1,0:T(8,128)S(1)}, u32[]{:S(2)}, u32[]{:S(2)}) %collective-permute-start.11) | collective-permute-done | bytes 4128 | tf_op jit(solution)/shard_map/ppermute | solution.py:365
  45.6 0.9 %shard_map.102 = (f32[128,512]{1,0:T(8,128)S(1)}, f32[128,512]{1,0:T(8,128)S(1)}) custom-call(s32[2]{0:T(128)S(1)} %pad_add_fusion.place_ref, f32[8,128]{1,0:T(8,128)S(1)} %add.19.after_ref.refs_2_, f32[256,512]{1,0:T(8,128)S(1)} %shard_map.101.folded_ref), custom_call_target="tpu_custom_call" | custom-call | tf_op jit(solution)/shard_map/pallas_call | solution.py:488
  46.5 0.1 collective-permute-start.12
  46.6 0.5 %collective-permute-start.13 = (f32[8,128]{1,0:T(8,128)S(1)}, f32[8,128]{1,0:T(8,128)S(1)}, u32[]{:S(2)}, u32[]{:S(2)}) collective-permute-start(f32[8,128]{1,0:T(8,128)S(1)} %add.19.after_ref.refs_2_), channel_id=1, source_target_pairs={{0,1},{1,0},{2,3},{3,2},{4,5},{5,4},{6,7},{7,6},{8,9},{9,8},{10,11... | collective-permute-start | bytes 12296 | tf_op jit(solution)/shard_map/ppermute | solution.py:375
  47.1 1.0 %collective-permute-done.13.refs_3_ = f32[8,128]{1,0:T(8,128)S(1)} collective-permute-done((f32[8,128]{1,0:T(8,128)S(1)}, f32[8,128]{1,0:T(8,128)S(1)}, u32[]{:S(2)}, u32[]{:S(2)}) %collective-permute-start.13) | collective-permute-done | bytes 4128 | tf_op jit(solution)/shard_map/ppermute | solution.py:375
  48.1 0.9 %shard_map.103 = (f32[128,512]{1,0:T(8,128)}, f32[128,512]{1,0:T(8,128)}) custom-call(f32[128,512]{1,0:T(8,128)S(1)} %get-tuple-element.23.own_ref, f32[128,512]{1,0:T(8,128)S(1)} %get-tuple-element.26.smooth_ref, f32[128,512]{1,0:T(8,128)S(1)} %get-tuple-element.38.refs_0_, f32[128,512]{1,0:T(8,128)S(1)} %collective-permute-done.12.refs_1_, ...), custom_call_target="tpu_custom_call" | custom-call | tf_op jit(solution)/shard_map/pallas_call | solution.py:500
  (10 shorter events, 0.0 us)
Async XLA Ops:
  10.4 3.8 %collective-permute-start = (f32[264,512]{1,0:T(8,128)S(1)}, f32[264,512]{1,0:T(8,128)S(1)}, u32[]{:S(2)}, u32[]{:S(2)}) collective-permute-start(f32[264,512]{1,0:T(8,128)S(1)} %get-tuple-element.22.refs_0_), channel_id=1, source_target_pairs={{0,1},{1,0},{2,3},{3,2},{4,5},{5,4},{6,7},{7,6},{8,9},{9,8},{10,11... | collective-permute-start | bytes 1622024 | tf_op jit(solution)/shard_map/ppermute | solution.py:375
  10.9 15.3 %collective-permute-start.3 = (f32[128,256]{1,0:T(8,128)S(1)}, f32[128,256]{1,0:T(8,128)S(1)}, u32[]{:S(2)}, u32[]{:S(2)}) collective-permute-start(f32[128,256]{1,0:T(8,128)S(1)} %get-tuple-element.25.weight_ref), channel_id=1, source_target_pairs={{0,2},{2,0},{4,6},{6,4},{1,3},{3,1},{5,7},{7,5},{8,10},{10,8},{12,... | collective-permute-start | bytes 393224 | tf_op jit(solution)/shard_map/ppermute | solution.py:429
  13.5 14.2 %collective-permute-start.4 = (f32[128,256]{1,0:T(8,128)S(1)}, f32[128,256]{1,0:T(8,128)S(1)}, u32[]{:S(2)}, u32[]{:S(2)}) collective-permute-start(f32[128,256]{1,0:T(8,128)S(1)} %get-tuple-element.25.weight_ref), channel_id=1, source_target_pairs={{2,4},{4,2},{3,5},{5,3},{10,12},{12,10},{11,13},{13,11},{18,20},{2... | collective-permute-start | bytes 393224 | tf_op jit(solution)/shard_map/ppermute | solution.py:429
  15.1 14.0 %collective-permute-start.1 = (f32[128,512]{1,0:T(8,128)S(1)}, f32[128,512]{1,0:T(8,128)S(1)}, u32[]{:S(2)}, u32[]{:S(2)}) collective-permute-start(f32[128,512]{1,0:T(8,128)S(1)} %get-tuple-element.23.own_ref), channel_id=1, source_target_pairs={{0,2},{2,0},{4,6},{6,4},{1,3},{3,1},{5,7},{7,5},{8,10},{10,8},{12,... | collective-permute-start | bytes 786440 | tf_op jit(solution)/shard_map/ppermute | solution.py:436
  19.6 9.6 %collective-permute-start.2 = (f32[128,512]{1,0:T(8,128)S(1)}, f32[128,512]{1,0:T(8,128)S(1)}, u32[]{:S(2)}, u32[]{:S(2)}) collective-permute-start(f32[128,512]{1,0:T(8,128)S(1)} %get-tuple-element.23.own_ref), channel_id=1, source_target_pairs={{2,4},{4,2},{3,5},{5,3},{10,12},{12,10},{11,13},{13,11},{18,20},{2... | collective-permute-start | bytes 786440 | tf_op jit(solution)/shard_map/ppermute | solution.py:436
  24.6 9.8 %collective-permute-start.7 = (f32[16,8,256]{2,1,0:T(8,128)S(1)}, f32[16,8,256]{2,1,0:T(8,128)S(1)}, u32[]{:S(2)}, u32[]{:S(2)}) collective-permute-start(f32[16,8,256]{2,1,0:T(8,128)S(1)} %shard_map.98.refs_0_), channel_id=1, source_target_pairs={{0,8},{8,16},{16,24},{24,0},{1,9},{9,17},{17,25},{25,1},{2,10},{10... | collective-permute-start | bytes 393224 | tf_op jit(solution)/shard_map/ppermute | solution.py:375
  26.2 8.2 %collective-permute-start.8 = (f32[16,8,256]{2,1,0:T(8,128)S(1)}, f32[16,8,256]{2,1,0:T(8,128)S(1)}, u32[]{:S(2)}, u32[]{:S(2)}) collective-permute-start(f32[16,8,256]{2,1,0:T(8,128)S(1)} %shard_map.98.refs_0_), channel_id=1, source_target_pairs={{0,16},{8,24},{16,0},{24,8},{1,17},{9,25},{17,1},{25,9},{2,18},{10... | collective-permute-start | bytes 393224 | tf_op jit(solution)/shard_map/ppermute | solution.py:375
  27.7 6.7 %collective-permute-start.9 = (f32[16,8,256]{2,1,0:T(8,128)S(1)}, f32[16,8,256]{2,1,0:T(8,128)S(1)}, u32[]{:S(2)}, u32[]{:S(2)}) collective-permute-start(f32[16,8,256]{2,1,0:T(8,128)S(1)} %shard_map.98.refs_0_), channel_id=1, source_target_pairs={{0,24},{8,0},{16,8},{24,16},{1,25},{9,1},{17,9},{25,17},{2,26},{10... | collective-permute-start | bytes 393224 | tf_op jit(solution)/shard_map/ppermute | solution.py:375
  30.2 3.7 %collective-permute-start.5 = (f32[8,128]{1,0:T(8,128)S(1)}, f32[8,128]{1,0:T(8,128)S(1)}, u32[]{:S(2)}, u32[]{:S(2)}) collective-permute-start(f32[8,128]{1,0:T(8,128)S(1)} %get-tuple-element.27), channel_id=1, source_target_pairs={{0,8},{8,0},{16,24},{24,16},{1,9},{9,1},{17,25},{25,17},{2,10},{10... | collective-permute-start | bytes 12296 | tf_op jit(solution)/shard_map/ppermute | solution.py:365
  33.9 3.6 %collective-permute-start.6 = (f32[8,128]{1,0:T(8,128)S(1)}, f32[8,128]{1,0:T(8,128)S(1)}, u32[]{:S(2)}, u32[]{:S(2)}) collective-permute-start(f32[8,128]{1,0:T(8,128)S(1)} %add.15), channel_id=1, source_target_pairs={{0,16},{8,24},{16,0},{24,8},{1,17},{9,25},{17,1},{25,9},{2,18},{10... | collective-permute-start | bytes 12296 | tf_op jit(solution)/shard_map/ppermute | solution.py:365
  37.5 3.6 %collective-permute-start.10 = (f32[8,128]{1,0:T(8,128)S(1)}, f32[8,128]{1,0:T(8,128)S(1)}, u32[]{:S(2)}, u32[]{:S(2)}) collective-permute-start(f32[8,128]{1,0:T(8,128)S(1)} %add_add_fusion), channel_id=1, source_target_pairs={{0,2},{2,0},{4,6},{6,4},{1,3},{3,1},{5,7},{7,5},{8,10},{10,8},{12,... | collective-permute-start | bytes 12296 | tf_op jit(solution)/shard_map/ppermute | solution.py:365
  41.1 4.5 %collective-permute-start.11 = (f32[8,128]{1,0:T(8,128)S(1)}, f32[8,128]{1,0:T(8,128)S(1)}, u32[]{:S(2)}, u32[]{:S(2)}) collective-permute-start(f32[8,128]{1,0:T(8,128)S(1)} %add.18.refs_1_), channel_id=1, source_target_pairs={{0,4},{2,6},{4,0},{6,2},{1,5},{3,7},{5,1},{7,3},{8,12},{10,14},{12... | collective-permute-start | bytes 12296 | tf_op jit(solution)/shard_map/ppermute | solution.py:365
  46.5 1.6 %collective-permute-start.12 = (f32[128,512]{1,0:T(8,128)S(1)}, f32[128,512]{1,0:T(8,128)S(1)}, u32[]{:S(2)}, u32[]{:S(2)}) collective-permute-start(f32[128,512]{1,0:T(8,128)S(1)} %get-tuple-element.39), channel_id=1, source_target_pairs={{0,1},{1,0},{2,3},{3,2},{4,5},{5,4},{6,7},{7,6},{8,9},{9,8},{10,11... | collective-permute-start | bytes 786440 | tf_op jit(solution)/shard_map/ppermute | solution.py:365
  46.6 1.5 %collective-permute-start.13 = (f32[8,128]{1,0:T(8,128)S(1)}, f32[8,128]{1,0:T(8,128)S(1)}, u32[]{:S(2)}, u32[]{:S(2)}) collective-permute-start(f32[8,128]{1,0:T(8,128)S(1)} %add.19.after_ref.refs_2_), channel_id=1, source_target_pairs={{0,1},{1,0},{2,3},{3,2},{4,5},{5,4},{6,7},{7,6},{8,9},{9,8},{10,11... | collective-permute-start | bytes 12296 | tf_op jit(solution)/shard_map/ppermute | solution.py:375

commit v3 on v2

--- a/solution.py
+++ b/solution.py
@@ -15,7 +15,6 @@
 f32 = jnp.float32
 bf16 = jnp.bfloat16
 VMEM = pl.BlockSpec(memory_space=pltpu.VMEM)
-SMEM = pl.BlockSpec(memory_space=pltpu.SMEM)
 HBM = pl.BlockSpec(memory_space=pltpu.HBM)
 TN = (((0,), (0,)), ((), ()))
 NT = (((1,), (1,)), ((), ()))
@@ -49,6 +48,10 @@
     cosine = jnp.where(turn == 0, one, zero) - jnp.where(turn == 2, one, zero)
     sine = jnp.where(turn == 1, one, zero) - jnp.where(turn == 3, one, zero)
     return cosine, sine
+
+
+def phase_of(phase_ref, block):
+    return phase_ref[2 * block : 2 * block + 1, :], phase_ref[2 * block + 1 : 2 * block + 2, :]
 
 
 def spread(values, row_weight, whigh, wlow, xhigh, xlow, k, coils, ty):
@@ -111,19 +114,29 @@
 
 
 def rhs_kernel(
-    coils, blocks, place_ref, tile_ref, cycle_ref, table_ref, cols_ref, rows_ref, data_ref, weight_ref, coil_any,
-    part_ref, whigh, wlow, fwd, adj, row_weight_ref, coil, kept_ref, xhigh, xlow, upper, sems,
+    coils, blocks, cycle_ref, tile_any, table_any, cols_any, rows_any, data_any, weight_any, coil_any,
+    part_ref, whigh, wlow, fwd, adj, row_weight_ref, coil, weight_ref, phase_ref,
+    tile_ref, table_ref, cols_ref, rows_ref, data_ref, xhigh, xlow, upper, sems,
 ):
     ny = table_ref.shape[1]
     half = ny // 2
     ty, tx = rows_ref.shape[0], cols_ref.shape[0]
     sb = rows_ref.shape[1] // blocks
-    fetches = [
-        pltpu.make_async_copy(coil_any.at[:, half:, :], upper, sems.at[0]),
-        pltpu.make_async_copy(coil_any.at[:, :half, :], coil.at[:, :half, :], sems.at[1]),
+    moves = [
+        (tile_any, tile_ref),
+        (table_any, table_ref),
+        (cols_any, cols_ref),
+        (rows_any, rows_ref),
+        (data_any, data_ref),
+        (weight_any, weight_ref),
+        (coil_any.at[:, half:, :], upper),
+        (coil_any.at[:, :half, :], coil.at[:, :half, :]),
     ]
+    fetches = [pltpu.make_async_copy(source, target, sems.at[i]) for i, (source, target) in enumerate(moves)]
     for fetch in fetches:
         fetch.start()
+    for fetch in fetches[:-3]:
+        fetch.wait()
 
     first = lax.broadcasted_iota(jnp.int32, (ty, half), 1) == 0
     for k in range(blocks):
@@ -159,12 +172,14 @@
         turned = rows_ref[:, here].astype(f32)
         row_weight = jnp.concatenate([turned, turned], axis=1)
         row_weight_ref[k] = row_weight
-        cosine, sine = quarter_turn(cycle_ref[0], k)
+        for i, part in enumerate(quarter_turn(cycle_ref[0], k)):
+            phase_ref[2 * k + i : 2 * k + i + 1, :] = jnp.full((1, sb), part, f32)
+        cosine, sine = phase_of(phase_ref, k)
         real, imag = data_ref[:, 0, here], data_ref[:, 1, here]
         values = jnp.concatenate([cosine * real + sine * imag, cosine * imag - sine * real], axis=1)
         spread(values, row_weight, whigh[k], wlow[k], xhigh, xlow, k, coils, ty)
 
-    for fetch in fetches:
+    for fetch in fetches[-3:]:
         fetch.wait()
     order = mirror(half)
     for c in range(coils):
@@ -172,14 +187,13 @@
     lower_rows, upper_rows = back_rows(adj, xhigh, xlow, coil, 0, coils)
     part_ref[:half, :] = lower_rows
     part_ref[half:ny, :] = upper_rows
-    kept_ref[...] = weight_ref[...]
     count = weight_ref.shape[0]
     edge = jnp.concatenate([weight_ref[0:1, :], weight_ref[count - 1 : count, :]], axis=0)
     edge = jnp.concatenate([edge, jnp.zeros((6, edge.shape[1]), f32)], axis=0)
     part_ref[ny:, :] = jnp.concatenate([edge, jnp.zeros_like(edge)], axis=1)
 
 
-def sum_kernel(ny, place_ref, *refs):
+def sum_kernel(ny, *refs):
     parts, (folded_ref, image_ref, mine_ref) = refs[:-3], refs[-3:]
     total = parts[0][:ny, :]
     for part in parts[1:]:
@@ -188,11 +202,11 @@
     image_ref[: ny // 2, :] = total[: ny // 2]
     image_ref[ny // 2 :, :] = mirrored(total[ny // 2 :])
     count = mine_ref.shape[0]
-    mine_ref[...] = image_ref[pl.ds(pl.multiple_of(place_ref[0] * count, count), count), :]
+    mine_ref[...] = image_ref[pl.ds(pl.multiple_of(lax.axis_index("row") * count, count), count), :]
 
 
 def predict_kernel(
-    coils, blocks, cycle_ref, row_weight_ref, image_ref, fwd, coil, whigh, wlow, out_ref, thigh, tlow
+    coils, blocks, phase_ref, row_weight_ref, image_ref, fwd, coil, whigh, wlow, out_ref, thigh, tlow
 ):
     ny, nx = image_ref.shape[0], image_ref.shape[1] // 2
     half = ny // 2
@@ -238,11 +252,11 @@
         )
         summed = jnp.sum(product.reshape(coils, ty, 2 * sb) * row_weight_ref[k][None, :, :], axis=1)
         real, imag = summed[:, :sb], summed[:, sb:]
-        cosine, sine = quarter_turn(cycle_ref[0], k)
+        cosine, sine = phase_of(phase_ref, k)
         out_ref[k] = jnp.concatenate([cosine * real - sine * imag, sine * real + cosine * imag], axis=1)
 
 
-def spread_kernel(coils, blocks, cycle_ref, row_weight_ref, whigh, wlow, *refs):
+def spread_kernel(coils, blocks, phase_ref, row_weight_ref, whigh, wlow, *refs):
     parts, (xhigh, xlow, sums_ref) = refs[:-3], refs[-3:]
     ty = row_weight_ref.shape[1]
     sb = row_weight_ref.shape[2] // 2
@@ -252,7 +266,7 @@
         for part in parts[1:]:
             total = total + part[k]
         squares += total * total
-        cosine, sine = quarter_turn(cycle_ref[0], k)
+        cosine, sine = phase_of(phase_ref, k)
         real, imag = total[:, :sb], total[:, sb:]
         values = jnp.concatenate([cosine * real + sine * imag, cosine * imag - sine * real], axis=1)
         spread(values, row_weight_ref[k], whigh[k], wlow[k], xhigh, xlow, k, coils, ty)
@@ -268,7 +282,7 @@
         out_ref[here, :] = rows + refs[0][here, :] if first else rows
 
 
-def cut_kernel(place_ref, after_ref, folded_ref, *refs):
+def cut_kernel(after_ref, folded_ref, *refs):
     *out_refs, whole = refs
     total = whole.shape[0]
     half = total // 2
@@ -276,14 +290,14 @@
     whole[half:, :] = mirrored(folded_ref[half:, :])
     for shift, out_ref in enumerate(out_refs):
         count = out_ref.shape[0]
-        start = lax.rem(place_ref[0] + shift, total // count) * count
+        start = lax.rem(lax.axis_index("row") + shift, total // count) * count
         out_ref[...] = whole[pl.ds(pl.multiple_of(start, count), count), :]
 
 
-def neighbours(place_ref, image_ref, weight, before_ref, after_ref):
+def neighbours(image_ref, weight, before_ref, after_ref):
     count, nx = weight.shape
     total = image_ref.shape[0]
-    place = place_ref[0]
+    place = lax.axis_index("row")
     start = place * count
     weight_up = jnp.where(place > 0, before_ref[total + 1 : total + 2, :nx], 0.0)
     weight_down = jnp.where(place < total // count - 1, after_ref[total : total + 1, :nx], 0.0)
@@ -302,13 +316,13 @@
 
 
 def smooth_kernel(
-    place_ref, image_ref, own_ref, even_ref, odd_ref, weight_ref, weight_even_ref, weight_odd_ref,
+    image_ref, own_ref, even_ref, odd_ref, weight_ref, weight_even_ref, weight_odd_ref,
     before_ref, after_ref, out_ref, sums_ref,
 ):
     nx = image_ref.shape[1] // 2
     weight, weight_even, weight_odd = weight_ref[...], weight_even_ref[...], weight_odd_ref[...]
     weight_up, weight_down, image_up, image_down, column, above, below = neighbours(
-        place_ref, image_ref, weight, before_ref, after_ref
+        image_ref, weight, before_ref, after_ref
     )
     weight_left = jnp.where(column == 0, 0.0, pltpu.roll(weight, 1, 1))
     weight_right = jnp.where(column == nx - 1, 0.0, pltpu.roll(weight, nx - 1, 1))
@@ -385,20 +399,19 @@
     sb = samples // blocks
     count = weight.shape[0]
     rows, groups = lax.axis_size("row"), lax.axis_size("grp")
-    row_place = lax.axis_index("row")
     table = jnp.asarray(dft_table(ny))
     wide = blocks * ty
     w_shape = (blocks, 2 * sb, nx)
     row_flops = 2 * 3 * coils * wide * ny * width
     col_flops = 2 * 3 * coils * ty * blocks * (2 * sb) * width
-    place = jnp.stack([row_place, jnp.int32(rows)])
     dma = pltpu.SemaphoreType.DMA
     x_shape = pltpu.VMEM((coils, wide, width), bf16)
 
-    data, weight, profiles, cols, rows_of, tile_index, table = (
-        pltpu.with_memory_space_constraint(x, pltpu.HBM)
-        for x in (data, weight, profiles, kernel_cols.T, kernel_rows.T, tile_index, table)
-    )
+    inputs = [tile_index, table, kernel_cols.T, kernel_rows.T, data, weight, profiles]
+    fetched = [
+        pltpu.SMEM(tile_index.shape, tile_index.dtype),
+        *[pltpu.VMEM(x.shape, x.dtype) for x in inputs[1:5]],
+    ]
     partial, *kept = call(
         functools.partial(rhs_kernel, coils, blocks),
         [
@@ -410,14 +423,15 @@
             pltpu.VMEM((blocks, ty, 2 * sb), f32),
             pltpu.VMEM(profiles.shape, bf16),
             pltpu.VMEM(weight.shape, f32),
+            pltpu.VMEM((2 * blocks, sb), f32),
         ],
-        [SMEM, SMEM, SMEM, VMEM, VMEM, VMEM, VMEM, VMEM, HBM],
-        [VMEM] * 8,
-        [x_shape, x_shape, pltpu.VMEM((coils, ny // 2, width), bf16), dma((2,))],
+        [pl.BlockSpec(memory_space=pltpu.SMEM)] + [HBM] * len(inputs),
+        [VMEM] * 9,
+        [*fetched, x_shape, x_shape, pltpu.VMEM((coils, ny // 2, width), bf16), dma((len(inputs) + 1,))],
         row_flops + 2 * col_flops,
         limit=large_vmem,
-    )(place, tile_index, caipi_cycle, table, cols, rows_of, data, weight, profiles)
-    whigh, wlow, fwd, adj, row_weight, coil, weight = (
+    )(caipi_cycle, *(pltpu.with_memory_space_constraint(x, pltpu.HBM) for x in inputs))
+    whigh, wlow, fwd, adj, row_weight, coil, weight, phases = (
         pltpu.with_memory_space_constraint(x, pltpu.VMEM) for x in kept
     )
 
@@ -430,42 +444,42 @@
     folded, image, mine = call(
         functools.partial(sum_kernel, ny),
         [shape((ny, width)), shape((ny, width)), shape((count, width))],
-        [SMEM] + [VMEM] * (1 + len(received)),
+        [VMEM] * (1 + len(received)),
         [VMEM] * 3,
-    )(place, partial, *received)
+    )(partial, *received)
     others = [lax.ppermute(mine, "grp", pairs) for pairs in (even_pairs, odd_pairs)]
 
     predicted = call(
         functools.partial(predict_kernel, coils, blocks),
         shape((blocks, coils, 2 * sb)),
-        [SMEM] + [VMEM] * 6,
+        [VMEM] * 7,
         VMEM,
         [pltpu.VMEM((blocks, 2, coils * ty, nx), bf16)] * 2,
         row_flops + col_flops,
         limit=large_vmem,
-    )(caipi_cycle, row_weight, folded, fwd, coil, whigh, wlow)
-
-    predicted = [predicted, *from_others(predicted, "band")]
+    )(phases, row_weight, folded, fwd, coil, whigh, wlow)
+
+    predicted = [predicted, *[exchange(predicted, "band", step) for step in range(lax.axis_size("band") - 1, 0, -1)]]
     smoothed, sums = call(
         smooth_kernel,
         [shape((count, width)), shape((8, 128))],
-        [SMEM] + [VMEM] * 9,
+        [VMEM] * 9,
         [VMEM, VMEM],
-    )(place, image, mine, *others, weight, *weights, received[0], received[-1])
-    for step in powers("band"):
-        sums = sums + exchange(sums, "band", step)
+    )(image, mine, *others, weight, *weights, received[0], received[-1])
+    bands = range(lax.axis_size("band") - 1, 0, -1)
+    sums = [sums, *[exchange(sums, "band", step) for step in bands]]
 
     *kept, squares = call(
         functools.partial(spread_kernel, coils, blocks),
         [x_shape, x_shape, shape((8, 128))],
-        [SMEM] + [VMEM] * (3 + len(predicted)),
+        [VMEM] * (4 + len(predicted)),
         [VMEM] * 3,
         (),
         col_flops,
         limit=large_vmem,
-    )(caipi_cycle, row_weight, whigh, wlow, *predicted)
+    )(phases, row_weight, whigh, wlow, *predicted)
     xhigh, xlow = (pltpu.with_memory_space_constraint(x, pltpu.VMEM) for x in kept)
-    sums = sums + squares
+    sums = sum(sums) + squares
 
     steps = powers("grp")
     for step in steps[:-1]:
@@ -488,10 +502,10 @@
     halves = call(
         cut_kernel,
         [shape((count, width))] * 2 if rows == 2 else [shape((ny, width))],
-        [SMEM] + [VMEM] * 2,
+        [VMEM] * 2,
         [VMEM] * (2 if rows == 2 else 1),
         [pltpu.VMEM((ny, width), f32)],
-    )(place, sums, unfinished)
+    )(sums, unfinished)
     if rows == 2:
         images = [halves[0], exchange(halves[1], "row", 1)]
     else:

time: 49.2 us -> 45.5 us (0.925)
  waiting for transfers between devices: 6.92 us -> 2.76 us
  starting transfers between devices: 19.2 us -> 23 us
  Pallas kernels: 21.5 us -> 18.1 us
    ppermute x5 -> x9, starting transfers between devices: 5.21 us -> 13.4 us  [exchange(): lax.ppermute(values, axis, [(i, i ^ step) for i in range(lax.axis_size(ax...]
    ppermute x5 -> x2, starting transfers between devices: 5.51 us -> 1.01 us  [from_others(): lax.ppermute(values, axis, [(i, (i + shift) % count) for i in range(count)])]
    ppermute x5 -> x9, waiting for transfers between devices: 5.87 us -> 1.72 us  [exchange(): lax.ppermute(values, axis, [(i, i ^ step) for i in range(lax.axis_size(ax...]
    pallas_call x1, Pallas kernels: 9.01 us -> 7.35 us  [on_device(): call(functools.partial(rhs_kernel, coils, blocks), [shape((ny + 8, width)...]
    pallas_call x1, Pallas kernels: 0.89 us -> 0.34 us  [on_device(): call(functools.partial(sum_kernel, ny), [shape((ny, width)), shape((ny, w...]
    pallas_call x1, Pallas kernels: 1.05 us -> 0.51 us  [on_device(): call(smooth_kernel, [shape((count, width)), shape((8, 128))], [VMEM] * 9,...]
    pallas_call x1, Pallas kernels: 0.89 us -> 0.34 us  [on_device(): call(cut_kernel, [shape((count, width))] * 2 if rows == 2 else [shape((ny...]
    ppermute x5 -> x2, waiting for transfers between devices: 1.04 us -> 1.03 us  [from_others(): lax.ppermute(values, axis, [(i, (i + shift) % count) for i in range(count)])]
  transfers between devices with their start and end apart: 14 -> 15, of which waited for: 5 -> 3; matrix products, arithmetic and copies ran while one was open for 0% -> 0% of each run, Pallas kernels for 22% -> 21%
where the time goes in v3:
time: 45.5 us; the launch traced here: 45.3 us
  starting transfers between devices  23 us (51%)
  Pallas kernels  18.1 us (40%)
  waiting for transfers between devices  2.76 us (6%)
  between operations  1.41 us (3%)
    ppermute x9, starting transfers between devices, exchange(): lax.ppermute(values, axis, [(i, i ^ step) for i in range(lax.axis_size(ax...  13.4 us
    pallas_call x1, Pallas kernels, on_device(): call(functools.partial(rhs_kernel, coils, blocks), [shape((ny + 8, width)...  7.35 us
    ppermute x2, starting transfers between devices, on_device(): lax.ppermute(mine, 'grp', pairs)  5.3 us
    pallas_call x1, Pallas kernels, on_device(): call(functools.partial(predict_kernel, coils, blocks), shape((blocks, coi...  4.33 us
    ppermute x2, starting transfers between devices, on_device(): lax.ppermute(weight, 'grp', pairs)  3.31 us
    pallas_call x2, Pallas kernels, add_rows(): call(functools.partial(rows_kernel, first, last), shape((ny, width)), [VM...  2.46 us
    pallas_call x1, Pallas kernels, on_device(): call(functools.partial(spread_kernel, coils, blocks), [x_shape, x_shape,...  1.87 us
    ppermute x9, waiting for transfers between devices, exchange(): lax.ppermute(values, axis, [(i, i ^ step) for i in range(lax.axis_size(ax...  1.72 us
  transfers between devices with their start and end apart: 15, of which 3 were waited for; matrix products, arithmetic and copies ran while one was open for 0% of the time, Pallas kernels for 21%

profile of v3, /device:TPU:0, one launch (start us, length us, event | category | flops | bytes accessed | tf_op | source)
XLA Modules:
  0.0 45.3 jit_solution(753328711378425290)
XLA Ops:
  1.3 7.3 %shard_map.95 = (f32[264,512]{1,0:T(8,128)S(1)}, bf16[16,256,256]{2,1,0:T(8,128)(2,1)S(1)}, bf16[16,256,256]{2,1,0:T(8,128)(2,1)S(1)}, bf16[256,768]{1,0:T(8,128...) custom-call(s32[1]{0:T(128)S(6)} %copy.10.cycle_ref, ...), custom_call_target="tpu_custom_call" | custom-call | flops 4831838208 | tf_op jit(solution)/shard_map/pallas_call | solution.py:415
  8.6 0.5 %collective-permute-start = (f32[264,512]{1,0:T(8,128)S(1)}, f32[264,512]{1,0:T(8,128)S(1)}, u32[]{:S(2)}, u32[]{:S(2)}) collective-permute-start(f32[264,512]{1,0:T(8,128)S(1)} %get-tuple-element.23.refs_0_), channel_id=1, source_target_pairs={{0,1},{1,0},{2,3},{3,2},{4,5},{5,4},{6,7},{7,6},{8,9},{9,8},{10,11... | collective-permute-start | bytes 1622024 | tf_op jit(solution)/shard_map/ppermute | solution.py:389
  9.2 2.6 %collective-permute-start.3 = (f32[128,256]{1,0:T(8,128)S(1)}, f32[128,256]{1,0:T(8,128)S(1)}, u32[]{:S(2)}, u32[]{:S(2)}) collective-permute-start(f32[128,256]{1,0:T(8,128)S(1)} %get-tuple-element.26.weight_ref), channel_id=1, source_target_pairs={{0,2},{2,0},{4,6},{6,4},{1,3},{3,1},{5,7},{7,5},{8,10},{10,8},{12,... | collective-permute-start | bytes 393224 | tf_op jit(solution)/shard_map/ppermute | solution.py:443
  11.8 0.7 %collective-permute-start.4 = (f32[128,256]{1,0:T(8,128)S(1)}, f32[128,256]{1,0:T(8,128)S(1)}, u32[]{:S(2)}, u32[]{:S(2)}) collective-permute-start(f32[128,256]{1,0:T(8,128)S(1)} %get-tuple-element.26.weight_ref), channel_id=1, source_target_pairs={{2,4},{4,2},{3,5},{5,3},{10,12},{12,10},{11,13},{13,11},{18,20},{2... | collective-permute-start | bytes 393224 | tf_op jit(solution)/shard_map/ppermute | solution.py:443
  12.5 0.3 shard_map.96
  12.8 4.5 %collective-permute-start.1 = (f32[128,512]{1,0:T(8,128)S(1)}, f32[128,512]{1,0:T(8,128)S(1)}, u32[]{:S(2)}, u32[]{:S(2)}) collective-permute-start(f32[128,512]{1,0:T(8,128)S(1)} %get-tuple-element.24.own_ref), channel_id=1, source_target_pairs={{0,2},{2,0},{4,6},{6,4},{1,3},{3,1},{5,7},{7,5},{8,10},{10,8},{12,... | collective-permute-start | bytes 786440 | tf_op jit(solution)/shard_map/ppermute | solution.py:450
  17.3 0.8 %collective-permute-start.2 = (f32[128,512]{1,0:T(8,128)S(1)}, f32[128,512]{1,0:T(8,128)S(1)}, u32[]{:S(2)}, u32[]{:S(2)}) collective-permute-start(f32[128,512]{1,0:T(8,128)S(1)} %get-tuple-element.24.own_ref), channel_id=1, source_target_pairs={{2,4},{4,2},{3,5},{5,3},{10,12},{12,10},{11,13},{13,11},{18,20},{2... | collective-permute-start | bytes 786440 | tf_op jit(solution)/shard_map/ppermute | solution.py:450
  18.1 4.3 %shard_map.98.refs_0_ = f32[16,8,256]{2,1,0:T(8,128)S(1)} custom-call(f32[32,128]{1,0:T(8,128)S(1)} %get-tuple-element.29.phase_ref, f32[16,16,256]{2,1,0:T(8,128)S(1)} %get-tuple-element.30.row_weight_ref, f32[256,512]{1,0:T(8,128)S(1)} %get-tuple-element.33.image_ref, bf16[256,768]{1,0:T(8,128)(2,1)S(1)} %get-tuple-element.34.fwd, ...), custom_call_target="tpu_custom_call" | custom-call | flops 3221225472 | tf_op jit(solution)/shard_map/pallas_call | solution.py:452
  22.5 2.5 %collective-permute-start.8 = (f32[16,8,256]{2,1,0:T(8,128)S(1)}, f32[16,8,256]{2,1,0:T(8,128)S(1)}, u32[]{:S(2)}, u32[]{:S(2)}) collective-permute-start(f32[16,8,256]{2,1,0:T(8,128)S(1)} %shard_map.98.refs_0_), channel_id=1, source_target_pairs={{0,24},{8,16},{16,8},{24,0},{1,25},{9,17},{17,9},{25,1},{2,26},{10... | collective-permute-start | bytes 393224 | tf_op jit(solution)/shard_map/ppermute | solution.py:379
  25.0 0.5 %collective-permute-start.9 = (f32[16,8,256]{2,1,0:T(8,128)S(1)}, f32[16,8,256]{2,1,0:T(8,128)S(1)}, u32[]{:S(2)}, u32[]{:S(2)}) collective-permute-start(f32[16,8,256]{2,1,0:T(8,128)S(1)} %shard_map.98.refs_0_), channel_id=1, source_target_pairs={{0,16},{8,24},{16,0},{24,8},{1,17},{9,25},{17,1},{25,9},{2,18},{10... | collective-permute-start | bytes 393224 | tf_op jit(solution)/shard_map/ppermute | solution.py:379
  25.5 0.5 %collective-permute-start.10 = (f32[16,8,256]{2,1,0:T(8,128)S(1)}, f32[16,8,256]{2,1,0:T(8,128)S(1)}, u32[]{:S(2)}, u32[]{:S(2)}) collective-permute-start(f32[16,8,256]{2,1,0:T(8,128)S(1)} %shard_map.98.refs_0_), channel_id=1, source_target_pairs={{0,8},{8,0},{16,24},{24,16},{1,9},{9,1},{17,25},{25,17},{2,10},{10... | collective-permute-start | bytes 393224 | tf_op jit(solution)/shard_map/ppermute | solution.py:379
  26.0 0.5 %shard_map.97 = (f32[128,512]{1,0:T(8,128)S(1)}, f32[8,128]{1,0:T(8,128)S(1)}) custom-call(f32[256,512]{1,0:T(8,128)S(1)} %get-tuple-element.25.image_ref, f32[128,512]{1,0:T(8,128)S(1)} %get-tuple-element.24.own_ref, f32[128,512]{1,0:T(8,128)S(1)} %collective-permute-done.1.even_ref, f32[128,512]{1,0:T(8,128)S(1)} %collective-permute-done.2.odd_ref, ...), custom_call_target="tpu_custom_call" | custom-call | tf_op jit(solution)/shard_map/pallas_call | solution.py:463
  26.6 1.6 %collective-permute-start.7 = (f32[8,128]{1,0:T(8,128)S(1)}, f32[8,128]{1,0:T(8,128)S(1)}, u32[]{:S(2)}, u32[]{:S(2)}) collective-permute-start(f32[8,128]{1,0:T(8,128)S(1)} %get-tuple-element.28), channel_id=1, source_target_pairs={{0,8},{8,0},{16,24},{24,16},{1,9},{9,1},{17,25},{25,17},{2,10},{10... | collective-permute-start | bytes 12296 | tf_op jit(solution)/shard_map/ppermute | solution.py:379
  28.1 1.5 %collective-permute-start.6 = (f32[8,128]{1,0:T(8,128)S(1)}, f32[8,128]{1,0:T(8,128)S(1)}, u32[]{:S(2)}, u32[]{:S(2)}) collective-permute-start(f32[8,128]{1,0:T(8,128)S(1)} %get-tuple-element.28), channel_id=1, source_target_pairs={{0,16},{8,24},{16,0},{24,8},{1,17},{9,25},{17,1},{25,9},{2,18},{10... | collective-permute-start | bytes 12296 | tf_op jit(solution)/shard_map/ppermute | solution.py:379
  29.6 0.0 collective-permute-done.8.refs_1_
  29.6 2.7 %collective-permute-start.5 = (f32[8,128]{1,0:T(8,128)S(1)}, f32[8,128]{1,0:T(8,128)S(1)}, u32[]{:S(2)}, u32[]{:S(2)}) collective-permute-start(f32[8,128]{1,0:T(8,128)S(1)} %get-tuple-element.28), channel_id=1, source_target_pairs={{0,24},{8,16},{16,8},{24,0},{1,25},{9,17},{17,9},{25,1},{2,26},{10... | collective-permute-start | bytes 12296 | tf_op jit(solution)/shard_map/ppermute | solution.py:379
  32.3 0.0 collective-permute-done.9.refs_2_
  32.3 0.0 collective-permute-done.10.refs_3_
  32.3 1.9 %shard_map.99 = (bf16[8,256,512]{2,1,0:T(8,128)(2,1)S(1)}, bf16[8,256,512]{2,1,0:T(8,128)(2,1)S(1)}, f32[8,128]{1,0:T(8,128)S(1)}) custom-call(f32[32,128]{1,0:T(8,128)S(1)} %get-tuple-element.29.phase_ref, f32[16,16,256]{2,1,0:T(8,128)S(1)} %get-tuple-element.30.row_weight_ref, bf16[16,256,256]{2,1,0:T(8,128)(2,1)S(1)} %get-tuple-element.31.whigh, ...), custom_call_target="tpu_custom_call" | custom-call | flops 1610612736 | tf_op jit(solution)/shard_map/pallas_call | solution.py:472
  34.2 0.0 collective-permute-done.7
  34.2 0.0 collective-permute-done.5
  34.2 1.3 %collective-permute-start.11 = (f32[8,128]{1,0:T(8,128)S(1)}, f32[8,128]{1,0:T(8,128)S(1)}, u32[]{:S(2)}, u32[]{:S(2)}) collective-permute-start(f32[8,128]{1,0:T(8,128)S(1)} %add_add_fusion), channel_id=1, source_target_pairs={{0,2},{2,0},{4,6},{6,4},{1,3},{3,1},{5,7},{7,5},{8,10},{10,8},{12,... | collective-permute-start | bytes 12296 | tf_op jit(solution)/shard_map/ppermute | solution.py:379
  35.5 1.2 %shard_map.100.refs_0_ = f32[256,512]{1,0:T(8,128)S(1)} custom-call(bf16[256,768]{1,0:T(8,128)(2,1)S(1)} %get-tuple-element.37.adj, bf16[8,256,512]{2,1,0:T(8,128)(2,1)S(1)} %get-tuple-element.35.coil, bf16[8,256,512]{2,1,0:T(8,128)(2,1)S(1)} %get-tuple-element.38.xhigh, bf16[8,256,512]{2,1,0:T(8,128)(2,1)S(1)} %get-tuple-element.39.xlow), custom_call_target="tpu_custom_call" | custom-call | flops 805306368 | tf_op jit(solution)/shard_map/pallas_call | solution.py:490
  36.7 1.2 %collective-permute-done.11 = f32[8,128]{1,0:T(8,128)S(1)} collective-permute-done((f32[8,128]{1,0:T(8,128)S(1)}, f32[8,128]{1,0:T(8,128)S(1)}, u32[]{:S(2)}, u32[]{:S(2)}) %collective-permute-start.11) | collective-permute-done | bytes 4128 | tf_op jit(solution)/shard_map/ppermute | solution.py:379
  37.9 2.7 %collective-permute-start.12 = (f32[8,128]{1,0:T(8,128)S(1)}, f32[8,128]{1,0:T(8,128)S(1)}, u32[]{:S(2)}, u32[]{:S(2)}) collective-permute-start(f32[8,128]{1,0:T(8,128)S(1)} %add.22.refs_1_), channel_id=1, source_target_pairs={{0,4},{2,6},{4,0},{6,2},{1,5},{3,7},{5,1},{7,3},{8,12},{10,14},{12... | collective-permute-start | bytes 12296 | tf_op jit(solution)/shard_map/ppermute | solution.py:379
  40.6 1.2 %shard_map.101.folded_ref = f32[256,512]{1,0:T(8,128)S(1)} custom-call(bf16[256,768]{1,0:T(8,128)(2,1)S(1)} %get-tuple-element.37.adj, bf16[8,256,512]{2,1,0:T(8,128)(2,1)S(1)} %get-tuple-element.35.coil, bf16[8,256,512]{2,1,0:T(8,128)(2,1)S(1)} %get-tuple-element.38.xhigh, bf16[8,256,512]{2,1,0:T(8,128)(2,1)S(1)} %get-tuple-element.39.xlow, ...), custom_call_target="tpu_custom_call" | custom-call | flops 805306368 | tf_op jit(solution)/shard_map/pallas_call | solution.py:490
  41.9 0.5 %collective-permute-done.12 = f32[8,128]{1,0:T(8,128)S(1)} collective-permute-done((f32[8,128]{1,0:T(8,128)S(1)}, f32[8,128]{1,0:T(8,128)S(1)}, u32[]{:S(2)}, u32[]{:S(2)}) %collective-permute-start.12) | collective-permute-done | bytes 4128 | tf_op jit(solution)/shard_map/ppermute | solution.py:379
  42.4 0.3 shard_map.102
  42.8 0.1 collective-permute-start.13
  42.9 0.5 %collective-permute-start.14 = (f32[8,128]{1,0:T(8,128)S(1)}, f32[8,128]{1,0:T(8,128)S(1)}, u32[]{:S(2)}, u32[]{:S(2)}) collective-permute-start(f32[8,128]{1,0:T(8,128)S(1)} %add.23.after_ref.refs_2_), channel_id=1, source_target_pairs={{0,1},{1,0},{2,3},{3,2},{4,5},{5,4},{6,7},{7,6},{8,9},{9,8},{10,11... | collective-permute-start | bytes 12296 | tf_op jit(solution)/shard_map/ppermute | solution.py:389
  43.3 1.0 %collective-permute-done.14.refs_3_ = f32[8,128]{1,0:T(8,128)S(1)} collective-permute-done((f32[8,128]{1,0:T(8,128)S(1)}, f32[8,128]{1,0:T(8,128)S(1)}, u32[]{:S(2)}, u32[]{:S(2)}) %collective-permute-start.14) | collective-permute-done | bytes 4128 | tf_op jit(solution)/shard_map/ppermute | solution.py:389
  44.4 0.9 %shard_map.103 = (f32[128,512]{1,0:T(8,128)}, f32[128,512]{1,0:T(8,128)}) custom-call(f32[128,512]{1,0:T(8,128)S(1)} %get-tuple-element.24.own_ref, f32[128,512]{1,0:T(8,128)S(1)} %get-tuple-element.27.smooth_ref, f32[128,512]{1,0:T(8,128)S(1)} %get-tuple-element.40.refs_0_, f32[128,512]{1,0:T(8,128)S(1)} %collective-permute-done.13.refs_1_, ...), custom_call_target="tpu_custom_call" | custom-call | tf_op jit(solution)/shard_map/pallas_call | solution.py:514
  (10 shorter events, 0.0 us)
Async XLA Ops:
  8.6 3.8 %collective-permute-start = (f32[264,512]{1,0:T(8,128)S(1)}, f32[264,512]{1,0:T(8,128)S(1)}, u32[]{:S(2)}, u32[]{:S(2)}) collective-permute-start(f32[264,512]{1,0:T(8,128)S(1)} %get-tuple-element.23.refs_0_), channel_id=1, source_target_pairs={{0,1},{1,0},{2,3},{3,2},{4,5},{5,4},{6,7},{7,6},{8,9},{9,8},{10,11... | collective-permute-start | bytes 1622024 | tf_op jit(solution)/shard_map/ppermute | solution.py:389
  9.2 15.8 %collective-permute-start.3 = (f32[128,256]{1,0:T(8,128)S(1)}, f32[128,256]{1,0:T(8,128)S(1)}, u32[]{:S(2)}, u32[]{:S(2)}) collective-permute-start(f32[128,256]{1,0:T(8,128)S(1)} %get-tuple-element.26.weight_ref), channel_id=1, source_target_pairs={{0,2},{2,0},{4,6},{6,4},{1,3},{3,1},{5,7},{7,5},{8,10},{10,8},{12,... | collective-permute-start | bytes 393224 | tf_op jit(solution)/shard_map/ppermute | solution.py:443
  11.8 13.7 %collective-permute-start.4 = (f32[128,256]{1,0:T(8,128)S(1)}, f32[128,256]{1,0:T(8,128)S(1)}, u32[]{:S(2)}, u32[]{:S(2)}) collective-permute-start(f32[128,256]{1,0:T(8,128)S(1)} %get-tuple-element.26.weight_ref), channel_id=1, source_target_pairs={{2,4},{4,2},{3,5},{5,3},{10,12},{12,10},{11,13},{13,11},{18,20},{2... | collective-permute-start | bytes 393224 | tf_op jit(solution)/shard_map/ppermute | solution.py:443
  12.8 13.2 %collective-permute-start.1 = (f32[128,512]{1,0:T(8,128)S(1)}, f32[128,512]{1,0:T(8,128)S(1)}, u32[]{:S(2)}, u32[]{:S(2)}) collective-permute-start(f32[128,512]{1,0:T(8,128)S(1)} %get-tuple-element.24.own_ref), channel_id=1, source_target_pairs={{0,2},{2,0},{4,6},{6,4},{1,3},{3,1},{5,7},{7,5},{8,10},{10,8},{12,... | collective-permute-start | bytes 786440 | tf_op jit(solution)/shard_map/ppermute | solution.py:450
  17.3 8.8 %collective-permute-start.2 = (f32[128,512]{1,0:T(8,128)S(1)}, f32[128,512]{1,0:T(8,128)S(1)}, u32[]{:S(2)}, u32[]{:S(2)}) collective-permute-start(f32[128,512]{1,0:T(8,128)S(1)} %get-tuple-element.24.own_ref), channel_id=1, source_target_pairs={{2,4},{4,2},{3,5},{5,3},{10,12},{12,10},{11,13},{13,11},{18,20},{2... | collective-permute-start | bytes 786440 | tf_op jit(solution)/shard_map/ppermute | solution.py:450
  22.5 7.2 %collective-permute-start.8 = (f32[16,8,256]{2,1,0:T(8,128)S(1)}, f32[16,8,256]{2,1,0:T(8,128)S(1)}, u32[]{:S(2)}, u32[]{:S(2)}) collective-permute-start(f32[16,8,256]{2,1,0:T(8,128)S(1)} %shard_map.98.refs_0_), channel_id=1, source_target_pairs={{0,24},{8,16},{16,8},{24,0},{1,25},{9,17},{17,9},{25,1},{2,26},{10... | collective-permute-start | bytes 393224 | tf_op jit(solution)/shard_map/ppermute | solution.py:379
  25.0 7.3 %collective-permute-start.9 = (f32[16,8,256]{2,1,0:T(8,128)S(1)}, f32[16,8,256]{2,1,0:T(8,128)S(1)}, u32[]{:S(2)}, u32[]{:S(2)}) collective-permute-start(f32[16,8,256]{2,1,0:T(8,128)S(1)} %shard_map.98.refs_0_), channel_id=1, source_target_pairs={{0,16},{8,24},{16,0},{24,8},{1,17},{9,25},{17,1},{25,9},{2,18},{10... | collective-permute-start | bytes 393224 | tf_op jit(solution)/shard_map/ppermute | solution.py:379
  25.5 6.8 %collective-permute-start.10 = (f32[16,8,256]{2,1,0:T(8,128)S(1)}, f32[16,8,256]{2,1,0:T(8,128)S(1)}, u32[]{:S(2)}, u32[]{:S(2)}) collective-permute-start(f32[16,8,256]{2,1,0:T(8,128)S(1)} %shard_map.98.refs_0_), channel_id=1, source_target_pairs={{0,8},{8,0},{16,24},{24,16},{1,9},{9,1},{17,25},{25,17},{2,10},{10... | collective-permute-start | bytes 393224 | tf_op jit(solution)/shard_map/ppermute | solution.py:379
  26.6 7.6 %collective-permute-start.7 = (f32[8,128]{1,0:T(8,128)S(1)}, f32[8,128]{1,0:T(8,128)S(1)}, u32[]{:S(2)}, u32[]{:S(2)}) collective-permute-start(f32[8,128]{1,0:T(8,128)S(1)} %get-tuple-element.28), channel_id=1, source_target_pairs={{0,8},{8,0},{16,24},{24,16},{1,9},{9,1},{17,25},{25,17},{2,10},{10... | collective-permute-start | bytes 12296 | tf_op jit(solution)/shard_map/ppermute | solution.py:379
  28.1 6.1 %collective-permute-start.6 = (f32[8,128]{1,0:T(8,128)S(1)}, f32[8,128]{1,0:T(8,128)S(1)}, u32[]{:S(2)}, u32[]{:S(2)}) collective-permute-start(f32[8,128]{1,0:T(8,128)S(1)} %get-tuple-element.28), channel_id=1, source_target_pairs={{0,16},{8,24},{16,0},{24,8},{1,17},{9,25},{17,1},{25,9},{2,18},{10... | collective-permute-start | bytes 12296 | tf_op jit(solution)/shard_map/ppermute | solution.py:379
  29.6 4.6 %collective-permute-start.5 = (f32[8,128]{1,0:T(8,128)S(1)}, f32[8,128]{1,0:T(8,128)S(1)}, u32[]{:S(2)}, u32[]{:S(2)}) collective-permute-start(f32[8,128]{1,0:T(8,128)S(1)} %get-tuple-element.28), channel_id=1, source_target_pairs={{0,24},{8,16},{16,8},{24,0},{1,25},{9,17},{17,9},{25,1},{2,26},{10... | collective-permute-start | bytes 12296 | tf_op jit(solution)/shard_map/ppermute | solution.py:379
  34.2 3.7 %collective-permute-start.11 = (f32[8,128]{1,0:T(8,128)S(1)}, f32[8,128]{1,0:T(8,128)S(1)}, u32[]{:S(2)}, u32[]{:S(2)}) collective-permute-start(f32[8,128]{1,0:T(8,128)S(1)} %add_add_fusion), channel_id=1, source_target_pairs={{0,2},{2,0},{4,6},{6,4},{1,3},{3,1},{5,7},{7,5},{8,10},{10,8},{12,... | collective-permute-start | bytes 12296 | tf_op jit(solution)/shard_map/ppermute | solution.py:379
  37.9 4.5 %collective-permute-start.12 = (f32[8,128]{1,0:T(8,128)S(1)}, f32[8,128]{1,0:T(8,128)S(1)}, u32[]{:S(2)}, u32[]{:S(2)}) collective-permute-start(f32[8,128]{1,0:T(8,128)S(1)} %add.22.refs_1_), channel_id=1, source_target_pairs={{0,4},{2,6},{4,0},{6,2},{1,5},{3,7},{5,1},{7,3},{8,12},{10,14},{12... | collective-permute-start | bytes 12296 | tf_op jit(solution)/shard_map/ppermute | solution.py:379
  42.8 1.6 %collective-permute-start.13 = (f32[128,512]{1,0:T(8,128)S(1)}, f32[128,512]{1,0:T(8,128)S(1)}, u32[]{:S(2)}, u32[]{:S(2)}) collective-permute-start(f32[128,512]{1,0:T(8,128)S(1)} %get-tuple-element.41), channel_id=1, source_target_pairs={{0,1},{1,0},{2,3},{3,2},{4,5},{5,4},{6,7},{7,6},{8,9},{9,8},{10,11... | collective-permute-start | bytes 786440 | tf_op jit(solution)/shard_map/ppermute | solution.py:379
  42.9 1.5 %collective-permute-start.14 = (f32[8,128]{1,0:T(8,128)S(1)}, f32[8,128]{1,0:T(8,128)S(1)}, u32[]{:S(2)}, u32[]{:S(2)}) collective-permute-start(f32[8,128]{1,0:T(8,128)S(1)} %add.23.after_ref.refs_2_), channel_id=1, source_target_pairs={{0,1},{1,0},{2,3},{3,2},{4,5},{5,4},{6,7},{7,6},{8,9},{9,8},{10,11... | collective-permute-start | bytes 12296 | tf_op jit(solution)/shard_map/ppermute | solution.py:389

commit v4 on v3

--- a/solution.py
+++ b/solution.py
@@ -113,10 +113,10 @@
     return jnp.concatenate(sums[:2], axis=1), jnp.concatenate(sums[2:], axis=1)
 
 
-def rhs_kernel(
+def tables_kernel(
     coils, blocks, cycle_ref, tile_any, table_any, cols_any, rows_any, data_any, weight_any, coil_any,
-    part_ref, whigh, wlow, fwd, adj, row_weight_ref, coil, weight_ref, phase_ref,
-    tile_ref, table_ref, cols_ref, rows_ref, data_ref, xhigh, xlow, upper, sems,
+    whigh, wlow, fwd, adj, row_weight_ref, coil, weight_ref, phase_ref, data_ref,
+    tile_ref, table_ref, cols_ref, rows_ref, upper, sems,
 ):
     ny = table_ref.shape[1]
     half = ny // 2
@@ -174,16 +174,26 @@
         row_weight_ref[k] = row_weight
         for i, part in enumerate(quarter_turn(cycle_ref[0], k)):
             phase_ref[2 * k + i : 2 * k + i + 1, :] = jnp.full((1, sb), part, f32)
-        cosine, sine = phase_of(phase_ref, k)
-        real, imag = data_ref[:, 0, here], data_ref[:, 1, here]
-        values = jnp.concatenate([cosine * real + sine * imag, cosine * imag - sine * real], axis=1)
-        spread(values, row_weight, whigh[k], wlow[k], xhigh, xlow, k, coils, ty)
-
     for fetch in fetches[-3:]:
         fetch.wait()
     order = mirror(half)
     for c in range(coils):
         coil[c, half:, :] = matmul(order, upper[c]).astype(bf16)
+
+
+def rhs_kernel(
+    coils, blocks, phase_ref, row_weight_ref, whigh, wlow, adj, coil, data_ref, weight_ref, part_ref, xhigh, xlow
+):
+    ny = adj.shape[0]
+    half = ny // 2
+    ty = row_weight_ref.shape[1]
+    sb = row_weight_ref.shape[2] // 2
+    for k in range(blocks):
+        here = slice(k * sb, (k + 1) * sb)
+        cosine, sine = phase_of(phase_ref, k)
+        real, imag = data_ref[:, 0, here], data_ref[:, 1, here]
+        values = jnp.concatenate([cosine * real + sine * imag, cosine * imag - sine * real], axis=1)
+        spread(values, row_weight_ref[k], whigh[k], wlow[k], xhigh, xlow, k, coils, ty)
     lower_rows, upper_rows = back_rows(adj, xhigh, xlow, coil, 0, coils)
     part_ref[:half, :] = lower_rows
     part_ref[half:ny, :] = upper_rows
@@ -256,22 +266,28 @@
         out_ref[k] = jnp.concatenate([cosine * real - sine * imag, sine * real + cosine * imag], axis=1)
 
 
-def spread_kernel(coils, blocks, phase_ref, row_weight_ref, whigh, wlow, *refs):
-    parts, (xhigh, xlow, sums_ref) = refs[:-3], refs[-3:]
+def collapse_kernel(bands, *refs):
+    parts, sums_refs, (out_ref, out_sums_ref) = refs[:bands], refs[bands:-2], refs[-2:]
+    total = parts[0][...]
+    for part in parts[1:]:
+        total = total + part[...]
+    out_ref[...] = total
+    sums = sums_refs[0][...]
+    for ref in sums_refs[1:]:
+        sums = sums + ref[...]
+    lane = lax.broadcasted_iota(jnp.int32, sums.shape, 1)
+    squares = jnp.sum(jnp.sum(total * total, axis=0))
+    out_sums_ref[...] = jnp.where(lane == 1, sums + squares, sums)
+
+
+def spread_kernel(coils, blocks, phase_ref, row_weight_ref, whigh, wlow, collapsed_ref, xhigh, xlow):
     ty = row_weight_ref.shape[1]
     sb = row_weight_ref.shape[2] // 2
-    squares = 0.0
     for k in range(blocks):
-        total = parts[0][k]
-        for part in parts[1:]:
-            total = total + part[k]
-        squares += total * total
         cosine, sine = phase_of(phase_ref, k)
-        real, imag = total[:, :sb], total[:, sb:]
+        real, imag = collapsed_ref[k, :, :sb], collapsed_ref[k, :, sb:]
         values = jnp.concatenate([cosine * real + sine * imag, cosine * imag - sine * real], axis=1)
         spread(values, row_weight_ref[k], whigh[k], wlow[k], xhigh, xlow, k, coils, ty)
-    lane = lax.broadcasted_iota(jnp.int32, sums_ref.shape, 1)
-    sums_ref[...] = jnp.where(lane == 1, jnp.sum(squares), 0.0)
 
 
 def rows_kernel(first, last, adj, coil, xhigh, xlow, *refs):
@@ -410,12 +426,11 @@
     inputs = [tile_index, table, kernel_cols.T, kernel_rows.T, data, weight, profiles]
     fetched = [
         pltpu.SMEM(tile_index.shape, tile_index.dtype),
-        *[pltpu.VMEM(x.shape, x.dtype) for x in inputs[1:5]],
+        *[pltpu.VMEM(x.shape, x.dtype) for x in inputs[1:4]],
     ]
-    partial, *kept = call(
-        functools.partial(rhs_kernel, coils, blocks),
+    kept = call(
+        functools.partial(tables_kernel, coils, blocks),
         [
-            shape((ny + 8, width)),
             pltpu.VMEM(w_shape, bf16),
             pltpu.VMEM(w_shape, bf16),
             pltpu.VMEM((wide, 3 * ny), bf16),
@@ -424,16 +439,26 @@
             pltpu.VMEM(profiles.shape, bf16),
             pltpu.VMEM(weight.shape, f32),
             pltpu.VMEM((2 * blocks, sb), f32),
+            pltpu.VMEM(data.shape, f32),
         ],
         [pl.BlockSpec(memory_space=pltpu.SMEM)] + [HBM] * len(inputs),
         [VMEM] * 9,
-        [*fetched, x_shape, x_shape, pltpu.VMEM((coils, ny // 2, width), bf16), dma((len(inputs) + 1,))],
-        row_flops + 2 * col_flops,
+        [*fetched, pltpu.VMEM((coils, ny // 2, width), bf16), dma((len(inputs) + 1,))],
+        col_flops,
         limit=large_vmem,
     )(caipi_cycle, *(pltpu.with_memory_space_constraint(x, pltpu.HBM) for x in inputs))
-    whigh, wlow, fwd, adj, row_weight, coil, weight, phases = (
+    whigh, wlow, fwd, adj, row_weight, coil, weight, phases, data = (
         pltpu.with_memory_space_constraint(x, pltpu.VMEM) for x in kept
     )
+    partial = call(
+        functools.partial(rhs_kernel, coils, blocks),
+        shape((ny + 8, width)),
+        [VMEM] * 8,
+        VMEM,
+        [x_shape, x_shape],
+        row_flops + col_flops,
+        limit=large_vmem,
+    )(phases, row_weight, whigh, wlow, adj, coil, data, weight)
 
     received = from_others(partial, "row")
     even_pairs = [(i, i ^ 1) for i in range(groups) if i ^ 1 < groups]
@@ -466,25 +491,27 @@
         [VMEM] * 9,
         [VMEM, VMEM],
     )(image, mine, *others, weight, *weights, received[0], received[-1])
-    bands = range(lax.axis_size("band") - 1, 0, -1)
-    sums = [sums, *[exchange(sums, "band", step) for step in bands]]
-
-    *kept, squares = call(
+    sums = [sums, *[exchange(sums, "band", step) for step in range(1, lax.axis_size("band"))]]
+    collapsed, sums = call(
+        functools.partial(collapse_kernel, len(predicted)),
+        [shape(predicted[0].shape), shape((8, 128))],
+        [VMEM] * (len(predicted) + len(sums)),
+        [VMEM, VMEM],
+    )(*predicted, *sums)
+    steps = powers("grp")
+    for step in steps[:-1]:
+        sums = sums + exchange(sums, "grp", step)
+
+    kept = call(
         functools.partial(spread_kernel, coils, blocks),
-        [x_shape, x_shape, shape((8, 128))],
-        [VMEM] * (4 + len(predicted)),
-        [VMEM] * 3,
+        [x_shape, x_shape],
+        [VMEM] * 5,
+        [VMEM] * 2,
         (),
         col_flops,
         limit=large_vmem,
-    )(phases, row_weight, whigh, wlow, *predicted)
+    )(phases, row_weight, whigh, wlow, collapsed)
     xhigh, xlow = (pltpu.with_memory_space_constraint(x, pltpu.VMEM) for x in kept)
-    sums = sum(sums) + squares
-
-    steps = powers("grp")
-    for step in steps[:-1]:
-        sums = sums + exchange(sums, "grp", step)
-    middle = coils // 2
 
     def add_rows(first, last, *before):
         return call(
@@ -493,11 +520,11 @@
             [VMEM] * (4 + len(before)),
             VMEM,
             (),
-            row_flops // 2,
+            row_flops * (last - first) // coils,
             limit=large_vmem,
         )(adj, coil, xhigh, xlow, *before)
 
-    unfinished = add_rows(middle, coils, add_rows(0, middle), sums)
+    unfinished = add_rows(0, coils, sums)
     sums = sums + exchange(sums, "grp", steps[-1])
     halves = call(
         cut_kernel,

time: 45.5 us -> 43.8 us (0.963)
  starting transfers between devices: 23 us -> 19.5 us
  waiting for transfers between devices: 2.76 us -> 5.65 us
  Pallas kernels: 18.1 us -> 17.1 us
    ppermute x9, starting transfers between devices: 13.4 us -> 9.69 us  [exchange(): lax.ppermute(values, axis, [(i, i ^ step) for i in range(lax.axis_size(ax...]
    ppermute x9, waiting for transfers between devices: 1.72 us -> 4.61 us  [exchange(): lax.ppermute(values, axis, [(i, i ^ step) for i in range(lax.axis_size(ax...]
    ppermute x2, starting transfers between devices: 3.31 us -> 6.14 us  [on_device(): lax.ppermute(weight, 'grp', pairs)]
    ppermute x2, starting transfers between devices: 5.3 us -> 2.63 us  [on_device(): lax.ppermute(mine, 'grp', pairs)]
    pallas_call x2 -> x4, Pallas kernels: 9.22 us -> 8.63 us  [the longest x1 4.19 us: on_device(): call(functools.partial(rhs_kernel, coils, blocks), shape((ny + 8, width))...]
    pallas_call x2 -> x1, Pallas kernels: 2.46 us -> 2.3 us  [add_rows(): call(functools.partial(rows_kernel, first, last), shape((ny, width)), [VM...]
  transfers between devices with their start and end apart: 15 -> 15, of which waited for: 3 -> 6; matrix products, arithmetic and copies ran while one was open for 0% -> 0% of each run, Pallas kernels for 21% -> 21%
where the time goes in v4:
time: 43.8 us; the launch traced here: 43.6 us
  starting transfers between devices  19.5 us (45%)
  Pallas kernels  17.1 us (39%)
  waiting for transfers between devices  5.65 us (13%)
  between operations  1.39 us (3%)
    ppermute x9, starting transfers between devices, exchange(): lax.ppermute(values, axis, [(i, i ^ step) for i in range(lax.axis_size(ax...  9.69 us
    ppermute x2, starting transfers between devices, on_device(): lax.ppermute(weight, 'grp', pairs)  6.14 us
    ppermute x9, waiting for transfers between devices, exchange(): lax.ppermute(values, axis, [(i, i ^ step) for i in range(lax.axis_size(ax...  4.61 us
    pallas_call x1, Pallas kernels, on_device(): call(functools.partial(rhs_kernel, coils, blocks), shape((ny + 8, width))...  4.19 us
    pallas_call x1, Pallas kernels, on_device(): call(functools.partial(predict_kernel, coils, blocks), shape((blocks, coi...  4.05 us
    ppermute x2, starting transfers between devices, on_device(): lax.ppermute(mine, 'grp', pairs)  2.63 us
    pallas_call x1, Pallas kernels, on_device(): call(functools.partial(tables_kernel, coils, blocks), [pltpu.VMEM(w_shape...  2.46 us
    pallas_call x1, Pallas kernels, add_rows(): call(functools.partial(rows_kernel, first, last), shape((ny, width)), [VM...  2.3 us
  transfers between devices with their start and end apart: 15, of which 6 were waited for; matrix products, arithmetic and copies ran while one was open for 0% of the time, Pallas kernels for 21%

profile of v4, /device:TPU:0, one launch (start us, length us, event | category | flops | bytes accessed | tf_op | source)
XLA Modules:
  0.0 43.6 jit_solution(2881160405349016589)
XLA Ops:
  1.3 2.5 %shard_map.95 = (bf16[16,256,256]{2,1,0:T(8,128)(2,1)S(1)}, bf16[16,256,256]{2,1,0:T(8,128)(2,1)S(1)}, bf16[256,768]{1,0:T(8,128)(2,1)S(1)}, bf16[256,768]{1,0:T...) custom-call(s32[1]{0:T(128)S(6)} %copy.10.cycle_ref, ...), custom_call_target="tpu_custom_call" | custom-call | flops 1610612736 | tf_op jit(solution)/shard_map/pallas_call | solution.py:431
  3.7 4.2 %shard_map.96.refs_0_ = f32[264,512]{1,0:T(8,128)S(1)} custom-call(f32[32,128]{1,0:T(8,128)S(1)} %get-tuple-element.24.phase_ref, f32[16,16,256]{2,1,0:T(8,128)S(1)} %get-tuple-element.25.row_weight_ref, bf16[16,256,256]{2,1,0:T(8,128)(2,1)S(1)} %get-tuple-element.26.whigh, bf16[16,256,256]{2,1,0:T(8,128)(2,1)S(1)} %get-tuple-element.27.wlow, ...), custom_call_target="tpu_custom_call" | custom-call | flops 3221225472 | tf_op jit(solution)/shard_map/pallas_call | solution.py:453
  7.9 0.5 %collective-permute-start = (f32[264,512]{1,0:T(8,128)S(1)}, f32[264,512]{1,0:T(8,128)S(1)}, u32[]{:S(2)}, u32[]{:S(2)}) collective-permute-start(f32[264,512]{1,0:T(8,128)S(1)} %shard_map.96.refs_0_), channel_id=1, source_target_pairs={{0,1},{1,0},{2,3},{3,2},{4,5},{5,4},{6,7},{7,6},{8,9},{9,8},{10,11... | collective-permute-start | bytes 1622024 | tf_op jit(solution)/shard_map/ppermute | solution.py:405
  8.5 0.7 %collective-permute-start.4 = (f32[128,256]{1,0:T(8,128)S(1)}, f32[128,256]{1,0:T(8,128)S(1)}, u32[]{:S(2)}, u32[]{:S(2)}) collective-permute-start(f32[128,256]{1,0:T(8,128)S(1)} %get-tuple-element.31.weight_ref), channel_id=1, source_target_pairs={{2,4},{4,2},{3,5},{5,3},{10,12},{12,10},{11,13},{13,11},{18,20},{2... | collective-permute-start | bytes 393224 | tf_op jit(solution)/shard_map/ppermute | solution.py:468
  9.1 5.5 %collective-permute-start.3 = (f32[128,256]{1,0:T(8,128)S(1)}, f32[128,256]{1,0:T(8,128)S(1)}, u32[]{:S(2)}, u32[]{:S(2)}) collective-permute-start(f32[128,256]{1,0:T(8,128)S(1)} %get-tuple-element.31.weight_ref), channel_id=1, source_target_pairs={{0,2},{2,0},{4,6},{6,4},{1,3},{3,1},{5,7},{7,5},{8,10},{10,8},{12,... | collective-permute-start | bytes 393224 | tf_op jit(solution)/shard_map/ppermute | solution.py:468
  14.6 0.0 collective-permute-done.refs_1_.before_ref.after_ref
  14.6 0.3 shard_map.97
  15.0 0.9 %collective-permute-start.2 = (f32[128,512]{1,0:T(8,128)S(1)}, f32[128,512]{1,0:T(8,128)S(1)}, u32[]{:S(2)}, u32[]{:S(2)}) collective-permute-start(f32[128,512]{1,0:T(8,128)S(1)} %get-tuple-element.32.own_ref), channel_id=1, source_target_pairs={{2,4},{4,2},{3,5},{5,3},{10,12},{12,10},{11,13},{13,11},{18,20},{2... | collective-permute-start | bytes 786440 | tf_op jit(solution)/shard_map/ppermute | solution.py:475
  15.8 1.8 %collective-permute-start.1 = (f32[128,512]{1,0:T(8,128)S(1)}, f32[128,512]{1,0:T(8,128)S(1)}, u32[]{:S(2)}, u32[]{:S(2)}) collective-permute-start(f32[128,512]{1,0:T(8,128)S(1)} %get-tuple-element.32.own_ref), channel_id=1, source_target_pairs={{0,2},{2,0},{4,6},{6,4},{1,3},{3,1},{5,7},{7,5},{8,10},{10,8},{12,... | collective-permute-start | bytes 786440 | tf_op jit(solution)/shard_map/ppermute | solution.py:475
  17.6 4.1 %shard_map.99.refs_0_ = f32[16,8,256]{2,1,0:T(8,128)S(1)} custom-call(f32[32,128]{1,0:T(8,128)S(1)} %get-tuple-element.24.phase_ref, f32[16,16,256]{2,1,0:T(8,128)S(1)} %get-tuple-element.25.row_weight_ref, f32[256,512]{1,0:T(8,128)S(1)} %get-tuple-element.35.image_ref, bf16[256,768]{1,0:T(8,128)(2,1)S(1)} %get-tuple-element.36.fwd, ...), custom_call_target="tpu_custom_call" | custom-call | flops 3221225472 | tf_op jit(solution)/shard_map/pallas_call | solution.py:477
  21.6 1.6 %collective-permute-start.7 = (f32[16,8,256]{2,1,0:T(8,128)S(1)}, f32[16,8,256]{2,1,0:T(8,128)S(1)}, u32[]{:S(2)}, u32[]{:S(2)}) collective-permute-start(f32[16,8,256]{2,1,0:T(8,128)S(1)} %shard_map.99.refs_0_), channel_id=1, source_target_pairs={{0,8},{8,0},{16,24},{24,16},{1,9},{9,1},{17,25},{25,17},{2,10},{10... | collective-permute-start | bytes 393224 | tf_op jit(solution)/shard_map/ppermute | solution.py:395
  23.2 1.5 %collective-permute-start.6 = (f32[16,8,256]{2,1,0:T(8,128)S(1)}, f32[16,8,256]{2,1,0:T(8,128)S(1)}, u32[]{:S(2)}, u32[]{:S(2)}) collective-permute-start(f32[16,8,256]{2,1,0:T(8,128)S(1)} %shard_map.99.refs_0_), channel_id=1, source_target_pairs={{0,16},{8,24},{16,0},{24,8},{1,17},{9,25},{17,1},{25,9},{2,18},{10... | collective-permute-start | bytes 393224 | tf_op jit(solution)/shard_map/ppermute | solution.py:395
  24.7 0.5 %collective-permute-start.5 = (f32[16,8,256]{2,1,0:T(8,128)S(1)}, f32[16,8,256]{2,1,0:T(8,128)S(1)}, u32[]{:S(2)}, u32[]{:S(2)}) collective-permute-start(f32[16,8,256]{2,1,0:T(8,128)S(1)} %shard_map.99.refs_0_), channel_id=1, source_target_pairs={{0,24},{8,16},{16,8},{24,0},{1,25},{9,17},{17,9},{25,1},{2,26},{10... | collective-permute-start | bytes 393224 | tf_op jit(solution)/shard_map/ppermute | solution.py:395
  25.2 0.5 %shard_map.98 = (f32[128,512]{1,0:T(8,128)S(1)}, f32[8,128]{1,0:T(8,128)S(1)}) custom-call(f32[256,512]{1,0:T(8,128)S(1)} %get-tuple-element.33.image_ref, f32[128,512]{1,0:T(8,128)S(1)} %get-tuple-element.32.own_ref, f32[128,512]{1,0:T(8,128)S(1)} %collective-permute-done.1.even_ref, f32[128,512]{1,0:T(8,128)S(1)} %collective-permute-done.2.odd_ref, ...), custom_call_target="tpu_custom_call" | custom-call | tf_op jit(solution)/shard_map/pallas_call | solution.py:488
  25.7 2.5 %collective-permute-start.10 = (f32[8,128]{1,0:T(8,128)S(1)}, f32[8,128]{1,0:T(8,128)S(1)}, u32[]{:S(2)}, u32[]{:S(2)}) collective-permute-start(f32[8,128]{1,0:T(8,128)S(1)} %get-tuple-element.37.refs_4_), channel_id=1, source_target_pairs={{0,24},{8,16},{16,8},{24,0},{1,25},{9,17},{17,9},{25,1},{2,26},{10... | collective-permute-start | bytes 12296 | tf_op jit(solution)/shard_map/ppermute | solution.py:395
  28.2 0.5 %collective-permute-start.9 = (f32[8,128]{1,0:T(8,128)S(1)}, f32[8,128]{1,0:T(8,128)S(1)}, u32[]{:S(2)}, u32[]{:S(2)}) collective-permute-start(f32[8,128]{1,0:T(8,128)S(1)} %get-tuple-element.37.refs_4_), channel_id=1, source_target_pairs={{0,16},{8,24},{16,0},{24,8},{1,17},{9,25},{17,1},{25,9},{2,18},{10... | collective-permute-start | bytes 12296 | tf_op jit(solution)/shard_map/ppermute | solution.py:395
  28.7 0.9 %collective-permute-start.8 = (f32[8,128]{1,0:T(8,128)S(1)}, f32[8,128]{1,0:T(8,128)S(1)}, u32[]{:S(2)}, u32[]{:S(2)}) collective-permute-start(f32[8,128]{1,0:T(8,128)S(1)} %get-tuple-element.37.refs_4_), channel_id=1, source_target_pairs={{0,8},{8,0},{16,24},{24,16},{1,9},{9,1},{17,25},{25,17},{2,10},{10... | collective-permute-start | bytes 12296 | tf_op jit(solution)/shard_map/ppermute | solution.py:395
  29.6 1.5 %collective-permute-done.6.refs_2_ = f32[16,8,256]{2,1,0:T(8,128)S(1)} collective-permute-done((f32[16,8,256]{2,1,0:T(8,128)S(1)}, f32[16,8,256]{2,1,0:T(8,128)S(1)}, u32[]{:S(2)}, u32[]{:S(2)}) %collective-permute-start.6) | collective-permute-done | bytes 131104 | tf_op jit(solution)/shard_map/ppermute | solution.py:395
  31.1 0.7 %collective-permute-done.9.refs_6_ = f32[8,128]{1,0:T(8,128)S(1)} collective-permute-done((f32[8,128]{1,0:T(8,128)S(1)}, f32[8,128]{1,0:T(8,128)S(1)}, u32[]{:S(2)}, u32[]{:S(2)}) %collective-permute-start.9) | collective-permute-done | bytes 4128 | tf_op jit(solution)/shard_map/ppermute | solution.py:395
  31.8 0.5 %collective-permute-done.8.refs_5_ = f32[8,128]{1,0:T(8,128)S(1)} collective-permute-done((f32[8,128]{1,0:T(8,128)S(1)}, f32[8,128]{1,0:T(8,128)S(1)}, u32[]{:S(2)}, u32[]{:S(2)}) %collective-permute-start.8) | collective-permute-done | bytes 4128 | tf_op jit(solution)/shard_map/ppermute | solution.py:395
  32.3 0.2 shard_map.100
  32.5 0.7 %collective-permute-start.11 = (f32[8,128]{1,0:T(8,128)S(1)}, f32[8,128]{1,0:T(8,128)S(1)}, u32[]{:S(2)}, u32[]{:S(2)}) collective-permute-start(f32[8,128]{1,0:T(8,128)S(1)} %get-tuple-element.38), channel_id=1, source_target_pairs={{0,2},{2,0},{4,6},{6,4},{1,3},{3,1},{5,7},{7,5},{8,10},{10,8},{12,... | collective-permute-start | bytes 12296 | tf_op jit(solution)/shard_map/ppermute | solution.py:395
  33.2 1.8 %shard_map.101 = (bf16[8,256,512]{2,1,0:T(8,128)(2,1)S(1)}, bf16[8,256,512]{2,1,0:T(8,128)(2,1)S(1)}) custom-call(f32[32,128]{1,0:T(8,128)S(1)} %get-tuple-element.24.phase_ref, f32[16,16,256]{2,1,0:T(8,128)S(1)} %get-tuple-element.25.row_weight_ref, bf16[16,256,256]{2,1,0:T(8,128)(2,1)S(1)} %get-tuple-element.26.whigh, ...), custom_call_target="tpu_custom_call" | custom-call | flops 1610612736 | tf_op jit(solution)/shard_map/pallas_call | solution.py:505
  35.0 1.2 %collective-permute-done.11 = f32[8,128]{1,0:T(8,128)S(1)} collective-permute-done((f32[8,128]{1,0:T(8,128)S(1)}, f32[8,128]{1,0:T(8,128)S(1)}, u32[]{:S(2)}, u32[]{:S(2)}) %collective-permute-start.11) | collective-permute-done | bytes 4128 | tf_op jit(solution)/shard_map/ppermute | solution.py:395
  36.2 1.5 %collective-permute-start.12 = (f32[8,128]{1,0:T(8,128)S(1)}, f32[8,128]{1,0:T(8,128)S(1)}, u32[]{:S(2)}, u32[]{:S(2)}) collective-permute-start(f32[8,128]{1,0:T(8,128)S(1)} %add.6.refs_0_), channel_id=1, source_target_pairs={{0,4},{2,6},{4,0},{6,2},{1,5},{3,7},{5,1},{7,3},{8,12},{10,14},{12... | collective-permute-start | bytes 12296 | tf_op jit(solution)/shard_map/ppermute | solution.py:395
  37.7 2.3 %shard_map.102.folded_ref = f32[256,512]{1,0:T(8,128)S(1)} custom-call(bf16[256,768]{1,0:T(8,128)(2,1)S(1)} %get-tuple-element.28.adj, bf16[8,256,512]{2,1,0:T(8,128)(2,1)S(1)} %get-tuple-element.29.coil, bf16[8,256,512]{2,1,0:T(8,128)(2,1)S(1)} %get-tuple-element.40.xhigh, bf16[8,256,512]{2,1,0:T(8,128)(2,1)S(1)} %get-tuple-element.41.xlow, ...), custom_call_target="tpu_custom_call" | custom-call | flops 1610612736 | tf_op jit(solution)/shard_map/pallas_call | solution.py:517
  40.0 0.7 %collective-permute-done.12 = f32[8,128]{1,0:T(8,128)S(1)} collective-permute-done((f32[8,128]{1,0:T(8,128)S(1)}, f32[8,128]{1,0:T(8,128)S(1)}, u32[]{:S(2)}, u32[]{:S(2)}) %collective-permute-start.12) | collective-permute-done | bytes 4128 | tf_op jit(solution)/shard_map/ppermute | solution.py:395
  40.7 0.3 shard_map.103
  41.1 0.1 collective-permute-start.13
  41.1 0.5 %collective-permute-start.14 = (f32[8,128]{1,0:T(8,128)S(1)}, f32[8,128]{1,0:T(8,128)S(1)}, u32[]{:S(2)}, u32[]{:S(2)}) collective-permute-start(f32[8,128]{1,0:T(8,128)S(1)} %add.7.after_ref.refs_2_), channel_id=1, source_target_pairs={{0,1},{1,0},{2,3},{3,2},{4,5},{5,4},{6,7},{7,6},{8,9},{9,8},{10,11... | collective-permute-start | bytes 12296 | tf_op jit(solution)/shard_map/ppermute | solution.py:405
  41.6 1.0 %collective-permute-done.14.refs_3_ = f32[8,128]{1,0:T(8,128)S(1)} collective-permute-done((f32[8,128]{1,0:T(8,128)S(1)}, f32[8,128]{1,0:T(8,128)S(1)}, u32[]{:S(2)}, u32[]{:S(2)}) %collective-permute-start.14) | collective-permute-done | bytes 4128 | tf_op jit(solution)/shard_map/ppermute | solution.py:405
  42.7 0.9 %shard_map.104 = (f32[128,512]{1,0:T(8,128)}, f32[128,512]{1,0:T(8,128)}) custom-call(f32[128,512]{1,0:T(8,128)S(1)} %get-tuple-element.32.own_ref, f32[128,512]{1,0:T(8,128)S(1)} %get-tuple-element.34.smooth_ref, f32[128,512]{1,0:T(8,128)S(1)} %get-tuple-element.42.refs_0_, f32[128,512]{1,0:T(8,128)S(1)} %collective-permute-done.13.refs_1_, ...), custom_call_target="tpu_custom_call" | custom-call | tf_op jit(solution)/shard_map/pallas_call | solution.py:541
  (10 shorter events, 0.0 us)
Async XLA Ops:
  7.9 6.7 %collective-permute-start = (f32[264,512]{1,0:T(8,128)S(1)}, f32[264,512]{1,0:T(8,128)S(1)}, u32[]{:S(2)}, u32[]{:S(2)}) collective-permute-start(f32[264,512]{1,0:T(8,128)S(1)} %shard_map.96.refs_0_), channel_id=1, source_target_pairs={{0,1},{1,0},{2,3},{3,2},{4,5},{5,4},{6,7},{7,6},{8,9},{9,8},{10,11... | collective-permute-start | bytes 1622024 | tf_op jit(solution)/shard_map/ppermute | solution.py:405
  8.5 14.8 %collective-permute-start.4 = (f32[128,256]{1,0:T(8,128)S(1)}, f32[128,256]{1,0:T(8,128)S(1)}, u32[]{:S(2)}, u32[]{:S(2)}) collective-permute-start(f32[128,256]{1,0:T(8,128)S(1)} %get-tuple-element.31.weight_ref), channel_id=1, source_target_pairs={{2,4},{4,2},{3,5},{5,3},{10,12},{12,10},{11,13},{13,11},{18,20},{2... | collective-permute-start | bytes 393224 | tf_op jit(solution)/shard_map/ppermute | solution.py:468
  9.1 15.6 %collective-permute-start.3 = (f32[128,256]{1,0:T(8,128)S(1)}, f32[128,256]{1,0:T(8,128)S(1)}, u32[]{:S(2)}, u32[]{:S(2)}) collective-permute-start(f32[128,256]{1,0:T(8,128)S(1)} %get-tuple-element.31.weight_ref), channel_id=1, source_target_pairs={{0,2},{2,0},{4,6},{6,4},{1,3},{3,1},{5,7},{7,5},{8,10},{10,8},{12,... | collective-permute-start | bytes 393224 | tf_op jit(solution)/shard_map/ppermute | solution.py:468
  15.0 10.3 %collective-permute-start.2 = (f32[128,512]{1,0:T(8,128)S(1)}, f32[128,512]{1,0:T(8,128)S(1)}, u32[]{:S(2)}, u32[]{:S(2)}) collective-permute-start(f32[128,512]{1,0:T(8,128)S(1)} %get-tuple-element.32.own_ref), channel_id=1, source_target_pairs={{2,4},{4,2},{3,5},{5,3},{10,12},{12,10},{11,13},{13,11},{18,20},{2... | collective-permute-start | bytes 786440 | tf_op jit(solution)/shard_map/ppermute | solution.py:475
  15.8 9.4 %collective-permute-start.1 = (f32[128,512]{1,0:T(8,128)S(1)}, f32[128,512]{1,0:T(8,128)S(1)}, u32[]{:S(2)}, u32[]{:S(2)}) collective-permute-start(f32[128,512]{1,0:T(8,128)S(1)} %get-tuple-element.32.own_ref), channel_id=1, source_target_pairs={{0,2},{2,0},{4,6},{6,4},{1,3},{3,1},{5,7},{7,5},{8,10},{10,8},{12,... | collective-permute-start | bytes 786440 | tf_op jit(solution)/shard_map/ppermute | solution.py:475
  21.6 7.1 %collective-permute-start.7 = (f32[16,8,256]{2,1,0:T(8,128)S(1)}, f32[16,8,256]{2,1,0:T(8,128)S(1)}, u32[]{:S(2)}, u32[]{:S(2)}) collective-permute-start(f32[16,8,256]{2,1,0:T(8,128)S(1)} %shard_map.99.refs_0_), channel_id=1, source_target_pairs={{0,8},{8,0},{16,24},{24,16},{1,9},{9,1},{17,25},{25,17},{2,10},{10... | collective-permute-start | bytes 393224 | tf_op jit(solution)/shard_map/ppermute | solution.py:395
  23.2 7.9 %collective-permute-start.6 = (f32[16,8,256]{2,1,0:T(8,128)S(1)}, f32[16,8,256]{2,1,0:T(8,128)S(1)}, u32[]{:S(2)}, u32[]{:S(2)}) collective-permute-start(f32[16,8,256]{2,1,0:T(8,128)S(1)} %shard_map.99.refs_0_), channel_id=1, source_target_pairs={{0,16},{8,24},{16,0},{24,8},{1,17},{9,25},{17,1},{25,9},{2,18},{10... | collective-permute-start | bytes 393224 | tf_op jit(solution)/shard_map/ppermute | solution.py:395
  24.7 6.4 %collective-permute-start.5 = (f32[16,8,256]{2,1,0:T(8,128)S(1)}, f32[16,8,256]{2,1,0:T(8,128)S(1)}, u32[]{:S(2)}, u32[]{:S(2)}) collective-permute-start(f32[16,8,256]{2,1,0:T(8,128)S(1)} %shard_map.99.refs_0_), channel_id=1, source_target_pairs={{0,24},{8,16},{16,8},{24,0},{1,25},{9,17},{17,9},{25,1},{2,26},{10... | collective-permute-start | bytes 393224 | tf_op jit(solution)/shard_map/ppermute | solution.py:395
  25.7 5.4 %collective-permute-start.10 = (f32[8,128]{1,0:T(8,128)S(1)}, f32[8,128]{1,0:T(8,128)S(1)}, u32[]{:S(2)}, u32[]{:S(2)}) collective-permute-start(f32[8,128]{1,0:T(8,128)S(1)} %get-tuple-element.37.refs_4_), channel_id=1, source_target_pairs={{0,24},{8,16},{16,8},{24,0},{1,25},{9,17},{17,9},{25,1},{2,26},{10... | collective-permute-start | bytes 12296 | tf_op jit(solution)/shard_map/ppermute | solution.py:395
  28.2 3.6 %collective-permute-start.9 = (f32[8,128]{1,0:T(8,128)S(1)}, f32[8,128]{1,0:T(8,128)S(1)}, u32[]{:S(2)}, u32[]{:S(2)}) collective-permute-start(f32[8,128]{1,0:T(8,128)S(1)} %get-tuple-element.37.refs_4_), channel_id=1, source_target_pairs={{0,16},{8,24},{16,0},{24,8},{1,17},{9,25},{17,1},{25,9},{2,18},{10... | collective-permute-start | bytes 12296 | tf_op jit(solution)/shard_map/ppermute | solution.py:395
  28.7 3.6 %collective-permute-start.8 = (f32[8,128]{1,0:T(8,128)S(1)}, f32[8,128]{1,0:T(8,128)S(1)}, u32[]{:S(2)}, u32[]{:S(2)}) collective-permute-start(f32[8,128]{1,0:T(8,128)S(1)} %get-tuple-element.37.refs_4_), channel_id=1, source_target_pairs={{0,8},{8,0},{16,24},{24,16},{1,9},{9,1},{17,25},{25,17},{2,10},{10... | collective-permute-start | bytes 12296 | tf_op jit(solution)/shard_map/ppermute | solution.py:395
  32.5 3.7 %collective-permute-start.11 = (f32[8,128]{1,0:T(8,128)S(1)}, f32[8,128]{1,0:T(8,128)S(1)}, u32[]{:S(2)}, u32[]{:S(2)}) collective-permute-start(f32[8,128]{1,0:T(8,128)S(1)} %get-tuple-element.38), channel_id=1, source_target_pairs={{0,2},{2,0},{4,6},{6,4},{1,3},{3,1},{5,7},{7,5},{8,10},{10,8},{12,... | collective-permute-start | bytes 12296 | tf_op jit(solution)/shard_map/ppermute | solution.py:395
  36.2 4.5 %collective-permute-start.12 = (f32[8,128]{1,0:T(8,128)S(1)}, f32[8,128]{1,0:T(8,128)S(1)}, u32[]{:S(2)}, u32[]{:S(2)}) collective-permute-start(f32[8,128]{1,0:T(8,128)S(1)} %add.6.refs_0_), channel_id=1, source_target_pairs={{0,4},{2,6},{4,0},{6,2},{1,5},{3,7},{5,1},{7,3},{8,12},{10,14},{12... | collective-permute-start | bytes 12296 | tf_op jit(solution)/shard_map/ppermute | solution.py:395
  41.1 1.6 %collective-permute-start.13 = (f32[128,512]{1,0:T(8,128)S(1)}, f32[128,512]{1,0:T(8,128)S(1)}, u32[]{:S(2)}, u32[]{:S(2)}) collective-permute-start(f32[128,512]{1,0:T(8,128)S(1)} %get-tuple-element.43), channel_id=1, source_target_pairs={{0,1},{1,0},{2,3},{3,2},{4,5},{5,4},{6,7},{7,6},{8,9},{9,8},{10,11... | collective-permute-start | bytes 786440 | tf_op jit(solution)/shard_map/ppermute | solution.py:395
  41.1 1.5 %collective-permute-start.14 = (f32[8,128]{1,0:T(8,128)S(1)}, f32[8,128]{1,0:T(8,128)S(1)}, u32[]{:S(2)}, u32[]{:S(2)}) collective-permute-start(f32[8,128]{1,0:T(8,128)S(1)} %add.7.after_ref.refs_2_), channel_id=1, source_target_pairs={{0,1},{1,0},{2,3},{3,2},{4,5},{5,4},{6,7},{7,6},{8,9},{9,8},{10,11... | collective-permute-start | bytes 12296 | tf_op jit(solution)/shard_map/ppermute | solution.py:405

commit v5 on v4

--- a/solution.py
+++ b/solution.py
@@ -87,22 +87,24 @@
     return matmul(order, high) + (matmul(order, rest) + matmul(order, low))
 
 
-def first_row(rows, columns):
-    return lax.broadcasted_iota(jnp.int32, (rows, columns), 0) == 0
+def with_first(first, values):
+    columns = values.shape[1]
+    edge = lax.broadcasted_iota(jnp.int32, (8, columns), 0) == 0
+    top = jnp.where(edge, first[:8], values[:8])
+    return jnp.concatenate([top, values[8:]], axis=0)
 
 
 def back_rows(adj, xhigh, xlow, coil, first, last):
     ny, nx = adj.shape[0], xhigh.shape[2] // 2
     half = ny // 2
-    edge = first_row(half, nx)
     sums = [None] * 4
     for c in range(first, last):
         high, low = xhigh[c], xlow[c]
         folded = matmul(adj[...], jnp.concatenate([high, high, low], axis=0))
         even_real, even_imag = folded[:half, :nx], folded[:half, nx:]
         odd_real, odd_imag = folded[half:, :nx], folded[half:, nx:]
-        lower = even_real - jnp.where(edge, 0.0, odd_imag), even_imag + jnp.where(edge, 0.0, odd_real)
-        upper = jnp.where(edge, odd_real, even_real + odd_imag), jnp.where(edge, odd_imag, even_imag - odd_real)
+        lower = with_first(even_real, even_real - odd_imag), with_first(even_imag, even_imag + odd_real)
+        upper = with_first(odd_real, even_real + odd_imag), with_first(odd_imag, even_imag - odd_real)
         for i, (real, imag) in enumerate((lower, upper)):
             here = slice(i * half, (i + 1) * half)
             coil_real = coil[c, here, :nx].astype(f32)
@@ -174,11 +176,12 @@
         row_weight_ref[k] = row_weight
         for i, part in enumerate(quarter_turn(cycle_ref[0], k)):
             phase_ref[2 * k + i : 2 * k + i + 1, :] = jnp.full((1, sb), part, f32)
-    for fetch in fetches[-3:]:
+    for fetch in fetches[-3:-1]:
         fetch.wait()
     order = mirror(half)
     for c in range(coils):
         coil[c, half:, :] = matmul(order, upper[c]).astype(bf16)
+    fetches[-1].wait()
 
 
 def rhs_kernel(
@@ -222,7 +225,6 @@
     half = ny // 2
     ty = row_weight_ref.shape[1]
     sb = row_weight_ref.shape[2] // 2
-    edge = first_row(half, nx)
     for c in range(coils):
         products = []
         for i in range(2):
@@ -233,14 +235,8 @@
             products.append(coil_real * image_real - coil_imag * image_imag)
             products.append(coil_real * image_imag + coil_imag * image_real)
         lower_real, lower_imag, upper_real, upper_imag = products
-        even = [
-            lower_real + jnp.where(edge, 0.0, upper_real),
-            lower_imag + jnp.where(edge, 0.0, upper_imag),
-        ]
-        odd = [
-            jnp.where(edge, upper_real, lower_imag - upper_imag),
-            jnp.where(edge, upper_imag, upper_real - lower_real),
-        ]
+        even = [with_first(lower_real, lower_real + upper_real), with_first(lower_imag, lower_imag + upper_imag)]
+        odd = [with_first(upper_real, lower_imag - upper_imag), with_first(upper_imag, upper_real - lower_real)]
         folded = jnp.concatenate([jnp.concatenate(even, axis=1), jnp.concatenate(odd, axis=1)], axis=0)
         high, low = split(folded)
         grid = matmul(fwd[...], jnp.concatenate([high, high, low], axis=0))
@@ -298,16 +294,17 @@
         out_ref[here, :] = rows + refs[0][here, :] if first else rows
 
 
-def cut_kernel(after_ref, folded_ref, *refs):
+def cut_kernel(count, sums_ref, folded_ref, *refs):
     *out_refs, whole = refs
     total = whole.shape[0]
     half = total // 2
     whole[:half, :] = folded_ref[:half, :]
     whole[half:, :] = mirrored(folded_ref[half:, :])
     for shift, out_ref in enumerate(out_refs):
-        count = out_ref.shape[0]
         start = lax.rem(lax.axis_index("row") + shift, total // count) * count
-        out_ref[...] = whole[pl.ds(pl.multiple_of(start, count), count), :]
+        out_ref[:count, :] = whole[pl.ds(pl.multiple_of(start, count), count), :]
+        if out_ref.shape[0] > count:
+            out_ref[count:, :] = jnp.concatenate([sums_ref[...]] * (whole.shape[1] // sums_ref.shape[1]), axis=1)
 
 
 def neighbours(image_ref, weight, before_ref, after_ref):
@@ -336,7 +333,10 @@
     before_ref, after_ref, out_ref, sums_ref,
 ):
     nx = image_ref.shape[1] // 2
-    weight, weight_even, weight_odd = weight_ref[...], weight_even_ref[...], weight_odd_ref[...]
+    weight, weight_even = weight_ref[...], weight_even_ref[...]
+    group = lax.axis_index("grp")
+    inside = jnp.logical_and(group > 0, group < lax.axis_size("grp") - 1)
+    weight_odd = jnp.where(inside, weight_odd_ref[...], 0.0)
     weight_up, weight_down, image_up, image_down, column, above, below = neighbours(
         image_ref, weight, before_ref, after_ref
     )
@@ -363,14 +363,18 @@
 
 def update_kernel(images, own_ref, smooth_ref, *refs):
     image_refs, sums_refs, (field_ref, residual_ref) = refs[:images], refs[images:-2], refs[-2:]
+    count = smooth_ref.shape[0]
     sums = sums_refs[0][0:1, :]
     for ref in sums_refs[1:]:
         sums = sums + ref[0:1, :]
+    for ref in image_refs:
+        if ref.shape[0] > count:
+            sums = sums + ref[count : count + 1, : sums.shape[1]]
     alpha = sums[:, 0:1] / sums[:, 1:2]
     here = own_ref[...]
     image = smooth_ref[...]
     for ref in image_refs:
-        image = image + ref[...]
+        image = image + ref[:count, :]
     field_ref[...] = alpha * here
     residual_ref[...] = here - alpha * image
 
@@ -462,17 +466,22 @@
 
     received = from_others(partial, "row")
     even_pairs = [(i, i ^ 1) for i in range(groups) if i ^ 1 < groups]
-    odd_pairs = []
-    for i in range(1, groups - 1, 2):
-        odd_pairs += [(i, i + 1), (i + 1, i)]
-    weights = [lax.ppermute(weight, "grp", pairs) for pairs in (even_pairs, odd_pairs)]
+    ends = (0, groups - 1)
+    beyond = [group if group in ends else ((group - 1) ^ 1) + 1 for group in range(groups)]
+    odd_pairs = [
+        (group * rows + row, beyond[group] * rows + ((row + 1) % rows if group in ends else row))
+        for group in range(groups)
+        for row in range(rows)
+    ]
+    beside = (("grp", even_pairs), (("grp", "row"), odd_pairs))
+    weights = [lax.ppermute(weight, axes, pairs) for axes, pairs in beside]
     folded, image, mine = call(
         functools.partial(sum_kernel, ny),
         [shape((ny, width)), shape((ny, width)), shape((count, width))],
         [VMEM] * (1 + len(received)),
         [VMEM] * 3,
     )(partial, *received)
-    others = [lax.ppermute(mine, "grp", pairs) for pairs in (even_pairs, odd_pairs)]
+    others = [lax.ppermute(mine, axes, pairs) for axes, pairs in beside]
 
     predicted = call(
         functools.partial(predict_kernel, coils, blocks),
@@ -526,18 +535,20 @@
 
     unfinished = add_rows(0, coils, sums)
     sums = sums + exchange(sums, "grp", steps[-1])
+    cuts = [(count, width), (count + sums.shape[0], width)] if rows == 2 else [(ny, width)]
     halves = call(
-        cut_kernel,
-        [shape((count, width))] * 2 if rows == 2 else [shape((ny, width))],
+        functools.partial(cut_kernel, count if rows == 2 else ny),
+        [shape(cut) for cut in cuts],
         [VMEM] * 2,
-        [VMEM] * (2 if rows == 2 else 1),
+        [VMEM] * len(cuts),
         [pltpu.VMEM((ny, width), f32)],
     )(sums, unfinished)
     if rows == 2:
         images = [halves[0], exchange(halves[1], "row", 1)]
+        all_sums = [sums]
     else:
         images = [lax.psum_scatter(halves[0], "row", scatter_dimension=0, tiled=True)]
-    all_sums = [sums, *from_others(sums, "row")]
+        all_sums = [sums, *from_others(sums, "row")]
     solution_field, residual = call(
         functools.partial(update_kernel, len(images)),
         [shape((count, width))] * 2,

time: 43.8 us -> 41.3 us (0.943)
  starting transfers between devices: 19.5 us -> 16.4 us
    ppermute x4, starting transfers between devices: 8.77 us -> 6.3 us  [the longest x2 4.24 us: on_device(): weights = [lax.ppermute(weight, axes, pairs) for axes, pairs in beside]]
    ppermute x9, waiting for transfers between devices: 4.61 us -> 6.03 us  [exchange(): lax.ppermute(values, axis, [(i, i ^ step) for i in range(lax.axis_size(ax...]
    ppermute x2 -> x1, waiting for transfers between devices: 1.03 us -> 0.01 us  [from_others(): lax.ppermute(values, axis, [(i, (i + shift) % count) for i in range(count)])]
    ppermute x2 -> x1, starting transfers between devices: 1.01 us -> 0.51 us  [from_others(): lax.ppermute(values, axis, [(i, (i + shift) % count) for i in range(count)])]
  transfers between devices with their start and end apart: 15 -> 14, of which waited for: 6 -> 6; matrix products, arithmetic and copies ran while one was open for 0% -> 0% of each run, Pallas kernels for 21% -> 22%
where the time goes in v5:
time: 41.3 us; the launch traced here: 41.1 us
  Pallas kernels  17.3 us (42%)
  starting transfers between devices  16.4 us (40%)
  waiting for transfers between devices  6.04 us (15%)
  between operations  1.38 us (3%)
    ppermute x9, starting transfers between devices, exchange(): lax.ppermute(values, axis, [(i, i ^ step) for i in range(lax.axis_size(ax...  9.63 us
    ppermute x9, waiting for transfers between devices, exchange(): lax.ppermute(values, axis, [(i, i ^ step) for i in range(lax.axis_size(ax...  6.03 us
    ppermute x2, starting transfers between devices, on_device(): weights = [lax.ppermute(weight, axes, pairs) for axes, pairs in beside]  4.24 us
    pallas_call x1, Pallas kernels, on_device(): call(functools.partial(rhs_kernel, coils, blocks), shape((ny + 8, width))...  4.18 us
    pallas_call x1, Pallas kernels, on_device(): call(functools.partial(predict_kernel, coils, blocks), shape((blocks, coi...  4.04 us
    pallas_call x1, Pallas kernels, on_device(): call(functools.partial(tables_kernel, coils, blocks), [pltpu.VMEM(w_shape...  2.46 us
    pallas_call x1, Pallas kernels, add_rows(): call(functools.partial(rows_kernel, first, last), shape((ny, width)), [VM...  2.3 us
    ppermute x2, starting transfers between devices, on_device(): others = [lax.ppermute(mine, axes, pairs) for axes, pairs in beside]  2.05 us
  transfers between devices with their start and end apart: 14, of which 6 were waited for; matrix products, arithmetic and copies ran while one was open for 0% of the time, Pallas kernels for 22%

profile of v5, /device:TPU:0, one launch (start us, length us, event | category | flops | bytes accessed | tf_op | source)
XLA Modules:
  0.0 41.1 jit_solution(15947515359577756880)
XLA Ops:
  1.3 2.5 %shard_map.95 = (bf16[16,256,256]{2,1,0:T(8,128)(2,1)S(1)}, bf16[16,256,256]{2,1,0:T(8,128)(2,1)S(1)}, bf16[256,768]{1,0:T(8,128)(2,1)S(1)}, bf16[256,768]{1,0:T...) custom-call(s32[1]{0:T(128)S(6)} %copy.10.cycle_ref, ...), custom_call_target="tpu_custom_call" | custom-call | flops 1610612736 | tf_op jit(solution)/shard_map/pallas_call | solution.py:435
  3.7 4.2 %shard_map.96.refs_0_ = f32[264,512]{1,0:T(8,128)S(1)} custom-call(f32[32,128]{1,0:T(8,128)S(1)} %get-tuple-element.24.phase_ref, f32[16,16,256]{2,1,0:T(8,128)S(1)} %get-tuple-element.25.row_weight_ref, bf16[16,256,256]{2,1,0:T(8,128)(2,1)S(1)} %get-tuple-element.26.whigh, bf16[16,256,256]{2,1,0:T(8,128)(2,1)S(1)} %get-tuple-element.27.wlow, ...), custom_call_target="tpu_custom_call" | custom-call | flops 3221225472 | tf_op jit(solution)/shard_map/pallas_call | solution.py:457
  7.9 0.5 %collective-permute-start = (f32[264,512]{1,0:T(8,128)S(1)}, f32[264,512]{1,0:T(8,128)S(1)}, u32[]{:S(2)}, u32[]{:S(2)}) collective-permute-start(f32[264,512]{1,0:T(8,128)S(1)} %shard_map.96.refs_0_), channel_id=1, source_target_pairs={{0,1},{1,0},{2,3},{3,2},{4,5},{5,4},{6,7},{7,6},{8,9},{9,8},{10,11... | collective-permute-start | bytes 1622024 | tf_op jit(solution)/shard_map/ppermute | solution.py:409
  8.4 0.1 collective-permute-start.4
  8.5 4.2 %collective-permute-start.3 = (f32[128,256]{1,0:T(8,128)S(1)}, f32[128,256]{1,0:T(8,128)S(1)}, u32[]{:S(2)}, u32[]{:S(2)}) collective-permute-start(f32[128,256]{1,0:T(8,128)S(1)} %get-tuple-element.31.weight_ref), channel_id=1, source_target_pairs={{0,2},{2,0},{4,6},{6,4},{1,3},{3,1},{5,7},{7,5},{8,10},{10,8},{12,... | collective-permute-start | bytes 393224 | tf_op jit(solution)/shard_map/ppermute | solution.py:477
  12.7 0.3 shard_map.97
  13.0 0.1 collective-permute-start.2
  13.1 2.0 %collective-permute-start.1 = (f32[128,512]{1,0:T(8,128)S(1)}, f32[128,512]{1,0:T(8,128)S(1)}, u32[]{:S(2)}, u32[]{:S(2)}) collective-permute-start(f32[128,512]{1,0:T(8,128)S(1)} %get-tuple-element.32.own_ref), channel_id=1, source_target_pairs={{0,2},{2,0},{4,6},{6,4},{1,3},{3,1},{5,7},{7,5},{8,10},{10,8},{12,... | collective-permute-start | bytes 786440 | tf_op jit(solution)/shard_map/ppermute | solution.py:484
  15.1 4.0 %shard_map.99.refs_0_ = f32[16,8,256]{2,1,0:T(8,128)S(1)} custom-call(f32[32,128]{1,0:T(8,128)S(1)} %get-tuple-element.24.phase_ref, f32[16,16,256]{2,1,0:T(8,128)S(1)} %get-tuple-element.25.row_weight_ref, f32[256,512]{1,0:T(8,128)S(1)} %get-tuple-element.35.image_ref, bf16[256,768]{1,0:T(8,128)(2,1)S(1)} %get-tuple-element.36.fwd, ...), custom_call_target="tpu_custom_call" | custom-call | flops 3221225472 | tf_op jit(solution)/shard_map/pallas_call | solution.py:486
  19.1 1.6 %collective-permute-start.7 = (f32[16,8,256]{2,1,0:T(8,128)S(1)}, f32[16,8,256]{2,1,0:T(8,128)S(1)}, u32[]{:S(2)}, u32[]{:S(2)}) collective-permute-start(f32[16,8,256]{2,1,0:T(8,128)S(1)} %shard_map.99.refs_0_), channel_id=1, source_target_pairs={{0,8},{8,0},{16,24},{24,16},{1,9},{9,1},{17,25},{25,17},{2,10},{10... | collective-permute-start | bytes 393224 | tf_op jit(solution)/shard_map/ppermute | solution.py:399
  20.7 0.0 collective-permute-done.4.weight_odd_ref
  20.7 1.5 %collective-permute-start.6 = (f32[16,8,256]{2,1,0:T(8,128)S(1)}, f32[16,8,256]{2,1,0:T(8,128)S(1)}, u32[]{:S(2)}, u32[]{:S(2)}) collective-permute-start(f32[16,8,256]{2,1,0:T(8,128)S(1)} %shard_map.99.refs_0_), channel_id=1, source_target_pairs={{0,16},{8,24},{16,0},{24,8},{1,17},{9,25},{17,1},{25,9},{2,18},{10... | collective-permute-start | bytes 393224 | tf_op jit(solution)/shard_map/ppermute | solution.py:399
  22.2 0.5 %collective-permute-start.5 = (f32[16,8,256]{2,1,0:T(8,128)S(1)}, f32[16,8,256]{2,1,0:T(8,128)S(1)}, u32[]{:S(2)}, u32[]{:S(2)}) collective-permute-start(f32[16,8,256]{2,1,0:T(8,128)S(1)} %shard_map.99.refs_0_), channel_id=1, source_target_pairs={{0,24},{8,16},{16,8},{24,0},{1,25},{9,17},{17,9},{25,1},{2,26},{10... | collective-permute-start | bytes 393224 | tf_op jit(solution)/shard_map/ppermute | solution.py:399
  22.7 0.0 collective-permute-done.1.even_ref
  22.7 0.5 %shard_map.98 = (f32[128,512]{1,0:T(8,128)S(1)}, f32[8,128]{1,0:T(8,128)S(1)}) custom-call(f32[256,512]{1,0:T(8,128)S(1)} %get-tuple-element.33.image_ref, f32[128,512]{1,0:T(8,128)S(1)} %get-tuple-element.32.own_ref, f32[128,512]{1,0:T(8,128)S(1)} %collective-permute-done.1.even_ref, f32[128,512]{1,0:T(8,128)S(1)} %collective-permute-done.2.odd_ref, ...), custom_call_target="tpu_custom_call" | custom-call | tf_op jit(solution)/shard_map/pallas_call | solution.py:497
  23.2 2.5 %collective-permute-start.10 = (f32[8,128]{1,0:T(8,128)S(1)}, f32[8,128]{1,0:T(8,128)S(1)}, u32[]{:S(2)}, u32[]{:S(2)}) collective-permute-start(f32[8,128]{1,0:T(8,128)S(1)} %get-tuple-element.37.refs_4_), channel_id=1, source_target_pairs={{0,24},{8,16},{16,8},{24,0},{1,25},{9,17},{17,9},{25,1},{2,26},{10... | collective-permute-start | bytes 12296 | tf_op jit(solution)/shard_map/ppermute | solution.py:399
  25.7 0.5 %collective-permute-start.9 = (f32[8,128]{1,0:T(8,128)S(1)}, f32[8,128]{1,0:T(8,128)S(1)}, u32[]{:S(2)}, u32[]{:S(2)}) collective-permute-start(f32[8,128]{1,0:T(8,128)S(1)} %get-tuple-element.37.refs_4_), channel_id=1, source_target_pairs={{0,16},{8,24},{16,0},{24,8},{1,17},{9,25},{17,1},{25,9},{2,18},{10... | collective-permute-start | bytes 12296 | tf_op jit(solution)/shard_map/ppermute | solution.py:399
  26.2 0.7 %collective-permute-start.8 = (f32[8,128]{1,0:T(8,128)S(1)}, f32[8,128]{1,0:T(8,128)S(1)}, u32[]{:S(2)}, u32[]{:S(2)}) collective-permute-start(f32[8,128]{1,0:T(8,128)S(1)} %get-tuple-element.37.refs_4_), channel_id=1, source_target_pairs={{0,8},{8,0},{16,24},{24,16},{1,9},{9,1},{17,25},{25,17},{2,10},{10... | collective-permute-start | bytes 12296 | tf_op jit(solution)/shard_map/ppermute | solution.py:399
  27.0 1.6 %collective-permute-done.6.refs_2_ = f32[16,8,256]{2,1,0:T(8,128)S(1)} collective-permute-done((f32[16,8,256]{2,1,0:T(8,128)S(1)}, f32[16,8,256]{2,1,0:T(8,128)S(1)}, u32[]{:S(2)}, u32[]{:S(2)}) %collective-permute-start.6) | collective-permute-done | bytes 131104 | tf_op jit(solution)/shard_map/ppermute | solution.py:399
  28.6 0.7 %collective-permute-done.9.refs_6_ = f32[8,128]{1,0:T(8,128)S(1)} collective-permute-done((f32[8,128]{1,0:T(8,128)S(1)}, f32[8,128]{1,0:T(8,128)S(1)}, u32[]{:S(2)}, u32[]{:S(2)}) %collective-permute-start.9) | collective-permute-done | bytes 4128 | tf_op jit(solution)/shard_map/ppermute | solution.py:399
  29.3 0.5 %collective-permute-done.8.refs_5_ = f32[8,128]{1,0:T(8,128)S(1)} collective-permute-done((f32[8,128]{1,0:T(8,128)S(1)}, f32[8,128]{1,0:T(8,128)S(1)}, u32[]{:S(2)}, u32[]{:S(2)}) %collective-permute-start.8) | collective-permute-done | bytes 4128 | tf_op jit(solution)/shard_map/ppermute | solution.py:399
  29.8 0.2 shard_map.100
  30.0 1.2 %collective-permute-start.11 = (f32[8,128]{1,0:T(8,128)S(1)}, f32[8,128]{1,0:T(8,128)S(1)}, u32[]{:S(2)}, u32[]{:S(2)}) collective-permute-start(f32[8,128]{1,0:T(8,128)S(1)} %get-tuple-element.38), channel_id=1, source_target_pairs={{0,2},{2,0},{4,6},{6,4},{1,3},{3,1},{5,7},{7,5},{8,10},{10,8},{12,... | collective-permute-start | bytes 12296 | tf_op jit(solution)/shard_map/ppermute | solution.py:399
  31.2 2.0 %shard_map.101 = (bf16[8,256,512]{2,1,0:T(8,128)(2,1)S(1)}, bf16[8,256,512]{2,1,0:T(8,128)(2,1)S(1)}) custom-call(f32[32,128]{1,0:T(8,128)S(1)} %get-tuple-element.24.phase_ref, f32[16,16,256]{2,1,0:T(8,128)S(1)} %get-tuple-element.25.row_weight_ref, bf16[16,256,256]{2,1,0:T(8,128)(2,1)S(1)} %get-tuple-element.26.whigh, ...), custom_call_target="tpu_custom_call" | custom-call | flops 1610612736 | tf_op jit(solution)/shard_map/pallas_call | solution.py:514
  33.2 0.5 %collective-permute-done.11 = f32[8,128]{1,0:T(8,128)S(1)} collective-permute-done((f32[8,128]{1,0:T(8,128)S(1)}, f32[8,128]{1,0:T(8,128)S(1)}, u32[]{:S(2)}, u32[]{:S(2)}) %collective-permute-start.11) | collective-permute-done | bytes 4128 | tf_op jit(solution)/shard_map/ppermute | solution.py:399
  33.7 1.0 %collective-permute-start.12 = (f32[8,128]{1,0:T(8,128)S(1)}, f32[8,128]{1,0:T(8,128)S(1)}, u32[]{:S(2)}, u32[]{:S(2)}) collective-permute-start(f32[8,128]{1,0:T(8,128)S(1)} %add.6.refs_0_), channel_id=1, source_target_pairs={{0,4},{2,6},{4,0},{6,2},{1,5},{3,7},{5,1},{7,3},{8,12},{10,14},{12... | collective-permute-start | bytes 12296 | tf_op jit(solution)/shard_map/ppermute | solution.py:399
  34.7 2.3 %shard_map.102.folded_ref = f32[256,512]{1,0:T(8,128)S(1)} custom-call(bf16[256,768]{1,0:T(8,128)(2,1)S(1)} %get-tuple-element.28.adj, bf16[8,256,512]{2,1,0:T(8,128)(2,1)S(1)} %get-tuple-element.29.coil, bf16[8,256,512]{2,1,0:T(8,128)(2,1)S(1)} %get-tuple-element.40.xhigh, bf16[8,256,512]{2,1,0:T(8,128)(2,1)S(1)} %get-tuple-element.41.xlow, ...), custom_call_target="tpu_custom_call" | custom-call | flops 1610612736 | tf_op jit(solution)/shard_map/pallas_call | solution.py:526
  37.0 1.2 %collective-permute-done.12 = f32[8,128]{1,0:T(8,128)S(1)} collective-permute-done((f32[8,128]{1,0:T(8,128)S(1)}, f32[8,128]{1,0:T(8,128)S(1)}, u32[]{:S(2)}, u32[]{:S(2)}) %collective-permute-start.12) | collective-permute-done | bytes 4128 | tf_op jit(solution)/shard_map/ppermute | solution.py:399
  38.2 0.3 shard_map.103
  38.6 0.1 collective-permute-start.13
  38.6 1.5 %collective-permute-done.13.refs_1_ = f32[136,512]{1,0:T(8,128)S(1)} collective-permute-done((f32[136,512]{1,0:T(8,128)S(1)}, f32[136,512]{1,0:T(8,128)S(1)}, u32[]{:S(2)}, u32[]{:S(2)}) %collective-permute-start.13) | collective-permute-done | bytes 278560 | tf_op jit(solution)/shard_map/ppermute | solution.py:399
  40.2 0.9 %shard_map.104 = (f32[128,512]{1,0:T(8,128)}, f32[128,512]{1,0:T(8,128)}) custom-call(f32[128,512]{1,0:T(8,128)S(1)} %get-tuple-element.32.own_ref, f32[128,512]{1,0:T(8,128)S(1)} %get-tuple-element.34.smooth_ref, f32[128,512]{1,0:T(8,128)S(1)} %get-tuple-element.42.refs_0_, f32[136,512]{1,0:T(8,128)S(1)} %collective-permute-done.13.refs_1_, ...), custom_call_target="tpu_custom_call" | custom-call | tf_op jit(solution)/shard_map/pallas_call | solution.py:552
  (8 shorter events, 0.0 us)
Async XLA Ops:
  7.9 4.8 %collective-permute-start = (f32[264,512]{1,0:T(8,128)S(1)}, f32[264,512]{1,0:T(8,128)S(1)}, u32[]{:S(2)}, u32[]{:S(2)}) collective-permute-start(f32[264,512]{1,0:T(8,128)S(1)} %shard_map.96.refs_0_), channel_id=1, source_target_pairs={{0,1},{1,0},{2,3},{3,2},{4,5},{5,4},{6,7},{7,6},{8,9},{9,8},{10,11... | collective-permute-start | bytes 1622024 | tf_op jit(solution)/shard_map/ppermute | solution.py:409
  8.4 12.3 %collective-permute-start.4 = (f32[128,256]{1,0:T(8,128)S(1)}, f32[128,256]{1,0:T(8,128)S(1)}, u32[]{:S(2)}, u32[]{:S(2)}) collective-permute-start(f32[128,256]{1,0:T(8,128)S(1)} %get-tuple-element.31.weight_ref), channel_id=1, source_target_pairs={{0,1},{1,0},{2,4},{3,5},{4,2},{5,3},{6,7},{7,6},{8,9},{9,8},{10,12... | collective-permute-start | bytes 393224 | tf_op jit(solution)/shard_map/ppermute | solution.py:477
  8.5 13.7 %collective-permute-start.3 = (f32[128,256]{1,0:T(8,128)S(1)}, f32[128,256]{1,0:T(8,128)S(1)}, u32[]{:S(2)}, u32[]{:S(2)}) collective-permute-start(f32[128,256]{1,0:T(8,128)S(1)} %get-tuple-element.31.weight_ref), channel_id=1, source_target_pairs={{0,2},{2,0},{4,6},{6,4},{1,3},{3,1},{5,7},{7,5},{8,10},{10,8},{12,... | collective-permute-start | bytes 393224 | tf_op jit(solution)/shard_map/ppermute | solution.py:477
  13.0 9.7 %collective-permute-start.2 = (f32[128,512]{1,0:T(8,128)S(1)}, f32[128,512]{1,0:T(8,128)S(1)}, u32[]{:S(2)}, u32[]{:S(2)}) collective-permute-start(f32[128,512]{1,0:T(8,128)S(1)} %get-tuple-element.32.own_ref), channel_id=1, source_target_pairs={{0,1},{1,0},{2,4},{3,5},{4,2},{5,3},{6,7},{7,6},{8,9},{9,8},{10,12... | collective-permute-start | bytes 786440 | tf_op jit(solution)/shard_map/ppermute | solution.py:484
  13.1 9.6 %collective-permute-start.1 = (f32[128,512]{1,0:T(8,128)S(1)}, f32[128,512]{1,0:T(8,128)S(1)}, u32[]{:S(2)}, u32[]{:S(2)}) collective-permute-start(f32[128,512]{1,0:T(8,128)S(1)} %get-tuple-element.32.own_ref), channel_id=1, source_target_pairs={{0,2},{2,0},{4,6},{6,4},{1,3},{3,1},{5,7},{7,5},{8,10},{10,8},{12,... | collective-permute-start | bytes 786440 | tf_op jit(solution)/shard_map/ppermute | solution.py:484
  19.1 7.1 %collective-permute-start.7 = (f32[16,8,256]{2,1,0:T(8,128)S(1)}, f32[16,8,256]{2,1,0:T(8,128)S(1)}, u32[]{:S(2)}, u32[]{:S(2)}) collective-permute-start(f32[16,8,256]{2,1,0:T(8,128)S(1)} %shard_map.99.refs_0_), channel_id=1, source_target_pairs={{0,8},{8,0},{16,24},{24,16},{1,9},{9,1},{17,25},{25,17},{2,10},{10... | collective-permute-start | bytes 393224 | tf_op jit(solution)/shard_map/ppermute | solution.py:399
  20.7 7.9 %collective-permute-start.6 = (f32[16,8,256]{2,1,0:T(8,128)S(1)}, f32[16,8,256]{2,1,0:T(8,128)S(1)}, u32[]{:S(2)}, u32[]{:S(2)}) collective-permute-start(f32[16,8,256]{2,1,0:T(8,128)S(1)} %shard_map.99.refs_0_), channel_id=1, source_target_pairs={{0,16},{8,24},{16,0},{24,8},{1,17},{9,25},{17,1},{25,9},{2,18},{10... | collective-permute-start | bytes 393224 | tf_op jit(solution)/shard_map/ppermute | solution.py:399
  22.2 6.4 %collective-permute-start.5 = (f32[16,8,256]{2,1,0:T(8,128)S(1)}, f32[16,8,256]{2,1,0:T(8,128)S(1)}, u32[]{:S(2)}, u32[]{:S(2)}) collective-permute-start(f32[16,8,256]{2,1,0:T(8,128)S(1)} %shard_map.99.refs_0_), channel_id=1, source_target_pairs={{0,24},{8,16},{16,8},{24,0},{1,25},{9,17},{17,9},{25,1},{2,26},{10... | collective-permute-start | bytes 393224 | tf_op jit(solution)/shard_map/ppermute | solution.py:399
  23.2 5.4 %collective-permute-start.10 = (f32[8,128]{1,0:T(8,128)S(1)}, f32[8,128]{1,0:T(8,128)S(1)}, u32[]{:S(2)}, u32[]{:S(2)}) collective-permute-start(f32[8,128]{1,0:T(8,128)S(1)} %get-tuple-element.37.refs_4_), channel_id=1, source_target_pairs={{0,24},{8,16},{16,8},{24,0},{1,25},{9,17},{17,9},{25,1},{2,26},{10... | collective-permute-start | bytes 12296 | tf_op jit(solution)/shard_map/ppermute | solution.py:399
  25.7 3.6 %collective-permute-start.9 = (f32[8,128]{1,0:T(8,128)S(1)}, f32[8,128]{1,0:T(8,128)S(1)}, u32[]{:S(2)}, u32[]{:S(2)}) collective-permute-start(f32[8,128]{1,0:T(8,128)S(1)} %get-tuple-element.37.refs_4_), channel_id=1, source_target_pairs={{0,16},{8,24},{16,0},{24,8},{1,17},{9,25},{17,1},{25,9},{2,18},{10... | collective-permute-start | bytes 12296 | tf_op jit(solution)/shard_map/ppermute | solution.py:399
  26.2 3.6 %collective-permute-start.8 = (f32[8,128]{1,0:T(8,128)S(1)}, f32[8,128]{1,0:T(8,128)S(1)}, u32[]{:S(2)}, u32[]{:S(2)}) collective-permute-start(f32[8,128]{1,0:T(8,128)S(1)} %get-tuple-element.37.refs_4_), channel_id=1, source_target_pairs={{0,8},{8,0},{16,24},{24,16},{1,9},{9,1},{17,25},{25,17},{2,10},{10... | collective-permute-start | bytes 12296 | tf_op jit(solution)/shard_map/ppermute | solution.py:399
  30.0 3.7 %collective-permute-start.11 = (f32[8,128]{1,0:T(8,128)S(1)}, f32[8,128]{1,0:T(8,128)S(1)}, u32[]{:S(2)}, u32[]{:S(2)}) collective-permute-start(f32[8,128]{1,0:T(8,128)S(1)} %get-tuple-element.38), channel_id=1, source_target_pairs={{0,2},{2,0},{4,6},{6,4},{1,3},{3,1},{5,7},{7,5},{8,10},{10,8},{12,... | collective-permute-start | bytes 12296 | tf_op jit(solution)/shard_map/ppermute | solution.py:399
  33.7 4.5 %collective-permute-start.12 = (f32[8,128]{1,0:T(8,128)S(1)}, f32[8,128]{1,0:T(8,128)S(1)}, u32[]{:S(2)}, u32[]{:S(2)}) collective-permute-start(f32[8,128]{1,0:T(8,128)S(1)} %add.6.refs_0_), channel_id=1, source_target_pairs={{0,4},{2,6},{4,0},{6,2},{1,5},{3,7},{5,1},{7,3},{8,12},{10,14},{12... | collective-permute-start | bytes 12296 | tf_op jit(solution)/shard_map/ppermute | solution.py:399
  38.6 1.6 %collective-permute-start.13 = (f32[136,512]{1,0:T(8,128)S(1)}, f32[136,512]{1,0:T(8,128)S(1)}, u32[]{:S(2)}, u32[]{:S(2)}) collective-permute-start(f32[136,512]{1,0:T(8,128)S(1)} %get-tuple-element.43), channel_id=1, source_target_pairs={{0,1},{1,0},{2,3},{3,2},{4,5},{5,4},{6,7},{7,6},{8,9},{9,8},{10,11... | collective-permute-start | bytes 835592 | tf_op jit(solution)/shard_map/ppermute | solution.py:399

commit v6 on v5

--- a/solution.py
+++ b/solution.py
@@ -262,18 +262,15 @@
         out_ref[k] = jnp.concatenate([cosine * real - sine * imag, sine * real + cosine * imag], axis=1)
 
 
-def collapse_kernel(bands, *refs):
-    parts, sums_refs, (out_ref, out_sums_ref) = refs[:bands], refs[bands:-2], refs[-2:]
+def collapse_kernel(*refs):
+    parts, (out_ref, sums_ref) = refs[:-2], refs[-2:]
     total = parts[0][...]
     for part in parts[1:]:
         total = total + part[...]
     out_ref[...] = total
-    sums = sums_refs[0][...]
-    for ref in sums_refs[1:]:
-        sums = sums + ref[...]
-    lane = lax.broadcasted_iota(jnp.int32, sums.shape, 1)
+    lane = lax.broadcasted_iota(jnp.int32, sums_ref.shape, 1)
     squares = jnp.sum(jnp.sum(total * total, axis=0))
-    out_sums_ref[...] = jnp.where(lane == 1, sums + squares, sums)
+    sums_ref[...] = jnp.where(lane == 1, squares, 0.0)
 
 
 def spread_kernel(coils, blocks, phase_ref, row_weight_ref, whigh, wlow, collapsed_ref, xhigh, xlow):
@@ -501,15 +498,18 @@
         [VMEM, VMEM],
     )(image, mine, *others, weight, *weights, received[0], received[-1])
     sums = [sums, *[exchange(sums, "band", step) for step in range(1, lax.axis_size("band"))]]
-    collapsed, sums = call(
-        functools.partial(collapse_kernel, len(predicted)),
+    collapsed, squares = call(
+        collapse_kernel,
         [shape(predicted[0].shape), shape((8, 128))],
-        [VMEM] * (len(predicted) + len(sums)),
+        [VMEM] * len(predicted),
         [VMEM, VMEM],
-    )(*predicted, *sums)
+    )(*predicted)
+    sums = sum(sums)
     steps = powers("grp")
     for step in steps[:-1]:
+        squares = squares + exchange(squares, "grp", step)
         sums = sums + exchange(sums, "grp", step)
+    sums = sums + squares
 
     kept = call(
         functools.partial(spread_kernel, coils, blocks),

time: 41.3 us -> 41 us (level)
  waiting for transfers between devices: 6.04 us -> 2.81 us
  starting transfers between devices: 16.4 us -> 19.4 us
    ppermute x9 -> x10, starting transfers between devices: 9.63 us -> 13 us  [exchange(): lax.ppermute(values, axis, [(i, i ^ step) for i in range(lax.axis_size(ax...]
    ppermute x9 -> x10, waiting for transfers between devices: 6.03 us -> 2.8 us  [exchange(): lax.ppermute(values, axis, [(i, i ^ step) for i in range(lax.axis_size(ax...]
    ppermute x2, starting transfers between devices: 4.24 us -> 2.82 us  [on_device(): weights = [lax.ppermute(weight, axes, pairs) for axes, pairs in beside]]
    ppermute x2, starting transfers between devices: 2.05 us -> 3.06 us  [on_device(): others = [lax.ppermute(mine, axes, pairs) for axes, pairs in beside]]
  transfers between devices with their start and end apart: 14 -> 15, of which waited for: 6 -> 5; matrix products, arithmetic and copies ran while one was open for 0% -> 0% of each run, Pallas kernels for 22% -> 23%
where the time goes in v6:
time: 41 us; the launch traced here: 40.9 us
  starting transfers between devices  19.4 us (47%)
  Pallas kernels  17.3 us (42%)
  waiting for transfers between devices  2.81 us (7%)
  between operations  1.4 us (3%)
    ppermute x10, starting transfers between devices, exchange(): lax.ppermute(values, axis, [(i, i ^ step) for i in range(lax.axis_size(ax...  13 us
    pallas_call x1, Pallas kernels, on_device(): call(functools.partial(rhs_kernel, coils, blocks), shape((ny + 8, width))...  4.17 us
    pallas_call x1, Pallas kernels, on_device(): call(functools.partial(predict_kernel, coils, blocks), shape((blocks, coi...  4.04 us
    ppermute x2, starting transfers between devices, on_device(): others = [lax.ppermute(mine, axes, pairs) for axes, pairs in beside]  3.06 us
    ppermute x2, starting transfers between devices, on_device(): weights = [lax.ppermute(weight, axes, pairs) for axes, pairs in beside]  2.82 us
    ppermute x10, waiting for transfers between devices, exchange(): lax.ppermute(values, axis, [(i, i ^ step) for i in range(lax.axis_size(ax...  2.8 us
    pallas_call x1, Pallas kernels, on_device(): call(functools.partial(tables_kernel, coils, blocks), [pltpu.VMEM(w_shape...  2.46 us
    pallas_call x1, Pallas kernels, add_rows(): call(functools.partial(rows_kernel, first, last), shape((ny, width)), [VM...  2.31 us
  transfers between devices with their start and end apart: 15, of which 5 were waited for; matrix products, arithmetic and copies ran while one was open for 0% of the time, Pallas kernels for 23%

profile of v6, /device:TPU:0, one launch (start us, length us, event | category | flops | bytes accessed | tf_op | source)
XLA Modules:
  0.0 40.9 jit_solution(12639986197332766985)
XLA Ops:
  1.3 2.5 %shard_map.95 = (bf16[16,256,256]{2,1,0:T(8,128)(2,1)S(1)}, bf16[16,256,256]{2,1,0:T(8,128)(2,1)S(1)}, bf16[256,768]{1,0:T(8,128)(2,1)S(1)}, bf16[256,768]{1,0:T...) custom-call(s32[1]{0:T(128)S(6)} %copy.10.cycle_ref, ...), custom_call_target="tpu_custom_call" | custom-call | flops 1610612736 | tf_op jit(solution)/shard_map/pallas_call | solution.py:432
  3.7 4.2 %shard_map.96.refs_0_ = f32[264,512]{1,0:T(8,128)S(1)} custom-call(f32[32,128]{1,0:T(8,128)S(1)} %get-tuple-element.24.phase_ref, f32[16,16,256]{2,1,0:T(8,128)S(1)} %get-tuple-element.25.row_weight_ref, bf16[16,256,256]{2,1,0:T(8,128)(2,1)S(1)} %get-tuple-element.26.whigh, bf16[16,256,256]{2,1,0:T(8,128)(2,1)S(1)} %get-tuple-element.27.wlow, ...), custom_call_target="tpu_custom_call" | custom-call | flops 3221225472 | tf_op jit(solution)/shard_map/pallas_call | solution.py:454
  7.9 0.5 %collective-permute-start = (f32[264,512]{1,0:T(8,128)S(1)}, f32[264,512]{1,0:T(8,128)S(1)}, u32[]{:S(2)}, u32[]{:S(2)}) collective-permute-start(f32[264,512]{1,0:T(8,128)S(1)} %shard_map.96.refs_0_), channel_id=1, source_target_pairs={{0,1},{1,0},{2,3},{3,2},{4,5},{5,4},{6,7},{7,6},{8,9},{9,8},{10,11... | collective-permute-start | bytes 1622024 | tf_op jit(solution)/shard_map/ppermute | solution.py:406
  8.4 2.7 %collective-permute-start.3 = (f32[128,256]{1,0:T(8,128)S(1)}, f32[128,256]{1,0:T(8,128)S(1)}, u32[]{:S(2)}, u32[]{:S(2)}) collective-permute-start(f32[128,256]{1,0:T(8,128)S(1)} %get-tuple-element.31.weight_ref), channel_id=1, source_target_pairs={{0,2},{2,0},{4,6},{6,4},{1,3},{3,1},{5,7},{7,5},{8,10},{10,8},{12,... | collective-permute-start | bytes 393224 | tf_op jit(solution)/shard_map/ppermute | solution.py:474
  11.1 0.2 collective-permute-start.4
  11.3 0.0 collective-permute-done.refs_1_.before_ref.after_ref
  11.3 0.3 shard_map.97
  11.6 3.1 %collective-permute-start.1 = (f32[128,512]{1,0:T(8,128)S(1)}, f32[128,512]{1,0:T(8,128)S(1)}, u32[]{:S(2)}, u32[]{:S(2)}) collective-permute-start(f32[128,512]{1,0:T(8,128)S(1)} %get-tuple-element.32.own_ref), channel_id=1, source_target_pairs={{0,2},{2,0},{4,6},{6,4},{1,3},{3,1},{5,7},{7,5},{8,10},{10,8},{12,... | collective-permute-start | bytes 786440 | tf_op jit(solution)/shard_map/ppermute | solution.py:481
  14.7 4.0 %shard_map.99.refs_0_ = f32[16,8,256]{2,1,0:T(8,128)S(1)} custom-call(f32[32,128]{1,0:T(8,128)S(1)} %get-tuple-element.24.phase_ref, f32[16,16,256]{2,1,0:T(8,128)S(1)} %get-tuple-element.25.row_weight_ref, f32[256,512]{1,0:T(8,128)S(1)} %get-tuple-element.36.image_ref, bf16[256,768]{1,0:T(8,128)(2,1)S(1)} %get-tuple-element.37.fwd, ...), custom_call_target="tpu_custom_call" | custom-call | flops 3221225472 | tf_op jit(solution)/shard_map/pallas_call | solution.py:483
  18.7 2.5 %collective-permute-start.9 = (f32[16,8,256]{2,1,0:T(8,128)S(1)}, f32[16,8,256]{2,1,0:T(8,128)S(1)}, u32[]{:S(2)}, u32[]{:S(2)}) collective-permute-start(f32[16,8,256]{2,1,0:T(8,128)S(1)} %shard_map.99.refs_0_), channel_id=1, source_target_pairs={{0,24},{8,16},{16,8},{24,0},{1,25},{9,17},{17,9},{25,1},{2,26},{10... | collective-permute-start | bytes 393224 | tf_op jit(solution)/shard_map/ppermute | solution.py:396
  21.2 0.0 collective-permute-done.3.weight_even_ref
  21.2 0.5 %collective-permute-start.10 = (f32[16,8,256]{2,1,0:T(8,128)S(1)}, f32[16,8,256]{2,1,0:T(8,128)S(1)}, u32[]{:S(2)}, u32[]{:S(2)}) collective-permute-start(f32[16,8,256]{2,1,0:T(8,128)S(1)} %shard_map.99.refs_0_), channel_id=1, source_target_pairs={{0,16},{8,24},{16,0},{24,8},{1,17},{9,25},{17,1},{25,9},{2,18},{10... | collective-permute-start | bytes 393224 | tf_op jit(solution)/shard_map/ppermute | solution.py:396
  21.7 0.0 collective-permute-done.4.weight_odd_ref
  21.7 0.5 %collective-permute-start.11 = (f32[16,8,256]{2,1,0:T(8,128)S(1)}, f32[16,8,256]{2,1,0:T(8,128)S(1)}, u32[]{:S(2)}, u32[]{:S(2)}) collective-permute-start(f32[16,8,256]{2,1,0:T(8,128)S(1)} %shard_map.99.refs_0_), channel_id=1, source_target_pairs={{0,8},{8,0},{16,24},{24,16},{1,9},{9,1},{17,25},{25,17},{2,10},{10... | collective-permute-start | bytes 393224 | tf_op jit(solution)/shard_map/ppermute | solution.py:396
  22.3 0.5 %shard_map.98 = (f32[128,512]{1,0:T(8,128)S(1)}, f32[8,128]{1,0:T(8,128)S(1)}) custom-call(f32[256,512]{1,0:T(8,128)S(1)} %get-tuple-element.33.image_ref, f32[128,512]{1,0:T(8,128)S(1)} %get-tuple-element.32.own_ref, f32[128,512]{1,0:T(8,128)S(1)} %collective-permute-done.1.even_ref, f32[128,512]{1,0:T(8,128)S(1)} %collective-permute-done.2.odd_ref, ...), custom_call_target="tpu_custom_call" | custom-call | tf_op jit(solution)/shard_map/pallas_call | solution.py:494
  22.8 2.5 %collective-permute-start.7 = (f32[8,128]{1,0:T(8,128)S(1)}, f32[8,128]{1,0:T(8,128)S(1)}, u32[]{:S(2)}, u32[]{:S(2)}) collective-permute-start(f32[8,128]{1,0:T(8,128)S(1)} %get-tuple-element.35), channel_id=1, source_target_pairs={{0,24},{8,16},{16,8},{24,0},{1,25},{9,17},{17,9},{25,1},{2,26},{10... | collective-permute-start | bytes 12296 | tf_op jit(solution)/shard_map/ppermute | solution.py:396
  25.3 0.5 %collective-permute-start.6 = (f32[8,128]{1,0:T(8,128)S(1)}, f32[8,128]{1,0:T(8,128)S(1)}, u32[]{:S(2)}, u32[]{:S(2)}) collective-permute-start(f32[8,128]{1,0:T(8,128)S(1)} %get-tuple-element.35), channel_id=1, source_target_pairs={{0,16},{8,24},{16,0},{24,8},{1,17},{9,25},{17,1},{25,9},{2,18},{10... | collective-permute-start | bytes 12296 | tf_op jit(solution)/shard_map/ppermute | solution.py:396
  25.8 0.1 collective-permute-done.9.refs_1_
  25.9 1.6 %collective-permute-start.5 = (f32[8,128]{1,0:T(8,128)S(1)}, f32[8,128]{1,0:T(8,128)S(1)}, u32[]{:S(2)}, u32[]{:S(2)}) collective-permute-start(f32[8,128]{1,0:T(8,128)S(1)} %get-tuple-element.35), channel_id=1, source_target_pairs={{0,8},{8,0},{16,24},{24,16},{1,9},{9,1},{17,25},{25,17},{2,10},{10... | collective-permute-start | bytes 12296 | tf_op jit(solution)/shard_map/ppermute | solution.py:396
  27.5 1.0 %collective-permute-done.10.refs_2_ = f32[16,8,256]{2,1,0:T(8,128)S(1)} collective-permute-done((f32[16,8,256]{2,1,0:T(8,128)S(1)}, f32[16,8,256]{2,1,0:T(8,128)S(1)}, u32[]{:S(2)}, u32[]{:S(2)}) %collective-permute-start.10) | collective-permute-done | bytes 131104 | tf_op jit(solution)/shard_map/ppermute | solution.py:396
  28.5 0.1 collective-permute-done.11.refs_3_
  28.6 0.2 shard_map.100
  28.8 0.9 %collective-permute-start.12 = (f32[8,128]{1,0:T(8,128)S(1)}, f32[8,128]{1,0:T(8,128)S(1)}, u32[]{:S(2)}, u32[]{:S(2)}) collective-permute-start(f32[8,128]{1,0:T(8,128)S(1)} %get-tuple-element.38), channel_id=1, source_target_pairs={{0,2},{2,0},{4,6},{6,4},{1,3},{3,1},{5,7},{7,5},{8,10},{10,8},{12,... | collective-permute-start | bytes 12296 | tf_op jit(solution)/shard_map/ppermute | solution.py:396
  29.7 1.6 %collective-permute-start.8 = (f32[8,128]{1,0:T(8,128)S(1)}, f32[8,128]{1,0:T(8,128)S(1)}, u32[]{:S(2)}, u32[]{:S(2)}) collective-permute-start(f32[8,128]{1,0:T(8,128)S(1)} %add_add_fusion.1), channel_id=1, source_target_pairs={{0,2},{2,0},{4,6},{6,4},{1,3},{3,1},{5,7},{7,5},{8,10},{10,8},{12,... | collective-permute-start | bytes 12296 | tf_op jit(solution)/shard_map/ppermute | solution.py:396
  31.3 2.0 %shard_map.101 = (bf16[8,256,512]{2,1,0:T(8,128)(2,1)S(1)}, bf16[8,256,512]{2,1,0:T(8,128)(2,1)S(1)}) custom-call(f32[32,128]{1,0:T(8,128)S(1)} %get-tuple-element.24.phase_ref, f32[16,16,256]{2,1,0:T(8,128)S(1)} %get-tuple-element.25.row_weight_ref, bf16[16,256,256]{2,1,0:T(8,128)(2,1)S(1)} %get-tuple-element.26.whigh, ...), custom_call_target="tpu_custom_call" | custom-call | flops 1610612736 | tf_op jit(solution)/shard_map/pallas_call | solution.py:514
  33.3 0.1 collective-permute-done.8
  33.4 2.2 %collective-permute-start.13 = (f32[8,128]{1,0:T(8,128)S(1)}, f32[8,128]{1,0:T(8,128)S(1)}, u32[]{:S(2)}, u32[]{:S(2)}) collective-permute-start(f32[8,128]{1,0:T(8,128)S(1)} %add_add_fusion.refs_0_), channel_id=1, source_target_pairs={{0,4},{2,6},{4,0},{6,2},{1,5},{3,7},{5,1},{7,3},{8,12},{10,14},{12... | collective-permute-start | bytes 12296 | tf_op jit(solution)/shard_map/ppermute | solution.py:396
  35.6 2.3 %shard_map.102.folded_ref = f32[256,512]{1,0:T(8,128)S(1)} custom-call(bf16[256,768]{1,0:T(8,128)(2,1)S(1)} %get-tuple-element.28.adj, bf16[8,256,512]{2,1,0:T(8,128)(2,1)S(1)} %get-tuple-element.29.coil, bf16[8,256,512]{2,1,0:T(8,128)(2,1)S(1)} %get-tuple-element.40.xhigh, bf16[8,256,512]{2,1,0:T(8,128)(2,1)S(1)} %get-tuple-element.41.xlow, ...), custom_call_target="tpu_custom_call" | custom-call | flops 1610612736 | tf_op jit(solution)/shard_map/pallas_call | solution.py:526
  38.0 0.3 shard_map.103
  38.3 0.1 collective-permute-start.14
  38.4 1.5 %collective-permute-done.14.refs_1_ = f32[136,512]{1,0:T(8,128)S(1)} collective-permute-done((f32[136,512]{1,0:T(8,128)S(1)}, f32[136,512]{1,0:T(8,128)S(1)}, u32[]{:S(2)}, u32[]{:S(2)}) %collective-permute-start.14) | collective-permute-done | bytes 278560 | tf_op jit(solution)/shard_map/ppermute | solution.py:396
  39.9 0.9 %shard_map.104 = (f32[128,512]{1,0:T(8,128)}, f32[128,512]{1,0:T(8,128)}) custom-call(f32[128,512]{1,0:T(8,128)S(1)} %get-tuple-element.32.own_ref, f32[128,512]{1,0:T(8,128)S(1)} %get-tuple-element.34.smooth_ref, f32[128,512]{1,0:T(8,128)S(1)} %get-tuple-element.42.refs_0_, f32[136,512]{1,0:T(8,128)S(1)} %collective-permute-done.14.refs_1_, ...), custom_call_target="tpu_custom_call" | custom-call | tf_op jit(solution)/shard_map/pallas_call | solution.py:552
  (11 shorter events, 0.0 us)
Async XLA Ops:
  7.9 3.3 %collective-permute-start = (f32[264,512]{1,0:T(8,128)S(1)}, f32[264,512]{1,0:T(8,128)S(1)}, u32[]{:S(2)}, u32[]{:S(2)}) collective-permute-start(f32[264,512]{1,0:T(8,128)S(1)} %shard_map.96.refs_0_), channel_id=1, source_target_pairs={{0,1},{1,0},{2,3},{3,2},{4,5},{5,4},{6,7},{7,6},{8,9},{9,8},{10,11... | collective-permute-start | bytes 1622024 | tf_op jit(solution)/shard_map/ppermute | solution.py:406
  8.4 12.8 %collective-permute-start.3 = (f32[128,256]{1,0:T(8,128)S(1)}, f32[128,256]{1,0:T(8,128)S(1)}, u32[]{:S(2)}, u32[]{:S(2)}) collective-permute-start(f32[128,256]{1,0:T(8,128)S(1)} %get-tuple-element.31.weight_ref), channel_id=1, source_target_pairs={{0,2},{2,0},{4,6},{6,4},{1,3},{3,1},{5,7},{7,5},{8,10},{10,8},{12,... | collective-permute-start | bytes 393224 | tf_op jit(solution)/shard_map/ppermute | solution.py:474
  11.1 10.6 %collective-permute-start.4 = (f32[128,256]{1,0:T(8,128)S(1)}, f32[128,256]{1,0:T(8,128)S(1)}, u32[]{:S(2)}, u32[]{:S(2)}) collective-permute-start(f32[128,256]{1,0:T(8,128)S(1)} %get-tuple-element.31.weight_ref), channel_id=1, source_target_pairs={{0,1},{1,0},{2,4},{3,5},{4,2},{5,3},{6,7},{7,6},{8,9},{9,8},{10,12... | collective-permute-start | bytes 393224 | tf_op jit(solution)/shard_map/ppermute | solution.py:474
  11.6 10.7 %collective-permute-start.1 = (f32[128,512]{1,0:T(8,128)S(1)}, f32[128,512]{1,0:T(8,128)S(1)}, u32[]{:S(2)}, u32[]{:S(2)}) collective-permute-start(f32[128,512]{1,0:T(8,128)S(1)} %get-tuple-element.32.own_ref), channel_id=1, source_target_pairs={{0,2},{2,0},{4,6},{6,4},{1,3},{3,1},{5,7},{7,5},{8,10},{10,8},{12,... | collective-permute-start | bytes 786440 | tf_op jit(solution)/shard_map/ppermute | solution.py:481
  14.7 7.6 %collective-permute-start.2 = (f32[128,512]{1,0:T(8,128)S(1)}, f32[128,512]{1,0:T(8,128)S(1)}, u32[]{:S(2)}, u32[]{:S(2)}) collective-permute-start(f32[128,512]{1,0:T(8,128)S(1)} %get-tuple-element.32.own_ref), channel_id=1, source_target_pairs={{0,1},{1,0},{2,4},{3,5},{4,2},{5,3},{6,7},{7,6},{8,9},{9,8},{10,12... | collective-permute-start | bytes 786440 | tf_op jit(solution)/shard_map/ppermute | solution.py:481
  18.7 7.2 %collective-permute-start.9 = (f32[16,8,256]{2,1,0:T(8,128)S(1)}, f32[16,8,256]{2,1,0:T(8,128)S(1)}, u32[]{:S(2)}, u32[]{:S(2)}) collective-permute-start(f32[16,8,256]{2,1,0:T(8,128)S(1)} %shard_map.99.refs_0_), channel_id=1, source_target_pairs={{0,24},{8,16},{16,8},{24,0},{1,25},{9,17},{17,9},{25,1},{2,26},{10... | collective-permute-start | bytes 393224 | tf_op jit(solution)/shard_map/ppermute | solution.py:396
  21.2 7.3 %collective-permute-start.10 = (f32[16,8,256]{2,1,0:T(8,128)S(1)}, f32[16,8,256]{2,1,0:T(8,128)S(1)}, u32[]{:S(2)}, u32[]{:S(2)}) collective-permute-start(f32[16,8,256]{2,1,0:T(8,128)S(1)} %shard_map.99.refs_0_), channel_id=1, source_target_pairs={{0,16},{8,24},{16,0},{24,8},{1,17},{9,25},{17,1},{25,9},{2,18},{10... | collective-permute-start | bytes 393224 | tf_op jit(solution)/shard_map/ppermute | solution.py:396
  21.7 6.8 %collective-permute-start.11 = (f32[16,8,256]{2,1,0:T(8,128)S(1)}, f32[16,8,256]{2,1,0:T(8,128)S(1)}, u32[]{:S(2)}, u32[]{:S(2)}) collective-permute-start(f32[16,8,256]{2,1,0:T(8,128)S(1)} %shard_map.99.refs_0_), channel_id=1, source_target_pairs={{0,8},{8,0},{16,24},{24,16},{1,9},{9,1},{17,25},{25,17},{2,10},{10... | collective-permute-start | bytes 393224 | tf_op jit(solution)/shard_map/ppermute | solution.py:396
  22.8 6.9 %collective-permute-start.7 = (f32[8,128]{1,0:T(8,128)S(1)}, f32[8,128]{1,0:T(8,128)S(1)}, u32[]{:S(2)}, u32[]{:S(2)}) collective-permute-start(f32[8,128]{1,0:T(8,128)S(1)} %get-tuple-element.35), channel_id=1, source_target_pairs={{0,24},{8,16},{16,8},{24,0},{1,25},{9,17},{17,9},{25,1},{2,26},{10... | collective-permute-start | bytes 12296 | tf_op jit(solution)/shard_map/ppermute | solution.py:396
  25.3 4.4 %collective-permute-start.6 = (f32[8,128]{1,0:T(8,128)S(1)}, f32[8,128]{1,0:T(8,128)S(1)}, u32[]{:S(2)}, u32[]{:S(2)}) collective-permute-start(f32[8,128]{1,0:T(8,128)S(1)} %get-tuple-element.35), channel_id=1, source_target_pairs={{0,16},{8,24},{16,0},{24,8},{1,17},{9,25},{17,1},{25,9},{2,18},{10... | collective-permute-start | bytes 12296 | tf_op jit(solution)/shard_map/ppermute | solution.py:396
  25.9 3.8 %collective-permute-start.5 = (f32[8,128]{1,0:T(8,128)S(1)}, f32[8,128]{1,0:T(8,128)S(1)}, u32[]{:S(2)}, u32[]{:S(2)}) collective-permute-start(f32[8,128]{1,0:T(8,128)S(1)} %get-tuple-element.35), channel_id=1, source_target_pairs={{0,8},{8,0},{16,24},{24,16},{1,9},{9,1},{17,25},{25,17},{2,10},{10... | collective-permute-start | bytes 12296 | tf_op jit(solution)/shard_map/ppermute | solution.py:396
  28.8 4.5 %collective-permute-start.12 = (f32[8,128]{1,0:T(8,128)S(1)}, f32[8,128]{1,0:T(8,128)S(1)}, u32[]{:S(2)}, u32[]{:S(2)}) collective-permute-start(f32[8,128]{1,0:T(8,128)S(1)} %get-tuple-element.38), channel_id=1, source_target_pairs={{0,2},{2,0},{4,6},{6,4},{1,3},{3,1},{5,7},{7,5},{8,10},{10,8},{12,... | collective-permute-start | bytes 12296 | tf_op jit(solution)/shard_map/ppermute | solution.py:396
  29.7 3.7 %collective-permute-start.8 = (f32[8,128]{1,0:T(8,128)S(1)}, f32[8,128]{1,0:T(8,128)S(1)}, u32[]{:S(2)}, u32[]{:S(2)}) collective-permute-start(f32[8,128]{1,0:T(8,128)S(1)} %add_add_fusion.1), channel_id=1, source_target_pairs={{0,2},{2,0},{4,6},{6,4},{1,3},{3,1},{5,7},{7,5},{8,10},{10,8},{12,... | collective-permute-start | bytes 12296 | tf_op jit(solution)/shard_map/ppermute | solution.py:396
  33.4 4.5 %collective-permute-start.13 = (f32[8,128]{1,0:T(8,128)S(1)}, f32[8,128]{1,0:T(8,128)S(1)}, u32[]{:S(2)}, u32[]{:S(2)}) collective-permute-start(f32[8,128]{1,0:T(8,128)S(1)} %add_add_fusion.refs_0_), channel_id=1, source_target_pairs={{0,4},{2,6},{4,0},{6,2},{1,5},{3,7},{5,1},{7,3},{8,12},{10,14},{12... | collective-permute-start | bytes 12296 | tf_op jit(solution)/shard_map/ppermute | solution.py:396
  38.3 1.6 %collective-permute-start.14 = (f32[136,512]{1,0:T(8,128)S(1)}, f32[136,512]{1,0:T(8,128)S(1)}, u32[]{:S(2)}, u32[]{:S(2)}) collective-permute-start(f32[136,512]{1,0:T(8,128)S(1)} %get-tuple-element.43), channel_id=1, source_target_pairs={{0,1},{1,0},{2,3},{3,2},{4,5},{5,4},{6,7},{7,6},{8,9},{9,8},{10,11... | collective-permute-start | bytes 835592 | tf_op jit(solution)/shard_map/ppermute | solution.py:396

commit v7 on v6

--- a/solution.py
+++ b/solution.py
@@ -326,7 +326,7 @@
 
 
 def smooth_kernel(
-    image_ref, own_ref, even_ref, odd_ref, weight_ref, weight_even_ref, weight_odd_ref,
+    image_ref, own_ref, odd_ref, even_ref, weight_ref, weight_odd_ref, weight_even_ref,
     before_ref, after_ref, out_ref, sums_ref,
 ):
     nx = image_ref.shape[1] // 2
@@ -496,7 +496,7 @@
         [shape((count, width)), shape((8, 128))],
         [VMEM] * 9,
         [VMEM, VMEM],
-    )(image, mine, *others, weight, *weights, received[0], received[-1])
+    )(image, mine, *others[::-1], weight, *weights[::-1], received[0], received[-1])
     sums = [sums, *[exchange(sums, "band", step) for step in range(1, lax.axis_size("band"))]]
     collapsed, squares = call(
         collapse_kernel,

time: 41 us -> 41.1 us (level)
  waiting for transfers between devices: 2.81 us -> 4.06 us
  starting transfers between devices: 19.4 us -> 18.2 us
    ppermute x10, starting transfers between devices: 13 us -> 11.4 us  [exchange(): lax.ppermute(values, axis, [(i, i ^ step) for i in range(lax.axis_size(ax...]
    ppermute x2, starting transfers between devices: 2.82 us -> 4.24 us  [on_device(): weights = [lax.ppermute(weight, axes, pairs) for axes, pairs in beside]]
    ppermute x10, waiting for transfers between devices: 2.8 us -> 4.04 us  [exchange(): lax.ppermute(values, axis, [(i, i ^ step) for i in range(lax.axis_size(ax...]
    ppermute x2, starting transfers between devices: 3.06 us -> 2.05 us  [on_device(): others = [lax.ppermute(mine, axes, pairs) for axes, pairs in beside]]
where the time goes in v7:
time: 41.1 us; the launch traced here: 40.9 us
  starting transfers between devices  18.2 us (44%)
  Pallas kernels  17.3 us (42%)
  waiting for transfers between devices  4.06 us (10%)
  between operations  1.39 us (3%)
    ppermute x10, starting transfers between devices, exchange(): lax.ppermute(values, axis, [(i, i ^ step) for i in range(lax.axis_size(ax...  11.4 us
    ppermute x2, starting transfers between devices, on_device(): weights = [lax.ppermute(weight, axes, pairs) for axes, pairs in beside]  4.24 us
    pallas_call x1, Pallas kernels, on_device(): call(functools.partial(rhs_kernel, coils, blocks), shape((ny + 8, width))...  4.18 us
    pallas_call x1, Pallas kernels, on_device(): call(functools.partial(predict_kernel, coils, blocks), shape((blocks, coi...  4.04 us
    ppermute x10, waiting for transfers between devices, exchange(): lax.ppermute(values, axis, [(i, i ^ step) for i in range(lax.axis_size(ax...  4.04 us
    pallas_call x1, Pallas kernels, on_device(): call(functools.partial(tables_kernel, coils, blocks), [pltpu.VMEM(w_shape...  2.46 us
    pallas_call x1, Pallas kernels, add_rows(): call(functools.partial(rows_kernel, first, last), shape((ny, width)), [VM...  2.3 us
    ppermute x2, starting transfers between devices, on_device(): others = [lax.ppermute(mine, axes, pairs) for axes, pairs in beside]  2.05 us
  transfers between devices with their start and end apart: 15, of which 5 were waited for; matrix products, arithmetic and copies ran while one was open for 0% of the time, Pallas kernels for 23%

profile of v7, /device:TPU:0, one launch (start us, length us, event | category | flops | bytes accessed | tf_op | source)
XLA Modules:
  0.0 40.9 jit_solution(1874453728975810251)
XLA Ops:
  1.3 2.5 %shard_map.95 = (bf16[16,256,256]{2,1,0:T(8,128)(2,1)S(1)}, bf16[16,256,256]{2,1,0:T(8,128)(2,1)S(1)}, bf16[256,768]{1,0:T(8,128)(2,1)S(1)}, bf16[256,768]{1,0:T...) custom-call(s32[1]{0:T(128)S(6)} %copy.10.cycle_ref, ...), custom_call_target="tpu_custom_call" | custom-call | flops 1610612736 | tf_op jit(solution)/shard_map/pallas_call | solution.py:432
  3.7 4.2 %shard_map.96.refs_0_ = f32[264,512]{1,0:T(8,128)S(1)} custom-call(f32[32,128]{1,0:T(8,128)S(1)} %get-tuple-element.24.phase_ref, f32[16,16,256]{2,1,0:T(8,128)S(1)} %get-tuple-element.25.row_weight_ref, bf16[16,256,256]{2,1,0:T(8,128)(2,1)S(1)} %get-tuple-element.26.whigh, bf16[16,256,256]{2,1,0:T(8,128)(2,1)S(1)} %get-tuple-element.27.wlow, ...), custom_call_target="tpu_custom_call" | custom-call | flops 3221225472 | tf_op jit(solution)/shard_map/pallas_call | solution.py:454
  7.9 0.5 %collective-permute-start = (f32[264,512]{1,0:T(8,128)S(1)}, f32[264,512]{1,0:T(8,128)S(1)}, u32[]{:S(2)}, u32[]{:S(2)}) collective-permute-start(f32[264,512]{1,0:T(8,128)S(1)} %shard_map.96.refs_0_), channel_id=1, source_target_pairs={{0,1},{1,0},{2,3},{3,2},{4,5},{5,4},{6,7},{7,6},{8,9},{9,8},{10,11... | collective-permute-start | bytes 1622024 | tf_op jit(solution)/shard_map/ppermute | solution.py:406
  8.4 0.1 collective-permute-start.3
  8.5 4.2 %collective-permute-start.4 = (f32[128,256]{1,0:T(8,128)S(1)}, f32[128,256]{1,0:T(8,128)S(1)}, u32[]{:S(2)}, u32[]{:S(2)}) collective-permute-start(f32[128,256]{1,0:T(8,128)S(1)} %get-tuple-element.31.weight_ref), channel_id=1, source_target_pairs={{0,2},{2,0},{4,6},{6,4},{1,3},{3,1},{5,7},{7,5},{8,10},{10,8},{12,... | collective-permute-start | bytes 393224 | tf_op jit(solution)/shard_map/ppermute | solution.py:474
  12.7 0.3 shard_map.97
  13.0 0.1 collective-permute-start.1
  13.1 2.0 %collective-permute-start.2 = (f32[128,512]{1,0:T(8,128)S(1)}, f32[128,512]{1,0:T(8,128)S(1)}, u32[]{:S(2)}, u32[]{:S(2)}) collective-permute-start(f32[128,512]{1,0:T(8,128)S(1)} %get-tuple-element.32.own_ref), channel_id=1, source_target_pairs={{0,2},{2,0},{4,6},{6,4},{1,3},{3,1},{5,7},{7,5},{8,10},{10,8},{12,... | collective-permute-start | bytes 786440 | tf_op jit(solution)/shard_map/ppermute | solution.py:481
  15.1 4.0 %shard_map.99.refs_0_ = f32[16,8,256]{2,1,0:T(8,128)S(1)} custom-call(f32[32,128]{1,0:T(8,128)S(1)} %get-tuple-element.24.phase_ref, f32[16,16,256]{2,1,0:T(8,128)S(1)} %get-tuple-element.25.row_weight_ref, f32[256,512]{1,0:T(8,128)S(1)} %get-tuple-element.36.image_ref, bf16[256,768]{1,0:T(8,128)(2,1)S(1)} %get-tuple-element.37.fwd, ...), custom_call_target="tpu_custom_call" | custom-call | flops 3221225472 | tf_op jit(solution)/shard_map/pallas_call | solution.py:483
  19.1 2.5 %collective-permute-start.9 = (f32[16,8,256]{2,1,0:T(8,128)S(1)}, f32[16,8,256]{2,1,0:T(8,128)S(1)}, u32[]{:S(2)}, u32[]{:S(2)}) collective-permute-start(f32[16,8,256]{2,1,0:T(8,128)S(1)} %shard_map.99.refs_0_), channel_id=1, source_target_pairs={{0,24},{8,16},{16,8},{24,0},{1,25},{9,17},{17,9},{25,1},{2,26},{10... | collective-permute-start | bytes 393224 | tf_op jit(solution)/shard_map/ppermute | solution.py:396
  21.7 0.0 collective-permute-done.3.weight_odd_ref
  21.7 0.5 %collective-permute-start.10 = (f32[16,8,256]{2,1,0:T(8,128)S(1)}, f32[16,8,256]{2,1,0:T(8,128)S(1)}, u32[]{:S(2)}, u32[]{:S(2)}) collective-permute-start(f32[16,8,256]{2,1,0:T(8,128)S(1)} %shard_map.99.refs_0_), channel_id=1, source_target_pairs={{0,16},{8,24},{16,0},{24,8},{1,17},{9,25},{17,1},{25,9},{2,18},{10... | collective-permute-start | bytes 393224 | tf_op jit(solution)/shard_map/ppermute | solution.py:396
  22.2 0.0 collective-permute-done.4.weight_even_ref
  22.2 0.5 %collective-permute-start.11 = (f32[16,8,256]{2,1,0:T(8,128)S(1)}, f32[16,8,256]{2,1,0:T(8,128)S(1)}, u32[]{:S(2)}, u32[]{:S(2)}) collective-permute-start(f32[16,8,256]{2,1,0:T(8,128)S(1)} %shard_map.99.refs_0_), channel_id=1, source_target_pairs={{0,8},{8,0},{16,24},{24,16},{1,9},{9,1},{17,25},{25,17},{2,10},{10... | collective-permute-start | bytes 393224 | tf_op jit(solution)/shard_map/ppermute | solution.py:396
  22.7 0.5 %shard_map.98 = (f32[128,512]{1,0:T(8,128)S(1)}, f32[8,128]{1,0:T(8,128)S(1)}) custom-call(f32[256,512]{1,0:T(8,128)S(1)} %get-tuple-element.33.image_ref, f32[128,512]{1,0:T(8,128)S(1)} %get-tuple-element.32.own_ref, f32[128,512]{1,0:T(8,128)S(1)} %collective-permute-done.1.odd_ref, f32[128,512]{1,0:T(8,128)S(1)} %collective-permute-done.2.even_ref, ...), custom_call_target="tpu_custom_call" | custom-call | tf_op jit(solution)/shard_map/pallas_call | solution.py:494
  23.2 2.5 %collective-permute-start.7 = (f32[8,128]{1,0:T(8,128)S(1)}, f32[8,128]{1,0:T(8,128)S(1)}, u32[]{:S(2)}, u32[]{:S(2)}) collective-permute-start(f32[8,128]{1,0:T(8,128)S(1)} %get-tuple-element.35), channel_id=1, source_target_pairs={{0,24},{8,16},{16,8},{24,0},{1,25},{9,17},{17,9},{25,1},{2,26},{10... | collective-permute-start | bytes 12296 | tf_op jit(solution)/shard_map/ppermute | solution.py:396
  25.7 0.5 %collective-permute-start.6 = (f32[8,128]{1,0:T(8,128)S(1)}, f32[8,128]{1,0:T(8,128)S(1)}, u32[]{:S(2)}, u32[]{:S(2)}) collective-permute-start(f32[8,128]{1,0:T(8,128)S(1)} %get-tuple-element.35), channel_id=1, source_target_pairs={{0,16},{8,24},{16,0},{24,8},{1,17},{9,25},{17,1},{25,9},{2,18},{10... | collective-permute-start | bytes 12296 | tf_op jit(solution)/shard_map/ppermute | solution.py:396
  26.2 1.7 %collective-permute-start.5 = (f32[8,128]{1,0:T(8,128)S(1)}, f32[8,128]{1,0:T(8,128)S(1)}, u32[]{:S(2)}, u32[]{:S(2)}) collective-permute-start(f32[8,128]{1,0:T(8,128)S(1)} %get-tuple-element.35), channel_id=1, source_target_pairs={{0,8},{8,0},{16,24},{24,16},{1,9},{9,1},{17,25},{25,17},{2,10},{10... | collective-permute-start | bytes 12296 | tf_op jit(solution)/shard_map/ppermute | solution.py:396
  28.0 0.2 shard_map.100
  28.1 0.8 %collective-permute-start.12 = (f32[8,128]{1,0:T(8,128)S(1)}, f32[8,128]{1,0:T(8,128)S(1)}, u32[]{:S(2)}, u32[]{:S(2)}) collective-permute-start(f32[8,128]{1,0:T(8,128)S(1)} %get-tuple-element.38), channel_id=1, source_target_pairs={{0,2},{2,0},{4,6},{6,4},{1,3},{3,1},{5,7},{7,5},{8,10},{10,8},{12,... | collective-permute-start | bytes 12296 | tf_op jit(solution)/shard_map/ppermute | solution.py:396
  28.9 0.4 collective-permute-done.6
  29.3 0.5 %collective-permute-done.5 = f32[8,128]{1,0:T(8,128)S(1)} collective-permute-done((f32[8,128]{1,0:T(8,128)S(1)}, f32[8,128]{1,0:T(8,128)S(1)}, u32[]{:S(2)}, u32[]{:S(2)}) %collective-permute-start.5) | collective-permute-done | bytes 4128 | tf_op jit(solution)/shard_map/ppermute | solution.py:396
  29.8 1.1 %collective-permute-start.8 = (f32[8,128]{1,0:T(8,128)S(1)}, f32[8,128]{1,0:T(8,128)S(1)}, u32[]{:S(2)}, u32[]{:S(2)}) collective-permute-start(f32[8,128]{1,0:T(8,128)S(1)} %add_add_fusion.1), channel_id=1, source_target_pairs={{0,2},{2,0},{4,6},{6,4},{1,3},{3,1},{5,7},{7,5},{8,10},{10,8},{12,... | collective-permute-start | bytes 12296 | tf_op jit(solution)/shard_map/ppermute | solution.py:396
  31.0 2.0 %shard_map.101 = (bf16[8,256,512]{2,1,0:T(8,128)(2,1)S(1)}, bf16[8,256,512]{2,1,0:T(8,128)(2,1)S(1)}) custom-call(f32[32,128]{1,0:T(8,128)S(1)} %get-tuple-element.24.phase_ref, f32[16,16,256]{2,1,0:T(8,128)S(1)} %get-tuple-element.25.row_weight_ref, bf16[16,256,256]{2,1,0:T(8,128)(2,1)S(1)} %get-tuple-element.26.whigh, ...), custom_call_target="tpu_custom_call" | custom-call | flops 1610612736 | tf_op jit(solution)/shard_map/pallas_call | solution.py:514
  33.0 0.4 %collective-permute-done.8 = f32[8,128]{1,0:T(8,128)S(1)} collective-permute-done((f32[8,128]{1,0:T(8,128)S(1)}, f32[8,128]{1,0:T(8,128)S(1)}, u32[]{:S(2)}, u32[]{:S(2)}) %collective-permute-start.8) | collective-permute-done | bytes 4128 | tf_op jit(solution)/shard_map/ppermute | solution.py:396
  33.5 1.0 %collective-permute-start.13 = (f32[8,128]{1,0:T(8,128)S(1)}, f32[8,128]{1,0:T(8,128)S(1)}, u32[]{:S(2)}, u32[]{:S(2)}) collective-permute-start(f32[8,128]{1,0:T(8,128)S(1)} %add_add_fusion.refs_0_), channel_id=1, source_target_pairs={{0,4},{2,6},{4,0},{6,2},{1,5},{3,7},{5,1},{7,3},{8,12},{10,14},{12... | collective-permute-start | bytes 12296 | tf_op jit(solution)/shard_map/ppermute | solution.py:396
  34.5 2.3 %shard_map.102.folded_ref = f32[256,512]{1,0:T(8,128)S(1)} custom-call(bf16[256,768]{1,0:T(8,128)(2,1)S(1)} %get-tuple-element.28.adj, bf16[8,256,512]{2,1,0:T(8,128)(2,1)S(1)} %get-tuple-element.29.coil, bf16[8,256,512]{2,1,0:T(8,128)(2,1)S(1)} %get-tuple-element.40.xhigh, bf16[8,256,512]{2,1,0:T(8,128)(2,1)S(1)} %get-tuple-element.41.xlow, ...), custom_call_target="tpu_custom_call" | custom-call | flops 1610612736 | tf_op jit(solution)/shard_map/pallas_call | solution.py:526
  36.8 1.2 %collective-permute-done.13 = f32[8,128]{1,0:T(8,128)S(1)} collective-permute-done((f32[8,128]{1,0:T(8,128)S(1)}, f32[8,128]{1,0:T(8,128)S(1)}, u32[]{:S(2)}, u32[]{:S(2)}) %collective-permute-start.13) | collective-permute-done | bytes 4128 | tf_op jit(solution)/shard_map/ppermute | solution.py:396
  38.0 0.3 shard_map.103
  38.3 0.1 collective-permute-start.14
  38.4 1.5 %collective-permute-done.14.refs_1_ = f32[136,512]{1,0:T(8,128)S(1)} collective-permute-done((f32[136,512]{1,0:T(8,128)S(1)}, f32[136,512]{1,0:T(8,128)S(1)}, u32[]{:S(2)}, u32[]{:S(2)}) %collective-permute-start.14) | collective-permute-done | bytes 278560 | tf_op jit(solution)/shard_map/ppermute | solution.py:396
  40.0 0.9 %shard_map.104 = (f32[128,512]{1,0:T(8,128)}, f32[128,512]{1,0:T(8,128)}) custom-call(f32[128,512]{1,0:T(8,128)S(1)} %get-tuple-element.32.own_ref, f32[128,512]{1,0:T(8,128)S(1)} %get-tuple-element.34.smooth_ref, f32[128,512]{1,0:T(8,128)S(1)} %get-tuple-element.42.refs_0_, f32[136,512]{1,0:T(8,128)S(1)} %collective-permute-done.14.refs_1_, ...), custom_call_target="tpu_custom_call" | custom-call | tf_op jit(solution)/shard_map/pallas_call | solution.py:552
  (11 shorter events, 0.0 us)
Async XLA Ops:
  7.9 4.8 %collective-permute-start = (f32[264,512]{1,0:T(8,128)S(1)}, f32[264,512]{1,0:T(8,128)S(1)}, u32[]{:S(2)}, u32[]{:S(2)}) collective-permute-start(f32[264,512]{1,0:T(8,128)S(1)} %shard_map.96.refs_0_), channel_id=1, source_target_pairs={{0,1},{1,0},{2,3},{3,2},{4,5},{5,4},{6,7},{7,6},{8,9},{9,8},{10,11... | collective-permute-start | bytes 1622024 | tf_op jit(solution)/shard_map/ppermute | solution.py:406
  8.4 13.2 %collective-permute-start.3 = (f32[128,256]{1,0:T(8,128)S(1)}, f32[128,256]{1,0:T(8,128)S(1)}, u32[]{:S(2)}, u32[]{:S(2)}) collective-permute-start(f32[128,256]{1,0:T(8,128)S(1)} %get-tuple-element.31.weight_ref), channel_id=1, source_target_pairs={{0,1},{1,0},{2,4},{3,5},{4,2},{5,3},{6,7},{7,6},{8,9},{9,8},{10,12... | collective-permute-start | bytes 393224 | tf_op jit(solution)/shard_map/ppermute | solution.py:474
  8.5 13.6 %collective-permute-start.4 = (f32[128,256]{1,0:T(8,128)S(1)}, f32[128,256]{1,0:T(8,128)S(1)}, u32[]{:S(2)}, u32[]{:S(2)}) collective-permute-start(f32[128,256]{1,0:T(8,128)S(1)} %get-tuple-element.31.weight_ref), channel_id=1, source_target_pairs={{0,2},{2,0},{4,6},{6,4},{1,3},{3,1},{5,7},{7,5},{8,10},{10,8},{12,... | collective-permute-start | bytes 393224 | tf_op jit(solution)/shard_map/ppermute | solution.py:474
  13.0 9.7 %collective-permute-start.1 = (f32[128,512]{1,0:T(8,128)S(1)}, f32[128,512]{1,0:T(8,128)S(1)}, u32[]{:S(2)}, u32[]{:S(2)}) collective-permute-start(f32[128,512]{1,0:T(8,128)S(1)} %get-tuple-element.32.own_ref), channel_id=1, source_target_pairs={{0,1},{1,0},{2,4},{3,5},{4,2},{5,3},{6,7},{7,6},{8,9},{9,8},{10,12... | collective-permute-start | bytes 786440 | tf_op jit(solution)/shard_map/ppermute | solution.py:481
  13.1 9.6 %collective-permute-start.2 = (f32[128,512]{1,0:T(8,128)S(1)}, f32[128,512]{1,0:T(8,128)S(1)}, u32[]{:S(2)}, u32[]{:S(2)}) collective-permute-start(f32[128,512]{1,0:T(8,128)S(1)} %get-tuple-element.32.own_ref), channel_id=1, source_target_pairs={{0,2},{2,0},{4,6},{6,4},{1,3},{3,1},{5,7},{7,5},{8,10},{10,8},{12,... | collective-permute-start | bytes 786440 | tf_op jit(solution)/shard_map/ppermute | solution.py:481
  19.1 7.1 %collective-permute-start.9 = (f32[16,8,256]{2,1,0:T(8,128)S(1)}, f32[16,8,256]{2,1,0:T(8,128)S(1)}, u32[]{:S(2)}, u32[]{:S(2)}) collective-permute-start(f32[16,8,256]{2,1,0:T(8,128)S(1)} %shard_map.99.refs_0_), channel_id=1, source_target_pairs={{0,24},{8,16},{16,8},{24,0},{1,25},{9,17},{17,9},{25,1},{2,26},{10... | collective-permute-start | bytes 393224 | tf_op jit(solution)/shard_map/ppermute | solution.py:396
  21.7 6.3 %collective-permute-start.10 = (f32[16,8,256]{2,1,0:T(8,128)S(1)}, f32[16,8,256]{2,1,0:T(8,128)S(1)}, u32[]{:S(2)}, u32[]{:S(2)}) collective-permute-start(f32[16,8,256]{2,1,0:T(8,128)S(1)} %shard_map.99.refs_0_), channel_id=1, source_target_pairs={{0,16},{8,24},{16,0},{24,8},{1,17},{9,25},{17,1},{25,9},{2,18},{10... | collective-permute-start | bytes 393224 | tf_op jit(solution)/shard_map/ppermute | solution.py:396
  22.2 5.8 %collective-permute-start.11 = (f32[16,8,256]{2,1,0:T(8,128)S(1)}, f32[16,8,256]{2,1,0:T(8,128)S(1)}, u32[]{:S(2)}, u32[]{:S(2)}) collective-permute-start(f32[16,8,256]{2,1,0:T(8,128)S(1)} %shard_map.99.refs_0_), channel_id=1, source_target_pairs={{0,8},{8,0},{16,24},{24,16},{1,9},{9,1},{17,25},{25,17},{2,10},{10... | collective-permute-start | bytes 393224 | tf_op jit(solution)/shard_map/ppermute | solution.py:396
  23.2 5.7 %collective-permute-start.7 = (f32[8,128]{1,0:T(8,128)S(1)}, f32[8,128]{1,0:T(8,128)S(1)}, u32[]{:S(2)}, u32[]{:S(2)}) collective-permute-start(f32[8,128]{1,0:T(8,128)S(1)} %get-tuple-element.35), channel_id=1, source_target_pairs={{0,24},{8,16},{16,8},{24,0},{1,25},{9,17},{17,9},{25,1},{2,26},{10... | collective-permute-start | bytes 12296 | tf_op jit(solution)/shard_map/ppermute | solution.py:396
  25.7 3.6 %collective-permute-start.6 = (f32[8,128]{1,0:T(8,128)S(1)}, f32[8,128]{1,0:T(8,128)S(1)}, u32[]{:S(2)}, u32[]{:S(2)}) collective-permute-start(f32[8,128]{1,0:T(8,128)S(1)} %get-tuple-element.35), channel_id=1, source_target_pairs={{0,16},{8,24},{16,0},{24,8},{1,17},{9,25},{17,1},{25,9},{2,18},{10... | collective-permute-start | bytes 12296 | tf_op jit(solution)/shard_map/ppermute | solution.py:396
  26.2 3.6 %collective-permute-start.5 = (f32[8,128]{1,0:T(8,128)S(1)}, f32[8,128]{1,0:T(8,128)S(1)}, u32[]{:S(2)}, u32[]{:S(2)}) collective-permute-start(f32[8,128]{1,0:T(8,128)S(1)} %get-tuple-element.35), channel_id=1, source_target_pairs={{0,8},{8,0},{16,24},{24,16},{1,9},{9,1},{17,25},{25,17},{2,10},{10... | collective-permute-start | bytes 12296 | tf_op jit(solution)/shard_map/ppermute | solution.py:396
  28.1 4.9 %collective-permute-start.12 = (f32[8,128]{1,0:T(8,128)S(1)}, f32[8,128]{1,0:T(8,128)S(1)}, u32[]{:S(2)}, u32[]{:S(2)}) collective-permute-start(f32[8,128]{1,0:T(8,128)S(1)} %get-tuple-element.38), channel_id=1, source_target_pairs={{0,2},{2,0},{4,6},{6,4},{1,3},{3,1},{5,7},{7,5},{8,10},{10,8},{12,... | collective-permute-start | bytes 12296 | tf_op jit(solution)/shard_map/ppermute | solution.py:396
  29.8 3.6 %collective-permute-start.8 = (f32[8,128]{1,0:T(8,128)S(1)}, f32[8,128]{1,0:T(8,128)S(1)}, u32[]{:S(2)}, u32[]{:S(2)}) collective-permute-start(f32[8,128]{1,0:T(8,128)S(1)} %add_add_fusion.1), channel_id=1, source_target_pairs={{0,2},{2,0},{4,6},{6,4},{1,3},{3,1},{5,7},{7,5},{8,10},{10,8},{12,... | collective-permute-start | bytes 12296 | tf_op jit(solution)/shard_map/ppermute | solution.py:396
  33.5 4.5 %collective-permute-start.13 = (f32[8,128]{1,0:T(8,128)S(1)}, f32[8,128]{1,0:T(8,128)S(1)}, u32[]{:S(2)}, u32[]{:S(2)}) collective-permute-start(f32[8,128]{1,0:T(8,128)S(1)} %add_add_fusion.refs_0_), channel_id=1, source_target_pairs={{0,4},{2,6},{4,0},{6,2},{1,5},{3,7},{5,1},{7,3},{8,12},{10,14},{12... | collective-permute-start | bytes 12296 | tf_op jit(solution)/shard_map/ppermute | solution.py:396
  38.3 1.6 %collective-permute-start.14 = (f32[136,512]{1,0:T(8,128)S(1)}, f32[136,512]{1,0:T(8,128)S(1)}, u32[]{:S(2)}, u32[]{:S(2)}) collective-permute-start(f32[136,512]{1,0:T(8,128)S(1)} %get-tuple-element.43), channel_id=1, source_target_pairs={{0,1},{1,0},{2,3},{3,2},{4,5},{5,4},{6,7},{7,6},{8,9},{9,8},{10,11... | collective-permute-start | bytes 835592 | tf_op jit(solution)/shard_map/ppermute | solution.py:396
